TPU v7x, 32 devices: a whole 2x2x4 slice. The times are simulated.
32 devices in a mesh: pos: 8 (over y, x, core), obj: 4 (over z).
Axes of the slice: x: 2, y: 2, z: 4, core: 2. Of those that a mesh axis runs over, the one named last changes fastest.
Arguments:
- object_field: float32 [2, 2048, 3072], P(None, 'obj', 'pos'), may hold values from -5 to 5
- probe: float32 [2, 256, 256], replicated, may hold values from -5 to 5
- amplitude: bfloat16 [512, 256, 256], P(('pos', 'obj')), may hold values from 0.19921875 to 3
- row_offset: int32 [512], P(('pos', 'obj')), may hold values from 0 to 256
- col_offset: int32 [512], P(('pos', 'obj')), may hold values from 0 to 128
- owner: int32 [512], P(('pos', 'obj')), may hold values from 0 to 7, as said below
Outputs:
- new_object: float32 [2, 2048, 3072], P(None, 'obj', 'pos')
- new_probe: float32 [2, 256, 256], replicated
Inputs may be any that keep to these rules, and one draw needn't show every extreme that they name: Among the 16 positions of one device no owner is named more than 3 times; in each row band one owner is named exactly 3 times by every device.
All inputs are finite; a program needn't handle non-finite values.
Results may differ from a plain program's by a relative error of at most 0.005.
The roundings to bfloat16 on the way count: a program that leaves them out, or rounds other values in their place, can miss the bound.
Values may be sent and summed in bfloat16 or wider, within the bound.
No kernel may reach another device: no remote copies, remote signals or barrier semaphores. Data moves between devices by JAX's collectives and lax.ppermute only.
A program may use at most 128 MiB of HBM per device.

v0:
```python
import math

import jax
import jax.numpy as jnp
from jax import lax
from jax.sharding import PartitionSpec as P


def padded_2(block, sides, width):
    for axis, dim in sides:
        count = lax.axis_size(axis)
        forward = [(i, i + 1) for i in range(count - 1)]
        forward.append((count - 1, 0))
        backward = [(target, source) for source, target in forward]
        low = lax.ppermute(
            lax.slice_in_dim(block, block.shape[dim] - width, None, axis=dim), axis, forward
        )
        high = lax.ppermute(lax.slice_in_dim(block, 0, width, axis=dim), axis, backward)
        block = jnp.concatenate([low, block, high], axis=dim)
    return block


def dft_tables(size):
    index = jnp.arange(size, dtype=jnp.int32)
    product = index[:, None] * index[None, :] % size
    angle = product.astype(jnp.float32) * (2.0 * math.pi / size)
    scale = 1.0 / math.sqrt(size)
    real_part = (jnp.cos(angle) * scale).astype(jnp.bfloat16)
    imag_part = (-jnp.sin(angle) * scale).astype(jnp.bfloat16)
    return (real_part, imag_part)


def left_apply(mat_re, mat_im, val_re, val_im):

    def product(matrix, values):
        return jnp.einsum("jk,bkl->bjl", matrix, values, preferred_element_type=jnp.float32)

    return (
        product(mat_re, val_re) - product(mat_im, val_im),
        product(mat_re, val_im) + product(mat_im, val_re),
    )


def right_apply(val_re, val_im, mat_re, mat_im):

    def product(values, matrix):
        return jnp.einsum("bjk,kl->bjl", values, matrix, preferred_element_type=jnp.float32)

    return (
        product(val_re, mat_re) - product(val_im, mat_im),
        product(val_re, mat_im) + product(val_im, mat_re),
    )


def position_terms(patches, amps, validity, probe, tables):
    four_re, four_im, conj_im = tables
    patch_re = patches[:, 0].astype(jnp.float32)
    patch_im = patches[:, 1].astype(jnp.float32)
    probe_re = probe[0]
    probe_im = probe[1]
    psi_re = (probe_re * patch_re - probe_im * patch_im).astype(jnp.bfloat16)
    psi_im = (probe_re * patch_im + probe_im * patch_re).astype(jnp.bfloat16)
    left_re, left_im = left_apply(four_re, four_im, psi_re, psi_im)
    wave_re, wave_im = right_apply(
        left_re.astype(jnp.bfloat16), left_im.astype(jnp.bfloat16), four_re, four_im
    )
    magnitude = jnp.sqrt(wave_re * wave_re + wave_im * wave_im)
    factor = 1.0 - amps.astype(jnp.float32) / jnp.maximum(magnitude, 0.5)
    diff_re = (wave_re * factor).astype(jnp.bfloat16)
    diff_im = (wave_im * factor).astype(jnp.bfloat16)
    back_re, back_im = left_apply(four_re, conj_im, diff_re, diff_im)
    chi_re, chi_im = right_apply(
        back_re.astype(jnp.bfloat16), back_im.astype(jnp.bfloat16), four_re, conj_im
    )
    chi_re = chi_re * validity[:, None, None]
    chi_im = chi_im * validity[:, None, None]
    grad_re = (probe_re * chi_re + probe_im * chi_im).astype(jnp.bfloat16)
    grad_im = (probe_re * chi_im - probe_im * chi_re).astype(jnp.bfloat16)
    term_re = jnp.sum(patch_re * chi_re + patch_im * chi_im, axis=0)
    term_im = jnp.sum(patch_re * chi_im - patch_im * chi_re, axis=0)
    return (jnp.stack([grad_re, grad_im], axis=1), jnp.stack([term_re, term_im]))


def run_terms(patches, amps, validity, probe, tables):
    count = patches.shape[0]
    size = patches.shape[2]
    batch_size = math.gcd(count, 8)
    groups = count // batch_size
    grouped = (
        patches.reshape(groups, batch_size, 2, size, size),
        amps.reshape(groups, batch_size, size, size),
        validity.reshape(groups, batch_size),
    )
    grads, terms = lax.map(
        lambda items: position_terms(items[0], items[1], items[2], probe, tables), grouped
    )
    return (grads.reshape(count, 2, size, size), jnp.sum(terms, axis=0))


def extract(tile, corners, size):
    zero = jnp.zeros((), jnp.int32)
    windows = jax.vmap(lambda row, col: lax.dynamic_slice(tile, (zero, row, col), (2, size, size)))(
        corners[:, 0], corners[:, 1]
    )
    return windows.astype(jnp.bfloat16)


def add_scaled(start_value, grads, corners, size):
    zero = jnp.zeros((), jnp.int32)

    def add_one(item, acc):
        corner = (zero, corners[item, 0], corners[item, 1])
        window = lax.dynamic_slice(acc, corner, (2, size, size))
        return lax.dynamic_update_slice(
            acc, window - 0.25 * grads[item].astype(jnp.float32), corner
        )

    return lax.fori_loop(0, grads.shape[0], add_one, start_value)


def shards(object_field, probe, amplitude, row_offset, col_offset, owner):
    n_pos = lax.axis_size("pos")
    n_obj = lax.axis_size("obj")
    pos_dev = amplitude.shape[0]
    size = amplitude.shape[1]
    capacity = max(2, pos_dev // n_pos + 1)
    slots = n_pos * capacity
    padded = padded_2(object_field.astype(jnp.bfloat16), (("pos", 2), ("obj", 1)), 1).astype(
        object_field.dtype
    )
    smooth = 4.0 * object_field - padded[:, :-2, 1:-1] - padded[:, 2:, 1:-1]
    smooth = smooth - padded[:, 1:-1, :-2] - padded[:, 1:-1, 2:]
    four_re, four_im = dft_tables(size)
    tables = (four_re, four_im, -four_im)
    onehot = (owner[:, None] == jnp.arange(n_pos, dtype=jnp.int32)[None, :]).astype(jnp.int32)
    earlier = jnp.cumsum(onehot, axis=0) - onehot
    ranking = jnp.sum(earlier * onehot, axis=1)
    target = owner * capacity + ranking
    matching = (target[:, None] == jnp.arange(slots, dtype=jnp.int32)[None, :]).astype(jnp.int32)
    source = jnp.sum(matching * jnp.arange(pos_dev, dtype=jnp.int32)[:, None], axis=0)
    filled = jnp.sum(matching, axis=0) > 0
    listing = jnp.stack([row_offset, col_offset, jnp.ones_like(row_offset)], axis=1)
    slot_info = jnp.where(filled[:, None], listing[source], 0).reshape(n_pos, capacity, 3)
    recv_info = lax.all_to_all(slot_info, "pos", split_axis=0, concat_axis=0, tiled=True)
    amp_slots = jnp.where(filled[:, None, None], amplitude[source], jnp.zeros((), jnp.bfloat16))
    recv_amp = lax.all_to_all(
        amp_slots.reshape(n_pos, capacity, size, size),
        "pos",
        split_axis=0,
        concat_axis=0,
        tiled=True,
    )
    corners = recv_info.reshape(slots, 3)
    windows = extract(object_field, corners, size)
    validity = corners[:, 2].astype(jnp.float32)
    incoming, probe_part = run_terms(
        windows, recv_amp.reshape(slots, size, size), validity, probe, tables
    )
    base = object_field - 0.125 * smooth
    new_object = add_scaled(base, incoming, corners, size)
    probe_grad = lax.psum(probe_part, ("pos", "obj"))
    n_total = pos_dev * n_pos * n_obj
    new_probe = probe - probe_grad * (1.0 / math.sqrt(n_total))
    return (new_object, new_probe)


def solution(mesh):
    placed = (
        P(None, "obj", "pos"),
        P(),
        P(("pos", "obj"), None, None),
        P(("pos", "obj")),
        P(("pos", "obj")),
        P(("pos", "obj")),
    )
    return jax.shard_map(
        shards, mesh=mesh, in_specs=placed, out_specs=(P(None, "obj", "pos"), P()), check_vma=False
    )
```

profile of v0, /device:TPU:12, one launch (start us, length us, event | category | flops | bytes accessed | tf_op | source)
XLA Modules:
  0.0 499.7 jit_solution(2474730043378262003)
XLA Ops:
  9.8 2.6 collective-permute-start.1
  14.5 3.8 all-to-all-start
  18.3 2.5 gather_fusion.1
  20.8 3.8 broadcast_select_fusion
  24.6 4.5 all-to-all-start.1
  29.2 69.0 %while.29 = (s32[]{:T(128)}, bf16[2,512,384]{2,1,0:T(8,128)(2,1)S(1)}, s32[24,3]{0,1:T(4,128)S(1)}, bf16[24,2,256,256]{3,2,1,0:T(8,128)(2,1)}, s32[]{:T(128)}) while((s32[]{:T(128)}, bf16[2,512,384]{2,1,0:T(8,128)(2,1)S(1)}, s32[24,3]{0,1:T(4,128)S(1)}, bf16[24,2,256,256]{3,2,1,0:T(8,128)(2,1)}, s32[]{:T(128)}) %tuple.88), condition=%wide.while_cond, body=%wide.while_body.sunk | while | flops 2 | bytes 525929 | solution.py:102
  29.9 2.2 bitcast_dynamic-update-slice_fusion.2
  32.7 2.2 bitcast_dynamic-update-slice_fusion.2
  35.6 2.2 bitcast_dynamic-update-slice_fusion.2
  38.5 2.2 bitcast_dynamic-update-slice_fusion.2
  41.4 2.2 bitcast_dynamic-update-slice_fusion.2
  44.2 2.2 bitcast_dynamic-update-slice_fusion.2
  47.1 2.2 bitcast_dynamic-update-slice_fusion.2
  50.0 2.2 bitcast_dynamic-update-slice_fusion.2
  52.9 2.2 bitcast_dynamic-update-slice_fusion.2
  55.8 2.2 bitcast_dynamic-update-slice_fusion.2
  58.7 2.2 bitcast_dynamic-update-slice_fusion.2
  61.5 2.2 bitcast_dynamic-update-slice_fusion.2
  64.4 2.2 bitcast_dynamic-update-slice_fusion.2
  67.3 2.2 bitcast_dynamic-update-slice_fusion.2
  70.2 2.2 bitcast_dynamic-update-slice_fusion.2
  73.0 2.2 bitcast_dynamic-update-slice_fusion.2
  75.9 2.2 bitcast_dynamic-update-slice_fusion.2
  78.8 2.2 bitcast_dynamic-update-slice_fusion.2
  81.6 2.2 bitcast_dynamic-update-slice_fusion.2
  84.5 2.2 bitcast_dynamic-update-slice_fusion.2
  87.4 2.2 bitcast_dynamic-update-slice_fusion.2
  90.2 2.2 bitcast_dynamic-update-slice_fusion.2
  93.1 2.2 bitcast_dynamic-update-slice_fusion.2
  96.0 2.2 bitcast_dynamic-update-slice_fusion.2
  104.3 2.6 fusion.144
  106.9 97.1 %while.30 = (s32[]{:T(128)}, bf16[3,8,2,256,256]{4,3,2,1,0:T(8,128)(2,1)}, f32[3,2,256,256]{3,2,1,0:T(8,128)}, f32[2,256,256]{2,1,0:T(8,128)S(1)}, bf16[3,8,2,25...) while((s32[]{:T(128)}, ...), condition=%wide.region_7.8_spmd.clone.clone, body=%wide.region_4.7_spmd.clone.clone.sunk | while | flops 4349231104 | bytes 88082136 | solution.py:94
  119.8 3.9 multiply_convert_fusion.9
  133.7 3.3 fusion.256
  152.2 3.9 multiply_convert_fusion.9
  166.0 3.3 fusion.256
  184.5 3.9 multiply_convert_fusion.9
  198.4 3.3 fusion.256
  203.9 2.4 reduce_sum.60
  206.3 284.5 %while.28 = (s32[]{:T(128)}, f32[2,512,384]{2,1,0:T(8,128)}, s32[24,3]{0,1:T(4,128)S(1)}, bf16[24,2,256,256]{3,2,1,0:T(8,128)(2,1)}, s32[]{:T(128)}, /*index=5*/s32[]{:T(128)}, s32[]{:T(128)}, s32[]{:T(128)}) while((s32[]{:T(128)}, f32[2,512,384]{2,1,0:T(8,128)}, s32[24,3]{0,1:T(4,128)S(1)}, bf16[24,2,256,256]{3,2,1,0:T(8,128)(2,1)}, ...), condition=%wide.region_9.10_spmd, body=%wide.region_8.9_spmd.sunk | while | flops 393224 | bytes 2359485 | solution.py:118
  211.9 6.4 %dynamic_update_slice.24 = f32[2,512,384]{2,1,0:T(8,128)} dynamic-update-slice(f32[2,512,384]{2,1,0:T(8,128)} %get-tuple-element.482, f32[2,256,256]{2,1,0:T(8,128)S(1)} %bitcast_subtract_fusion.2, s32[]{:T(128)} %constant.95.clone.1..sunk, s32[]{:T(128)S(6)} %select_n.179, s32[]{:T(128)S(6)} %select_n.180) | dynamic-update-slice | bytes 1048580 | tf_op jit(solution)/shard_map/while/body/eval_jaxpr/dynamic_update_slice | solution.py:114
  223.9 6.5 %dynamic_update_slice.24 = f32[2,512,384]{2,1,0:T(8,128)} dynamic-update-slice(f32[2,512,384]{2,1,0:T(8,128)} %get-tuple-element.482, f32[2,256,256]{2,1,0:T(8,128)S(1)} %bitcast_subtract_fusion.2, s32[]{:T(128)} %constant.95.clone.1..sunk, s32[]{:T(128)S(6)} %select_n.179, s32[]{:T(128)S(6)} %select_n.180) | dynamic-update-slice | bytes 1048580 | tf_op jit(solution)/shard_map/while/body/eval_jaxpr/dynamic_update_slice | solution.py:114
  235.9 6.5 %dynamic_update_slice.24 = f32[2,512,384]{2,1,0:T(8,128)} dynamic-update-slice(f32[2,512,384]{2,1,0:T(8,128)} %get-tuple-element.482, f32[2,256,256]{2,1,0:T(8,128)S(1)} %bitcast_subtract_fusion.2, s32[]{:T(128)} %constant.95.clone.1..sunk, s32[]{:T(128)S(6)} %select_n.179, s32[]{:T(128)S(6)} %select_n.180) | dynamic-update-slice | bytes 1048580 | tf_op jit(solution)/shard_map/while/body/eval_jaxpr/dynamic_update_slice | solution.py:114
  247.9 6.5 %dynamic_update_slice.24 = f32[2,512,384]{2,1,0:T(8,128)} dynamic-update-slice(f32[2,512,384]{2,1,0:T(8,128)} %get-tuple-element.482, f32[2,256,256]{2,1,0:T(8,128)S(1)} %bitcast_subtract_fusion.2, s32[]{:T(128)} %constant.95.clone.1..sunk, s32[]{:T(128)S(6)} %select_n.179, s32[]{:T(128)S(6)} %select_n.180) | dynamic-update-slice | bytes 1048580 | tf_op jit(solution)/shard_map/while/body/eval_jaxpr/dynamic_update_slice | solution.py:114
  259.9 6.5 %dynamic_update_slice.24 = f32[2,512,384]{2,1,0:T(8,128)} dynamic-update-slice(f32[2,512,384]{2,1,0:T(8,128)} %get-tuple-element.482, f32[2,256,256]{2,1,0:T(8,128)S(1)} %bitcast_subtract_fusion.2, s32[]{:T(128)} %constant.95.clone.1..sunk, s32[]{:T(128)S(6)} %select_n.179, s32[]{:T(128)S(6)} %select_n.180) | dynamic-update-slice | bytes 1048580 | tf_op jit(solution)/shard_map/while/body/eval_jaxpr/dynamic_update_slice | solution.py:114
  272.0 6.2 %dynamic_update_slice.24 = f32[2,512,384]{2,1,0:T(8,128)} dynamic-update-slice(f32[2,512,384]{2,1,0:T(8,128)} %get-tuple-element.482, f32[2,256,256]{2,1,0:T(8,128)S(1)} %bitcast_subtract_fusion.2, s32[]{:T(128)} %constant.95.clone.1..sunk, s32[]{:T(128)S(6)} %select_n.179, s32[]{:T(128)S(6)} %select_n.180) | dynamic-update-slice | bytes 1048580 | tf_op jit(solution)/shard_map/while/body/eval_jaxpr/dynamic_update_slice | solution.py:114
  283.7 6.2 %dynamic_update_slice.24 = f32[2,512,384]{2,1,0:T(8,128)} dynamic-update-slice(f32[2,512,384]{2,1,0:T(8,128)} %get-tuple-element.482, f32[2,256,256]{2,1,0:T(8,128)S(1)} %bitcast_subtract_fusion.2, s32[]{:T(128)} %constant.95.clone.1..sunk, s32[]{:T(128)S(6)} %select_n.179, s32[]{:T(128)S(6)} %select_n.180) | dynamic-update-slice | bytes 1048580 | tf_op jit(solution)/shard_map/while/body/eval_jaxpr/dynamic_update_slice | solution.py:114
  295.5 6.2 %dynamic_update_slice.24 = f32[2,512,384]{2,1,0:T(8,128)} dynamic-update-slice(f32[2,512,384]{2,1,0:T(8,128)} %get-tuple-element.482, f32[2,256,256]{2,1,0:T(8,128)S(1)} %bitcast_subtract_fusion.2, s32[]{:T(128)} %constant.95.clone.1..sunk, s32[]{:T(128)S(6)} %select_n.179, s32[]{:T(128)S(6)} %select_n.180) | dynamic-update-slice | bytes 1048580 | tf_op jit(solution)/shard_map/while/body/eval_jaxpr/dynamic_update_slice | solution.py:114
  307.2 6.3 %dynamic_update_slice.24 = f32[2,512,384]{2,1,0:T(8,128)} dynamic-update-slice(f32[2,512,384]{2,1,0:T(8,128)} %get-tuple-element.482, f32[2,256,256]{2,1,0:T(8,128)S(1)} %bitcast_subtract_fusion.2, s32[]{:T(128)} %constant.95.clone.1..sunk, s32[]{:T(128)S(6)} %select_n.179, s32[]{:T(128)S(6)} %select_n.180) | dynamic-update-slice | bytes 1048580 | tf_op jit(solution)/shard_map/while/body/eval_jaxpr/dynamic_update_slice | solution.py:114
  319.1 6.4 %dynamic_update_slice.24 = f32[2,512,384]{2,1,0:T(8,128)} dynamic-update-slice(f32[2,512,384]{2,1,0:T(8,128)} %get-tuple-element.482, f32[2,256,256]{2,1,0:T(8,128)S(1)} %bitcast_subtract_fusion.2, s32[]{:T(128)} %constant.95.clone.1..sunk, s32[]{:T(128)S(6)} %select_n.179, s32[]{:T(128)S(6)} %select_n.180) | dynamic-update-slice | bytes 1048580 | tf_op jit(solution)/shard_map/while/body/eval_jaxpr/dynamic_update_slice | solution.py:114
  331.0 6.2 %dynamic_update_slice.24 = f32[2,512,384]{2,1,0:T(8,128)} dynamic-update-slice(f32[2,512,384]{2,1,0:T(8,128)} %get-tuple-element.482, f32[2,256,256]{2,1,0:T(8,128)S(1)} %bitcast_subtract_fusion.2, s32[]{:T(128)} %constant.95.clone.1..sunk, s32[]{:T(128)S(6)} %select_n.179, s32[]{:T(128)S(6)} %select_n.180) | dynamic-update-slice | bytes 1048580 | tf_op jit(solution)/shard_map/while/body/eval_jaxpr/dynamic_update_slice | solution.py:114
  342.8 6.4 %dynamic_update_slice.24 = f32[2,512,384]{2,1,0:T(8,128)} dynamic-update-slice(f32[2,512,384]{2,1,0:T(8,128)} %get-tuple-element.482, f32[2,256,256]{2,1,0:T(8,128)S(1)} %bitcast_subtract_fusion.2, s32[]{:T(128)} %constant.95.clone.1..sunk, s32[]{:T(128)S(6)} %select_n.179, s32[]{:T(128)S(6)} %select_n.180) | dynamic-update-slice | bytes 1048580 | tf_op jit(solution)/shard_map/while/body/eval_jaxpr/dynamic_update_slice | solution.py:114
  354.7 6.2 %dynamic_update_slice.24 = f32[2,512,384]{2,1,0:T(8,128)} dynamic-update-slice(f32[2,512,384]{2,1,0:T(8,128)} %get-tuple-element.482, f32[2,256,256]{2,1,0:T(8,128)S(1)} %bitcast_subtract_fusion.2, s32[]{:T(128)} %constant.95.clone.1..sunk, s32[]{:T(128)S(6)} %select_n.179, s32[]{:T(128)S(6)} %select_n.180) | dynamic-update-slice | bytes 1048580 | tf_op jit(solution)/shard_map/while/body/eval_jaxpr/dynamic_update_slice | solution.py:114
  366.5 5.9 %dynamic_update_slice.24 = f32[2,512,384]{2,1,0:T(8,128)} dynamic-update-slice(f32[2,512,384]{2,1,0:T(8,128)} %get-tuple-element.482, f32[2,256,256]{2,1,0:T(8,128)S(1)} %bitcast_subtract_fusion.2, s32[]{:T(128)} %constant.95.clone.1..sunk, s32[]{:T(128)S(6)} %select_n.179, s32[]{:T(128)S(6)} %select_n.180) | dynamic-update-slice | bytes 1048580 | tf_op jit(solution)/shard_map/while/body/eval_jaxpr/dynamic_update_slice | solution.py:114
  378.0 5.9 %dynamic_update_slice.24 = f32[2,512,384]{2,1,0:T(8,128)} dynamic-update-slice(f32[2,512,384]{2,1,0:T(8,128)} %get-tuple-element.482, f32[2,256,256]{2,1,0:T(8,128)S(1)} %bitcast_subtract_fusion.2, s32[]{:T(128)} %constant.95.clone.1..sunk, s32[]{:T(128)S(6)} %select_n.179, s32[]{:T(128)S(6)} %select_n.180) | dynamic-update-slice | bytes 1048580 | tf_op jit(solution)/shard_map/while/body/eval_jaxpr/dynamic_update_slice | solution.py:114
  389.5 6.5 %dynamic_update_slice.24 = f32[2,512,384]{2,1,0:T(8,128)} dynamic-update-slice(f32[2,512,384]{2,1,0:T(8,128)} %get-tuple-element.482, f32[2,256,256]{2,1,0:T(8,128)S(1)} %bitcast_subtract_fusion.2, s32[]{:T(128)} %constant.95.clone.1..sunk, s32[]{:T(128)S(6)} %select_n.179, s32[]{:T(128)S(6)} %select_n.180) | dynamic-update-slice | bytes 1048580 | tf_op jit(solution)/shard_map/while/body/eval_jaxpr/dynamic_update_slice | solution.py:114
  401.5 6.4 %dynamic_update_slice.24 = f32[2,512,384]{2,1,0:T(8,128)} dynamic-update-slice(f32[2,512,384]{2,1,0:T(8,128)} %get-tuple-element.482, f32[2,256,256]{2,1,0:T(8,128)S(1)} %bitcast_subtract_fusion.2, s32[]{:T(128)} %constant.95.clone.1..sunk, s32[]{:T(128)S(6)} %select_n.179, s32[]{:T(128)S(6)} %select_n.180) | dynamic-update-slice | bytes 1048580 | tf_op jit(solution)/shard_map/while/body/eval_jaxpr/dynamic_update_slice | solution.py:114
  413.4 6.1 %dynamic_update_slice.24 = f32[2,512,384]{2,1,0:T(8,128)} dynamic-update-slice(f32[2,512,384]{2,1,0:T(8,128)} %get-tuple-element.482, f32[2,256,256]{2,1,0:T(8,128)S(1)} %bitcast_subtract_fusion.2, s32[]{:T(128)} %constant.95.clone.1..sunk, s32[]{:T(128)S(6)} %select_n.179, s32[]{:T(128)S(6)} %select_n.180) | dynamic-update-slice | bytes 1048580 | tf_op jit(solution)/shard_map/while/body/eval_jaxpr/dynamic_update_slice | solution.py:114
  425.1 6.3 %dynamic_update_slice.24 = f32[2,512,384]{2,1,0:T(8,128)} dynamic-update-slice(f32[2,512,384]{2,1,0:T(8,128)} %get-tuple-element.482, f32[2,256,256]{2,1,0:T(8,128)S(1)} %bitcast_subtract_fusion.2, s32[]{:T(128)} %constant.95.clone.1..sunk, s32[]{:T(128)S(6)} %select_n.179, s32[]{:T(128)S(6)} %select_n.180) | dynamic-update-slice | bytes 1048580 | tf_op jit(solution)/shard_map/while/body/eval_jaxpr/dynamic_update_slice | solution.py:114
  436.9 6.5 %dynamic_update_slice.24 = f32[2,512,384]{2,1,0:T(8,128)} dynamic-update-slice(f32[2,512,384]{2,1,0:T(8,128)} %get-tuple-element.482, f32[2,256,256]{2,1,0:T(8,128)S(1)} %bitcast_subtract_fusion.2, s32[]{:T(128)} %constant.95.clone.1..sunk, s32[]{:T(128)S(6)} %select_n.179, s32[]{:T(128)S(6)} %select_n.180) | dynamic-update-slice | bytes 1048580 | tf_op jit(solution)/shard_map/while/body/eval_jaxpr/dynamic_update_slice | solution.py:114
  448.9 6.2 %dynamic_update_slice.24 = f32[2,512,384]{2,1,0:T(8,128)} dynamic-update-slice(f32[2,512,384]{2,1,0:T(8,128)} %get-tuple-element.482, f32[2,256,256]{2,1,0:T(8,128)S(1)} %bitcast_subtract_fusion.2, s32[]{:T(128)} %constant.95.clone.1..sunk, s32[]{:T(128)S(6)} %select_n.179, s32[]{:T(128)S(6)} %select_n.180) | dynamic-update-slice | bytes 1048580 | tf_op jit(solution)/shard_map/while/body/eval_jaxpr/dynamic_update_slice | solution.py:114
  460.6 6.2 %dynamic_update_slice.24 = f32[2,512,384]{2,1,0:T(8,128)} dynamic-update-slice(f32[2,512,384]{2,1,0:T(8,128)} %get-tuple-element.482, f32[2,256,256]{2,1,0:T(8,128)S(1)} %bitcast_subtract_fusion.2, s32[]{:T(128)} %constant.95.clone.1..sunk, s32[]{:T(128)S(6)} %select_n.179, s32[]{:T(128)S(6)} %select_n.180) | dynamic-update-slice | bytes 1048580 | tf_op jit(solution)/shard_map/while/body/eval_jaxpr/dynamic_update_slice | solution.py:114
  472.3 6.5 %dynamic_update_slice.24 = f32[2,512,384]{2,1,0:T(8,128)} dynamic-update-slice(f32[2,512,384]{2,1,0:T(8,128)} %get-tuple-element.482, f32[2,256,256]{2,1,0:T(8,128)S(1)} %bitcast_subtract_fusion.2, s32[]{:T(128)} %constant.95.clone.1..sunk, s32[]{:T(128)S(6)} %select_n.179, s32[]{:T(128)S(6)} %select_n.180) | dynamic-update-slice | bytes 1048580 | tf_op jit(solution)/shard_map/while/body/eval_jaxpr/dynamic_update_slice | solution.py:114
  484.3 6.5 %dynamic_update_slice.24 = f32[2,512,384]{2,1,0:T(8,128)} dynamic-update-slice(f32[2,512,384]{2,1,0:T(8,128)} %get-tuple-element.482, f32[2,256,256]{2,1,0:T(8,128)S(1)} %bitcast_subtract_fusion.2, s32[]{:T(128)} %constant.95.clone.1..sunk, s32[]{:T(128)S(6)} %select_n.179, s32[]{:T(128)S(6)} %select_n.180) | dynamic-update-slice | bytes 1048580 | tf_op jit(solution)/shard_map/while/body/eval_jaxpr/dynamic_update_slice | solution.py:114
  (211 shorter events, 152.6 us)
Async XLA Ops:
  7.2 11.1 %copy-start = (bf16[16,256,256]{2,1,0:T(8,128)(2,1)S(1)}, bf16[16,256,256]{2,1,0:T(8,128)(2,1)}, u32[]{:S(2)}) copy-start(bf16[16,256,256]{2,1,0:T(8,128)(2,1)} %param.12) | copy-start | bytes 6291460
  7.2 5.2 %copy-start.4 = (s32[16]{0:T(128)S(1)}, s32[16]{0:T(128)}, u32[]{:S(2)}) copy-start(s32[16]{0:T(128)} %param.15) | copy-start | bytes 196
  7.2 5.7 %copy-start.6 = (s32[16]{0:T(128)S(1)}, s32[16]{0:T(128)}, u32[]{:S(2)}) copy-start(s32[16]{0:T(128)} %param.13) | copy-start | bytes 196
  7.2 5.7 %copy-start.5 = (s32[16]{0:T(128)S(1)}, s32[16]{0:T(128)}, u32[]{:S(2)}) copy-start(s32[16]{0:T(128)} %param.14) | copy-start | bytes 196
  9.8 88.4 %collective-permute-start = (bf16[2,512,1]{2,1,0:T(8,128)(2,1)}, bf16[2,512,1]{2,1,0:T(8,128)(2,1)S(1)}, u32[]{:S(2)}, u32[]{:S(2)}) collective-permute-start(bf16[2,512,1]{2,1,0:T(8,128)(2,1)} %get-tuple-element.313), channel_id=1, source_target_pairs={{0,4},{4,8},{8,12},{12,16},{16,20},{20,24},{24,28},{28,0},{1,5},{5... | collective-permute-start | bytes 6152 | tf_op jit(solution)/shard_map/ppermute | solution.py:15
  9.8 88.4 %collective-permute-start.1 = (bf16[2,512,1]{2,1,0:T(8,128)(2,1)}, bf16[2,512,1]{2,1,0:T(8,128)(2,1)S(1)}, u32[]{:S(2)}, u32[]{:S(2)}) collective-permute-start(bf16[2,512,1]{2,1,0:T(8,128)(2,1)} %get-tuple-element.314), channel_id=1, source_target_pairs={{4,0},{8,4},{12,8},{16,12},{20,16},{24,20},{28,24},{0,28},{5,1},{9... | collective-permute-start | bytes 6152 | tf_op jit(solution)/shard_map/ppermute | solution.py:18
  14.5 10.1 %all-to-all-start = ((s32[8,3,3]{1,2,0:T(4,128)}), s32[8,3,3]{1,2,0:T(4,128)S(1)}, u32[]{:S(2)}, u32[]{:S(2)}) async-start(s32[8,3,3]{1,2,0:T(4,128)} %copy.88), calls=%async_computation | async-start | bytes 32768 | tf_op jit(solution)/shard_map/all_to_all | solution.py:144
  24.6 82.3 %all-to-all-start.1 = ((bf16[8,3,256,256]{3,2,1,0:T(8,128)(2,1)}), bf16[8,3,256,256]{3,2,1,0:T(8,128)(2,1)}, u32[]{:S(2)}, u32[]{:S(2)}) async-start(bf16[8,3,256,256]{3,2,1,0:T(8,128)(2,1)} %broadcast_select_fusion), calls=%async_computation.1 | async-start | bytes 6291456 | tf_op jit(solution)/shard_map/all_to_all | solution.py:146
  29.0 461.8 %all-reduce.2.cloned.1.call-start = ((), (), s32[]{:S(2)}) async-start(), calls=%async_computation.2 | async-start | bytes 1048576 | tf_op jit(solution)/shard_map/psum | solution.py:161
  98.2 6.1 %copy-start.3 = (f32[2,512,384]{2,1,0:T(8,128)S(1)}, f32[2,512,384]{2,1,0:T(8,128)}, u32[]{:S(2)}) copy-start(f32[2,512,384]{2,1,0:T(8,128)} %param.10) | copy-start | bytes 4718596
  98.3 3.7 collective-permute-start.2
  99.9 3.6 collective-permute-start.3
  104.3 2.6 copy-start.2
  490.8 2.1 copy-start.1
Sparse Core Ops, SparseCore 0:
  206.5 129.1 all-reduce.1
where the time goes:
time: 507 us; the launch traced here: 500 us
  local copies, waits for them, and re-layouts  245 us (48%)
  loops' own time  85.2 us (17%)
  matrix products  84.4 us (17%)
  other arithmetic  54.7 us (11%)
  between operations  14.1 us (3%)
  starting transfers between devices  13 us (3%)
    dynamic_update_slice x24, local copies, waits for them, and re-layouts, add_one(): lax.dynamic_update_slice(acc, window - 0.25 * grads[item].astype(jnp.floa...  151 us
    another operation x1, loops' own time, add_scaled(): return lax.fori_loop(0, grads.shape[0], add_one, start_value)  84.8 us
    gather x72, local copies, waits for them, and re-layouts  68.9 us
    dot_general x24, matrix products, product(): jnp.einsum('bjk,kl->bjl', values, matrix, preferred_element_type=jnp.floa...  47.1 us
    dot_general x24, matrix products, product(): jnp.einsum('jk,bkl->bjl', matrix, values, preferred_element_type=jnp.floa...  37.3 us
    sub x24, other arithmetic, add_one(): window - 0.25 * grads[item].astype(jnp.float32)  34 us
    dynamic_slice x24, local copies, waits for them, and re-layouts, add_one(): corner = (zero, corners[item, 0], corners[item, 1])  14.2 us
  transfers between devices with their start and end apart: 7, of which 2 were waited for; matrix products, arithmetic and copies ran while one was open for 56% of the time, Pallas kernels for 0%

commit v1 on v0

v1 whole, which is shorter than its diff:
```python
import functools
import math

import jax
import jax.numpy as jnp
import numpy as np
from jax import lax
from jax.experimental import pallas as pl
from jax.experimental.pallas import tpu as pltpu
from jax.sharding import PartitionSpec as P

LANES = 128
INFO_ROWS = 16
VMEM_LIMIT = 56 * 2**20
bf16 = jnp.bfloat16
f32 = jnp.float32


def dft_blocks(size):
    index = np.arange(size, dtype=np.int32)
    product = index[:, None] * index[None, :] % size
    angle = product.astype(np.float32) * np.float32(2.0 * math.pi / size)
    scale = np.float32(1.0 / math.sqrt(size))
    real_part = (np.cos(angle) * scale).astype(bf16)
    imag_part = (-np.sin(angle) * scale).astype(bf16)
    left = np.block([[real_part, -imag_part], [imag_part, real_part]])
    right = np.block([[real_part, imag_part], [-imag_part, real_part]])
    return left, right


def exchange(value, axis, distance):
    count = lax.axis_size(axis)
    return lax.ppermute(value, axis, [(i, i ^ distance) for i in range(count)])


def dot(a, b):
    return jnp.dot(a, b, preferred_element_type=f32)


def pack_kernel(n_pos, capacity, pos_dev, size, me_ref, owner, row, col, amp, *rest):
    outs = rest[:n_pos]
    counts, source, info, sems, info_sems = rest[n_pos:]
    me = me_ref[0]
    for q in range(n_pos):
        counts[q] = 0
    for item in range(pos_dev):
        who = owner[item]
        rank = counts[who]
        source[who * capacity + rank] = item
        counts[who] = rank + 1
    lane = lax.broadcasted_iota(jnp.int32, (INFO_ROWS, size), 1)
    copies = []
    for d in range(n_pos):
        partner = jnp.bitwise_xor(me, d)
        held = counts[partner]
        block = jnp.zeros((INFO_ROWS, size), f32)
        for k in range(capacity):
            valid = k < held
            item = jnp.where(valid, source[partner * capacity + k], 0)
            copy = pltpu.make_async_copy(amp.at[item], outs[d].at[pl.ds(k * size, size)], sems.at[d, k])
            pl.when(valid)(copy.start)
            copies.append((valid, copy))
            numbers = (jnp.where(valid, row[item], 0), jnp.where(valid, col[item], 0), valid.astype(jnp.int32))
            for j, number in enumerate(numbers):
                block = jnp.where(lane == 3 * k + j, number.astype(f32), block)
        info[d] = block.astype(bf16)
        copy = pltpu.make_async_copy(info.at[d], outs[d].at[pl.ds(capacity * size, INFO_ROWS)], info_sems.at[d])
        copy.start()
        copies.append((None, copy))
    for valid, copy in copies:
        if valid is None:
            copy.wait()
        else:
            pl.when(valid)(copy.wait)


def pack(me, owner, row, col, amplitude, n_pos, capacity):
    pos_dev, size, _ = amplitude.shape
    smem = pl.BlockSpec(memory_space=pltpu.SMEM)
    hbm = pl.BlockSpec(memory_space=pl.ANY)
    rows = capacity * size + INFO_ROWS
    return pl.pallas_call(
        functools.partial(pack_kernel, n_pos, capacity, pos_dev, size),
        in_specs=[smem, smem, smem, smem, hbm],
        out_specs=[hbm] * n_pos,
        out_shape=[jax.ShapeDtypeStruct((rows, size), bf16)] * n_pos,
        scratch_shapes=[
            pltpu.SMEM((n_pos,), jnp.int32),
            pltpu.SMEM((n_pos * capacity,), jnp.int32),
            pltpu.VMEM((n_pos, INFO_ROWS, size), bf16),
            pltpu.SemaphoreType.DMA((n_pos, capacity)),
            pltpu.SemaphoreType.DMA((n_pos,)),
        ],
        compiler_params=pltpu.CompilerParams(vmem_limit_bytes=16 * 2**20),
        name="pack",
    )(me, owner, row, col, amplitude)


def prepare_kernel(parts, tile, out):
    for plane in range(2):
        for k in range(parts):
            block = tile[plane, :, k * LANES : (k + 1) * LANES]
            out[plane * parts + k] = block.astype(bf16).astype(f32)


def prepare(tile):
    _, rows, cols = tile.shape
    parts = cols // LANES
    return pl.pallas_call(
        functools.partial(prepare_kernel, parts),
        out_shape=jax.ShapeDtypeStruct((2 * parts, rows, LANES), f32),
        compiler_params=pltpu.CompilerParams(vmem_limit_bytes=VMEM_LIMIT),
        name="prepare",
    )(tile)


def read_info(block, count):
    lane = lax.broadcasted_iota(jnp.int32, block.shape, 1)
    first = lax.broadcasted_iota(jnp.int32, block.shape, 0) == 0
    values = block.astype(f32)
    return [
        jnp.sum(jnp.where(first & (lane == j), values, 0.0)).astype(jnp.int32) for j in range(count)
    ]


def window(tile, plane, row, col, size, parts):
    shift = lax.rem(LANES - col, LANES)
    keep = lax.broadcasted_iota(jnp.int32, (size, LANES), 1) < LANES - col
    rolled = [
        pltpu.roll(tile[plane * parts + k, pl.ds(row, size), :], shift, 1) for k in range(size // LANES + 1)
    ]
    return jnp.concatenate(
        [jnp.where(keep, rolled[k], rolled[k + 1]) for k in range(size // LANES)], axis=1
    )


def side_by_side(stacked, size):
    return jnp.concatenate([stacked[:size], stacked[size:]], axis=1)


def terms_kernel(count, capacity, size, tile, probe, left, right, term_in, *rest):
    amps, outs, term, info = rest[:count], rest[count : 2 * count], rest[2 * count], rest[2 * count + 1]
    parts = tile.shape[0] // 2
    term[...] = term_in[...]
    for amp, out in zip(amps, outs):
        block = amp[pl.ds(capacity * size, INFO_ROWS), :]
        for j, number in enumerate(read_info(block, 3 * capacity)):
            info[j] = number

        def one(slot, carry, amp=amp, out=out):
            @pl.when(info[3 * slot + 2] > 0)
            def _():
                row = info[3 * slot]
                col = info[3 * slot + 1]
                patch_re = window(tile, 0, row, col, size, parts)
                patch_im = window(tile, 1, row, col, size, parts)
                probe_re = probe[0]
                probe_im = probe[1]
                psi_re = (probe_re * patch_re - probe_im * patch_im).astype(bf16)
                psi_im = (probe_re * patch_im + probe_im * patch_re).astype(bf16)
                half = dot(left[...], jnp.concatenate([psi_re, psi_im], axis=0)).astype(bf16)
                wave = dot(side_by_side(half, size), right[...])
                wave_re = wave[:, :size]
                wave_im = wave[:, size:]
                square = wave_re * wave_re + wave_im * wave_im
                measured = amp[pl.ds(pl.multiple_of(slot * size, size), size), :].astype(f32)
                factor = 1.0 - measured * lax.rsqrt(jnp.maximum(square, 0.25))
                diff_re = (wave_re * factor).astype(bf16)
                diff_im = (wave_im * factor).astype(bf16)
                back = dot(right[...], jnp.concatenate([diff_re, diff_im], axis=0)).astype(bf16)
                chi = dot(side_by_side(back, size), left[...])
                chi_re = chi[:, :size]
                chi_im = chi[:, size:]
                out[slot, 0] = (probe_re * chi_re + probe_im * chi_im).astype(bf16)
                out[slot, 1] = (probe_re * chi_im - probe_im * chi_re).astype(bf16)
                patch_re = window(tile, 0, row, col, size, parts)
                patch_im = window(tile, 1, row, col, size, parts)
                term[0] += patch_re * chi_re + patch_im * chi_im
                term[1] += patch_re * chi_im - patch_im * chi_re

            return carry

        lax.fori_loop(0, capacity, one, 0)


def terms(tile, probe, left, right, term, amps, capacity):
    size = probe.shape[1]
    count = len(amps)
    full = pl.BlockSpec(memory_space=pltpu.VMEM)
    work = 16 * 2 * size**3 * capacity * count
    results = pl.pallas_call(
        functools.partial(terms_kernel, count, capacity, size),
        in_specs=[full] * (5 + count),
        out_specs=[full] * (count + 1),
        out_shape=[jax.ShapeDtypeStruct((capacity, 2, size, size), bf16)] * count
        + [jax.ShapeDtypeStruct(term.shape, f32)],
        scratch_shapes=[pltpu.SMEM((3 * capacity,), jnp.int32)],
        compiler_params=pltpu.CompilerParams(vmem_limit_bytes=VMEM_LIMIT),
        cost_estimate=pl.CostEstimate(flops=4 * work, bytes_accessed=2**22, transcendentals=0),
        name="terms",
    )(tile, probe, left, right, term, *amps)
    return results[:count], results[count]


def scatter_kernel(count, capacity, size, base, *rest):
    amp_infos, grads, out, info = rest[:count], rest[count : 2 * count], rest[2 * count], rest[2 * count + 1]
    cols = base.shape[2]
    parts = cols // LANES
    acc = rest[2 * count + 2]
    for plane in range(2):
        for k in range(parts):
            acc[plane * parts + k] = base[plane, :, k * LANES : (k + 1) * LANES]
    inner = size // LANES
    for amp, grad in zip(amp_infos, grads):
        for j, number in enumerate(read_info(amp[...], 3 * capacity)):
            info[j] = number

        def one(slot, carry, grad=grad):
            @pl.when(info[3 * slot + 2] > 0)
            def _():
                row = info[3 * slot]
                col = info[3 * slot + 1]
                keep = lax.broadcasted_iota(jnp.int32, (size, LANES), 1) >= col
                zero = jnp.zeros((size, LANES), f32)
                for plane in range(2):
                    rolled = [
                        pltpu.roll(grad[slot, plane, :, k * LANES : (k + 1) * LANES].astype(f32), lax.rem(col, LANES), 1)
                        * 0.25
                        for k in range(inner)
                    ]
                    for k in range(inner + 1):
                        here = rolled[k] if k < inner else zero
                        before = rolled[k - 1] if k > 0 else zero
                        acc[plane * parts + k, pl.ds(row, size), :] -= jnp.where(keep, here, before)

            return carry

        lax.fori_loop(0, capacity, one, 0)
    for plane in range(2):
        for k in range(parts):
            out[plane, :, k * LANES : (k + 1) * LANES] = acc[plane * parts + k]


def scatter(base, infos, grads, capacity, size):
    count = len(grads)
    _, rows, cols = base.shape
    full = pl.BlockSpec(memory_space=pltpu.VMEM)
    return pl.pallas_call(
        functools.partial(scatter_kernel, count, capacity, size),
        in_specs=[full] * (1 + 2 * count),
        out_specs=full,
        out_shape=jax.ShapeDtypeStruct(base.shape, f32),
        scratch_shapes=[
            pltpu.SMEM((3 * capacity,), jnp.int32),
            pltpu.VMEM((2 * cols // LANES, rows, LANES), f32),
        ],
        compiler_params=pltpu.CompilerParams(vmem_limit_bytes=VMEM_LIMIT),
        cost_estimate=pl.CostEstimate(flops=2**30, bytes_accessed=2**23, transcendentals=0),
        name="scatter",
    )(base, *infos, *grads)


def with_halo(block, sides, width):
    for axis, dim in sides:
        count = lax.axis_size(axis)
        forward = [(i, (i + 1) % count) for i in range(count)]
        backward = [(target, source) for source, target in forward]
        low = lax.ppermute(lax.slice_in_dim(block, block.shape[dim] - width, None, axis=dim), axis, forward)
        high = lax.ppermute(lax.slice_in_dim(block, 0, width, axis=dim), axis, backward)
        block = jnp.concatenate([low, block, high], axis=dim)
    return block


def neighbours(tile):
    rows = with_halo(tile, (("obj", 1),), 1)
    cols = with_halo(tile, (("pos", 2),), 1)
    return rows[:, :-2] + rows[:, 2:] + cols[:, :, :-2] + cols[:, :, 2:]


def sum_everywhere(value):
    n_pos = lax.axis_size("pos")
    n_obj = lax.axis_size("obj")
    me = lax.axis_index("pos")
    rows = value.shape[1] // n_pos

    def piece(which):
        return lax.dynamic_slice_in_dim(value, which * rows, rows, axis=1)

    total = piece(me)
    for d in range(1, n_pos):
        total = total + exchange(piece(me ^ d), "pos", d)
    step = 1
    while step < n_obj:
        total = total + exchange(total, "obj", step)
        step *= 2
    result = lax.dynamic_update_slice_in_dim(value, total, me * rows, axis=1)
    for d in range(1, n_pos):
        result = lax.dynamic_update_slice_in_dim(result, exchange(total, "pos", d), (me ^ d) * rows, axis=1)
    return result


def shards(object_field, probe, amplitude, row_offset, col_offset, owner):
    n_pos = lax.axis_size("pos")
    n_obj = lax.axis_size("obj")
    pos_dev, size, _ = amplitude.shape
    capacity = max(2, pos_dev // n_pos + 1)
    left_np, right_np = dft_blocks(size)
    left = jnp.asarray(left_np)
    right = jnp.asarray(right_np)
    me = lax.axis_index("pos").astype(jnp.int32).reshape(1)
    packed = pack(me, owner, row_offset, col_offset, amplitude, n_pos, capacity)
    received = {0: packed[0]}
    order = [2, 4, 1, 3, 5, 6, 7] if n_pos == 8 else list(range(1, n_pos))
    for d in order:
        received[d] = exchange(packed[d], "pos", d)
    groups = [[0], [1], [2, 4], [3, 5], [6], [7]] if n_pos == 8 else [[d] for d in range(n_pos)]
    tile = prepare(object_field)
    term = jnp.zeros(probe.shape, f32)
    infos, grads = [], []
    for group in groups:
        outs, term = terms(tile, probe, left, right, term, [received[d] for d in group], capacity)
        grads += outs
        infos += [received[d][capacity * size :] for d in group]
    base = object_field - 0.125 * (4.0 * object_field - neighbours(object_field))
    new_object = scatter(base, infos, grads, capacity, size)
    probe_grad = sum_everywhere(term)
    new_probe = probe - probe_grad * (1.0 / math.sqrt(pos_dev * n_pos * n_obj))
    return (new_object, new_probe)


def solution(mesh):
    placed = (
        P(None, "obj", "pos"),
        P(),
        P(("pos", "obj"), None, None),
        P(("pos", "obj")),
        P(("pos", "obj")),
        P(("pos", "obj")),
    )
    return jax.shard_map(
        shards, mesh=mesh, in_specs=placed, out_specs=(P(None, "obj", "pos"), P()), check_vma=False
    )
```

time: 507 us -> 139 us (0.27)
  the two profiles are of different devices: /device:TPU:12 before, /device:TPU:0 now
where the time goes in v1:
time: 139 us; the launch traced here: 138 us
  Pallas kernels  60.2 us (43%)
  starting transfers between devices  33.4 us (24%)
  local copies, waits for them, and re-layouts  19.8 us (14%)
  waiting for transfers between devices  19.6 us (14%)
  other arithmetic  4.08 us (3%)
    pallas_call x6, Pallas kernels, terms(): pl.pallas_call(functools.partial(terms_kernel, count, capacity, size), in...  45.2 us
    ppermute x23, starting transfers between devices, exchange(): return lax.ppermute(value, axis, [(i, i ^ distance) for i in range(count)])  28.6 us
    ppermute x23, waiting for transfers between devices, exchange(): return lax.ppermute(value, axis, [(i, i ^ distance) for i in range(count)])  15.3 us
    slice x8, local copies, waits for them, and re-layouts, shards(): infos += [received[d][capacity * size:] for d in group]  10.3 us
    pallas_call x1, Pallas kernels, scatter(): pl.pallas_call(functools.partial(scatter_kernel, count, capacity, size),...  8.29 us
    unnamed x22, local copies, waits for them, and re-layouts  6.57 us
    ppermute x2, starting transfers between devices, with_halo(): lax.ppermute(lax.slice_in_dim(block, 0, width, axis=dim), axis, backward)  4.85 us
    ppermute x2, waiting for transfers between devices, with_halo(): lax.ppermute(lax.slice_in_dim(block, block.shape[dim] - width, None, axis...  4.26 us
  transfers between devices with their start and end apart: 27, of which 8 were waited for; matrix products, arithmetic and copies ran while one was open for 11% of the time, Pallas kernels for 35%

profile of v1, /device:TPU:0, one launch (start us, length us, event | category | flops | bytes accessed | tf_op | source)
XLA Modules:
  0.0 137.8 jit_solution(13100509074079181326)
XLA Ops:
  0.6 1.6 %copy-done = bf16[16,256,256]{2,1,0:T(8,128)(2,1)S(1)} copy-done((bf16[16,256,256]{2,1,0:T(8,128)(2,1)S(1)}, bf16[16,256,256]{2,1,0:T(8,128)(2,1)}, u32[]{:S(2)}) %copy-start) | copy-done | bytes 2097176
  2.2 0.7 copy-done.1
  2.9 0.7 copy-done.2
  3.5 0.7 copy-done.3
  4.2 4.0 %pack.1 = (bf16[784,256]{1,0:T(8,128)(2,1)S(1)}, bf16[784,256]{1,0:T(8,128)(2,1)S(1)}, bf16[784,256]{1,0:T(8,128)(2,1)S(1)}, bf16[784,256]{1,0:T(8,128)(2,1)S(1)...) custom-call(s32[1]{0:T(128)} %bitcast.me_ref, ...), custom_call_target="tpu_custom_call" | custom-call | tf_op jit(solution)/shard_map/pack/pallas_call | solution.py:82
  8.2 0.8 copy-done.4
  9.0 0.5 collective-permute-start.4
  9.5 2.5 %collective-permute-start.5 = (bf16[784,256]{1,0:T(8,128)(2,1)S(1)}, bf16[784,256]{1,0:T(8,128)(2,1)}, u32[]{:S(2)}, u32[]{:S(2)}) collective-permute-start(bf16[784,256]{1,0:T(8,128)(2,1)S(1)} %get-tuple-element.26), channel_id=1, source_target_pairs={{0,8},{4,12},{8,0},{12,4},{16,24},{20,28},{24,16},{28,20},{1,9},{5... | collective-permute-start | bytes 1204232 | tf_op jit(solution)/shard_map/ppermute | solution.py:33
  11.9 1.5 %collective-permute-start.6 = (bf16[784,256]{1,0:T(8,128)(2,1)S(1)}, bf16[784,256]{1,0:T(8,128)(2,1)}, u32[]{:S(2)}, u32[]{:S(2)}) collective-permute-start(bf16[784,256]{1,0:T(8,128)(2,1)S(1)} %get-tuple-element.27), channel_id=1, source_target_pairs={{0,16},{4,20},{8,24},{12,28},{16,0},{20,4},{24,8},{28,12},{1,17},{... | collective-permute-start | bytes 1204232 | tf_op jit(solution)/shard_map/ppermute | solution.py:33
  13.5 0.1 collective-permute-start.7
  13.6 0.2 collective-permute-start.8
  13.8 2.7 %prepare.1.tile = f32[6,512,128]{2,1,0:T(8,128)} custom-call(f32[2,512,384]{2,1,0:T(8,128)} %tile.1), custom_call_target="tpu_custom_call" | custom-call | tf_op jit(solution)/shard_map/prepare/pallas_call | solution.py:109
  16.4 0.8 broadcast_in_dim.3.term_in
  17.2 6.8 %terms.6 = (bf16[3,2,256,256]{3,2,1,0:T(8,128)(2,1)}, f32[2,256,256]{2,1,0:T(8,128)}) custom-call(f32[6,512,128]{2,1,0:T(8,128)} %prepare.1.tile, f32[2,256,256]{2,1,0:T(8,128)} %probe.11, bf16[512,512]{1,0:T(8,128)(2,1)} %constant.38.clone.left, bf16[512,512]{1,0:T(8,128)(2,1)} %constant.39.clone.right, f32[2,256,256]{2,1,0:T(8,128)} %broadcast_in_dim.3.term_in, ...), custom_call_target="tpu_custom_call" | custom-call | flops 6442450944 | bytes 4194304 | tf_op jit(solution)/shard_map/terms/pallas_call | solution.py:191
  24.0 0.0 collective-permute-done.4.rest_0_
  24.0 0.1 collective-permute-start.9
  24.1 0.7 copy-done.8
  24.8 5.1 %terms.7 = (bf16[3,2,256,256]{3,2,1,0:T(8,128)(2,1)}, f32[2,256,256]{2,1,0:T(8,128)}) custom-call(f32[6,512,128]{2,1,0:T(8,128)} %prepare.1.tile, f32[2,256,256]{2,1,0:T(8,128)} %probe.11, bf16[512,512]{1,0:T(8,128)(2,1)} %constant.38.clone.left, bf16[512,512]{1,0:T(8,128)(2,1)} %constant.39.clone.right, f32[2,256,256]{2,1,0:T(8,128)} %get-tuple-element.33.term_in, ...), custom_call_target="tpu_custom_call" | custom-call | flops 6442450944 | bytes 4194304 | tf_op jit(solution)/shard_map/terms/pallas_call | solution.py:191
  29.9 3.6 %collective-permute-start.10 = (bf16[784,256]{1,0:T(8,128)(2,1)S(1)}, bf16[784,256]{1,0:T(8,128)(2,1)S(1)}, u32[]{:S(2)}, u32[]{:S(2)}) collective-permute-start(bf16[784,256]{1,0:T(8,128)(2,1)S(1)} %get-tuple-element.31), channel_id=1, source_target_pairs={{0,28},{4,24},{8,20},{12,16},{16,12},{20,8},{24,4},{28,0},{1,29},{... | collective-permute-start | bytes 1204232 | tf_op jit(solution)/shard_map/ppermute | solution.py:33
  33.5 5.6 %terms.8 = (bf16[3,2,256,256]{3,2,1,0:T(8,128)(2,1)}, bf16[3,2,256,256]{3,2,1,0:T(8,128)(2,1)}, f32[2,256,256]{2,1,0:T(8,128)}) custom-call(f32[6,512,128]{2,1,0:T(8,128)} %prepare.1.tile, f32[2,256,256]{2,1,0:T(8,128)} %probe.11, bf16[512,512]{1,0:T(8,128)(2,1)} %constant.38.clone.left, bf16[512,512]{1,0:T(8,128)(2,1)} %constant.39.clone.right, ...), custom_call_target="tpu_custom_call" | custom-call | flops 12884901888 | bytes 4194304 | tf_op jit(solution)/shard_map/terms/pallas_call | solution.py:191
  39.1 9.1 %collective-permute-done.8.rest_1_ = bf16[784,256]{1,0:T(8,128)(2,1)} collective-permute-done((bf16[784,256]{1,0:T(8,128)(2,1)S(1)}, bf16[784,256]{1,0:T(8,128)(2,1)}, u32[]{:S(2)}, u32[]{:S(2)}) %collective-permute-start.8) | collective-permute-done | bytes 401440 | tf_op jit(solution)/shard_map/ppermute | solution.py:33
  48.2 12.4 %terms.9 = (bf16[3,2,256,256]{3,2,1,0:T(8,128)(2,1)}, bf16[3,2,256,256]{3,2,1,0:T(8,128)(2,1)}, f32[2,256,256]{2,1,0:T(8,128)}) custom-call(f32[6,512,128]{2,1,0:T(8,128)} %prepare.1.tile, f32[2,256,256]{2,1,0:T(8,128)} %probe.11, bf16[512,512]{1,0:T(8,128)(2,1)} %constant.38.clone.left, bf16[512,512]{1,0:T(8,128)(2,1)} %constant.39.clone.right, ...), custom_call_target="tpu_custom_call" | custom-call | flops 12884901888 | bytes 4194304 | tf_op jit(solution)/shard_map/terms/pallas_call | solution.py:191
  60.6 0.8 copy-done.9
  61.4 6.8 %terms.10 = (bf16[3,2,256,256]{3,2,1,0:T(8,128)(2,1)}, f32[2,256,256]{2,1,0:T(8,128)}) custom-call(f32[6,512,128]{2,1,0:T(8,128)} %prepare.1.tile, f32[2,256,256]{2,1,0:T(8,128)} %probe.11, bf16[512,512]{1,0:T(8,128)(2,1)} %constant.38.clone.left, bf16[512,512]{1,0:T(8,128)(2,1)} %constant.39.clone.right, f32[2,256,256]{2,1,0:T(8,128)} %get-tuple-element.41.term_in, ...), custom_call_target="tpu_custom_call" | custom-call | flops 6442450944 | bytes 4194304 | tf_op jit(solution)/shard_map/terms/pallas_call | solution.py:191
  68.2 0.8 copy-done.10
  68.9 8.6 %terms.11 = (bf16[3,2,256,256]{3,2,1,0:T(8,128)(2,1)}, f32[2,256,256]{2,1,0:T(8,128)}) custom-call(f32[6,512,128]{2,1,0:T(8,128)} %prepare.1.tile, f32[2,256,256]{2,1,0:T(8,128)} %probe.11, bf16[512,512]{1,0:T(8,128)(2,1)} %constant.38.clone.left, bf16[512,512]{1,0:T(8,128)(2,1)} %constant.39.clone.right, f32[2,256,256]{2,1,0:T(8,128)} %get-tuple-element.43.term_in, ...), custom_call_target="tpu_custom_call" | custom-call | flops 6442450944 | bytes 4194304 | tf_op jit(solution)/shard_map/terms/pallas_call | solution.py:191
  77.5 1.8 %constant_dynamic-slice_fusion.6 = (f32[2,32,256]{2,1,0:T(8,128)S(1)}, f32[2,32,256]{2,1,0:T(8,128)S(1)}, f32[2,32,256]{2,1,0:T(8,128)S(1)}, f32[2,32,256]{2,1,0...) fusion(f32[2,256,256]{2,1,0:T(8,128)} %get-tuple-element.45, ...), kind=kLoop, calls=%fused_computation.26 | loop fusion | bytes 917532 | tf_op jit(solution)/shard_map/dynamic_slice | solution.py:287
  79.3 1.7 %collective-permute-start.16 = (f32[2,32,256]{2,1,0:T(8,128)S(1)}, f32[2,32,256]{2,1,0:T(8,128)S(1)}, u32[]{:S(2)}, u32[]{:S(2)}) collective-permute-start(f32[2,32,256]{2,1,0:T(8,128)S(1)} %get-tuple-element.54), channel_id=1, source_target_pairs={{0,24},{4,28},{8,16},{12,20},{16,8},{20,12},{24,0},{28,4},{1,25},{... | collective-permute-start | bytes 196616 | tf_op jit(solution)/shard_map/ppermute | solution.py:33
  81.0 5.3 %collective-permute-start.15 = (f32[2,32,256]{2,1,0:T(8,128)}, f32[2,32,256]{2,1,0:T(8,128)S(1)}, u32[]{:S(2)}, u32[]{:S(2)}) collective-permute-start(f32[2,32,256]{2,1,0:T(8,128)} %get-tuple-element.55), channel_id=1, source_target_pairs={{0,20},{4,16},{8,28},{12,24},{16,4},{20,0},{24,12},{28,8},{1,21},{... | collective-permute-start | bytes 196616 | tf_op jit(solution)/shard_map/ppermute | solution.py:33
  86.3 0.3 collective-permute-start.14
  86.6 2.9 %collective-permute-start.13 = (f32[2,32,256]{2,1,0:T(8,128)S(1)}, f32[2,32,256]{2,1,0:T(8,128)}, u32[]{:S(2)}, u32[]{:S(2)}) collective-permute-start(f32[2,32,256]{2,1,0:T(8,128)S(1)} %get-tuple-element.57), channel_id=1, source_target_pairs={{0,12},{4,8},{8,4},{12,0},{16,28},{20,24},{24,20},{28,16},{1,13},{... | collective-permute-start | bytes 196616 | tf_op jit(solution)/shard_map/ppermute | solution.py:33
  89.5 0.6 collective-permute-start.11
  90.1 0.2 fusion.7
  90.3 1.3 collective-permute-start.3
  91.6 0.2 collective-permute-done.13
  91.8 2.0 %collective-permute-done.12 = f32[2,32,256]{2,1,0:T(8,128)} collective-permute-done((f32[2,32,256]{2,1,0:T(8,128)S(1)}, f32[2,32,256]{2,1,0:T(8,128)}, u32[]{:S(2)}, u32[]{:S(2)}) %collective-permute-start.12) | collective-permute-done | bytes 65568 | tf_op jit(solution)/shard_map/ppermute | solution.py:33
  93.8 1.0 add_add_fusion
  94.8 0.9 collective-permute-start.18
  95.7 3.5 %collective-permute-start.1 = (f32[2,1,384]{2,1,0:T(1,128)S(1)}, f32[2,1,384]{2,1,0:T(1,128)S(1)}, u32[]{:S(2)}, u32[]{:S(2)}) collective-permute-start(f32[2,1,384]{2,1,0:T(1,128)S(1)} %get-tuple-element.49), channel_id=1, source_target_pairs={{1,0},{2,1},{3,2},{0,3},{5,4},{6,5},{7,6},{4,7},{9,8},{10,9},{11,1... | collective-permute-start | bytes 9224 | tf_op jit(solution)/shard_map/ppermute | solution.py:269
  99.2 1.3 slice.60.rest_0_
  100.6 1.6 %collective-permute-start.19 = (f32[2,32,256]{2,1,0:T(8,128)S(1)}, f32[2,32,256]{2,1,0:T(8,128)S(1)}, u32[]{:S(2)}, u32[]{:S(2)}) collective-permute-start(f32[2,32,256]{2,1,0:T(8,128)S(1)} %add.86), channel_id=1, source_target_pairs={{0,2},{1,3},{2,0},{3,1},{4,6},{5,7},{6,4},{7,5},{8,10},{9,11},{10,... | collective-permute-start | bytes 196616 | tf_op jit(solution)/shard_map/ppermute | solution.py:33
  102.2 2.5 %collective-permute-done = f32[2,1,384]{2,1,0:T(1,128)S(1)} collective-permute-done((f32[2,1,384]{2,1,0:T(1,128)S(1)}, f32[2,1,384]{2,1,0:T(1,128)S(1)}, u32[]{:S(2)}, u32[]{:S(2)}) %collective-permute-start) | collective-permute-done | bytes 3104 | tf_op jit(solution)/shard_map/ppermute | solution.py:268
  104.7 1.8 %collective-permute-done.2 = f32[2,512,1]{2,1,0:T(8,128)S(1)} collective-permute-done((f32[2,512,1]{2,1,0:T(8,128)S(1)}, f32[2,512,1]{2,1,0:T(8,128)S(1)}, u32[]{:S(2)}, u32[]{:S(2)}) %collective-permute-start.2) | collective-permute-done | bytes 4128 | tf_op jit(solution)/shard_map/ppermute | solution.py:268
  106.4 2.2 %fusion.3.base = f32[2,512,384]{2,1,0:T(8,128)} fusion(f32[2,512,384]{2,1,0:T(8,128)S(1)} %copy-done.5, f32[2,512,1]{2,1,0:T(8,128)S(1)} %collective-permute-done.3, f32[2,512,1]{2,1,0:T(8,128)S(1)} %collective-permute-done.2, f32[2,1,384]{2,1,0:T(1,128)S(1)} %collective-permute-done.1, f32[2,1,384]{2,1,0:T(1,128)S(1)} %collective-permute-done), kind=kLoop, calls=%fused_computation.4 | loop fusion | flops 4325376 | bytes 3160064 | tf_op jit(solution)/shard_map/sub | solution.py:324
  108.6 1.3 slice.68.rest_1_
  109.9 1.3 slice.69.rest_2_
  111.2 1.3 slice.70.rest_3_
  112.5 1.3 slice.71.rest_4_
  113.8 1.3 slice.72.rest_5_
  115.1 1.3 slice.73.rest_6_
  116.4 1.3 slice.74.rest_7_
  117.7 0.1 collective-permute-start.20
  117.8 0.0 copy-start.7
  117.8 8.3 %scatter.1 = f32[2,512,384]{2,1,0:T(8,128)} custom-call(f32[2,512,384]{2,1,0:T(8,128)} %fusion.3.base, bf16[16,256]{1,0:T(8,128)(2,1)} %slice.60.rest_0_, bf16[16,256]{1,0:T(8,128)(2,1)} %slice.68.rest_1_, bf16[16,256]{1,0:T(8,128)(2,1)} %slice.69.rest_2_, bf16[16,256]{1,0:T(8,128)(2,1)} %slice.70.rest_3_, bf16[16,256]{1,0:T(8,128)(2,1)} %slice.71.rest_4_, ...), custom_call_target="tpu_custom_call" | custom-call | flops 1073741824 | bytes 8388608 | tf_op jit(solution)/shard_map/scatter/pallas_call | solution.py:248
  126.1 1.3 collective-permute-start.21
  127.4 1.1 collective-permute-start.22
  128.5 0.0 collective-permute-start.23
  128.5 1.4 collective-permute-start.24
  129.9 1.7 %collective-permute-start.25 = (f32[2,32,256]{2,1,0:T(8,128)S(1)}, f32[2,32,256]{2,1,0:T(8,128)S(1)}, u32[]{:S(2)}, u32[]{:S(2)}) collective-permute-start(f32[2,32,256]{2,1,0:T(8,128)S(1)} %get-tuple-element.47), channel_id=1, source_target_pairs={{0,24},{4,28},{8,16},{12,20},{16,8},{20,12},{24,0},{28,4},{1,25},{... | collective-permute-start | bytes 196616 | tf_op jit(solution)/shard_map/ppermute | solution.py:33
  131.6 1.3 collective-permute-start.26
  133.0 0.2 collective-permute-done.23
  133.3 2.2 %collective-permute-done.25 = f32[2,32,256]{2,1,0:T(8,128)S(1)} collective-permute-done((f32[2,32,256]{2,1,0:T(8,128)S(1)}, f32[2,32,256]{2,1,0:T(8,128)S(1)}, u32[]{:S(2)}, u32[]{:S(2)}) %collective-permute-start.25) | collective-permute-done | bytes 65568 | tf_op jit(solution)/shard_map/ppermute | solution.py:33
  135.5 1.4 %collective-permute-done.26 = f32[2,32,256]{2,1,0:T(8,128)S(1)} collective-permute-done((f32[2,32,256]{2,1,0:T(8,128)S(1)}, f32[2,32,256]{2,1,0:T(8,128)S(1)}, u32[]{:S(2)}, u32[]{:S(2)}) %collective-permute-start.26) | collective-permute-done | bytes 65568 | tf_op jit(solution)/shard_map/ppermute | solution.py:33
  137.0 0.9 multiply_subtract_fusion
  (45 shorter events, 0.2 us)
Async XLA Ops:
  0.6 1.6 %copy-start = (bf16[16,256,256]{2,1,0:T(8,128)(2,1)S(1)}, bf16[16,256,256]{2,1,0:T(8,128)(2,1)}, u32[]{:S(2)}) copy-start(bf16[16,256,256]{2,1,0:T(8,128)(2,1)} %amp.1) | copy-start | bytes 6291460
  2.2 0.7 copy-start.1
  2.9 0.7 copy-start.2
  3.5 0.7 copy-start.3
  8.2 0.8 copy-start.4
  9.0 15.0 %collective-permute-start.4 = (bf16[784,256]{1,0:T(8,128)(2,1)S(1)}, bf16[784,256]{1,0:T(8,128)(2,1)S(1)}, u32[]{:S(2)}, u32[]{:S(2)}) collective-permute-start(bf16[784,256]{1,0:T(8,128)(2,1)S(1)} %get-tuple-element.25), channel_id=1, source_target_pairs={{0,4},{4,0},{8,12},{12,8},{16,20},{20,16},{24,28},{28,24},{1,5},{5... | collective-permute-start | bytes 1204232 | tf_op jit(solution)/shard_map/ppermute | solution.py:33
  9.5 20.4 %collective-permute-start.5 = (bf16[784,256]{1,0:T(8,128)(2,1)S(1)}, bf16[784,256]{1,0:T(8,128)(2,1)}, u32[]{:S(2)}, u32[]{:S(2)}) collective-permute-start(bf16[784,256]{1,0:T(8,128)(2,1)S(1)} %get-tuple-element.26), channel_id=1, source_target_pairs={{0,8},{4,12},{8,0},{12,4},{16,24},{20,28},{24,16},{28,20},{1,9},{5... | collective-permute-start | bytes 1204232 | tf_op jit(solution)/shard_map/ppermute | solution.py:33
  11.9 21.5 %collective-permute-start.6 = (bf16[784,256]{1,0:T(8,128)(2,1)S(1)}, bf16[784,256]{1,0:T(8,128)(2,1)}, u32[]{:S(2)}, u32[]{:S(2)}) collective-permute-start(bf16[784,256]{1,0:T(8,128)(2,1)S(1)} %get-tuple-element.27), channel_id=1, source_target_pairs={{0,16},{4,20},{8,24},{12,28},{16,0},{20,4},{24,8},{28,12},{1,17},{... | collective-permute-start | bytes 1204232 | tf_op jit(solution)/shard_map/ppermute | solution.py:33
  13.5 25.6 %collective-permute-start.7 = (bf16[784,256]{1,0:T(8,128)(2,1)S(1)}, bf16[784,256]{1,0:T(8,128)(2,1)}, u32[]{:S(2)}, u32[]{:S(2)}) collective-permute-start(bf16[784,256]{1,0:T(8,128)(2,1)S(1)} %get-tuple-element.28), channel_id=1, source_target_pairs={{0,12},{4,8},{8,4},{12,0},{16,28},{20,24},{24,20},{28,16},{1,13},{... | collective-permute-start | bytes 1204232 | tf_op jit(solution)/shard_map/ppermute | solution.py:33
  13.6 34.6 %collective-permute-start.8 = (bf16[784,256]{1,0:T(8,128)(2,1)S(1)}, bf16[784,256]{1,0:T(8,128)(2,1)}, u32[]{:S(2)}, u32[]{:S(2)}) collective-permute-start(bf16[784,256]{1,0:T(8,128)(2,1)S(1)} %get-tuple-element.29), channel_id=1, source_target_pairs={{0,20},{4,16},{8,28},{12,24},{16,4},{20,0},{24,12},{28,8},{1,21},{... | collective-permute-start | bytes 1204232 | tf_op jit(solution)/shard_map/ppermute | solution.py:33
  24.0 0.8 copy-start.8
  24.0 36.6 %collective-permute-start.9 = (bf16[784,256]{1,0:T(8,128)(2,1)S(1)}, bf16[784,256]{1,0:T(8,128)(2,1)S(1)}, u32[]{:S(2)}, u32[]{:S(2)}) collective-permute-start(bf16[784,256]{1,0:T(8,128)(2,1)S(1)} %get-tuple-element.30), channel_id=1, source_target_pairs={{0,24},{4,28},{8,16},{12,20},{16,8},{20,12},{24,0},{28,4},{1,25},{... | collective-permute-start | bytes 1204232 | tf_op jit(solution)/shard_map/ppermute | solution.py:33
  29.9 38.3 %collective-permute-start.10 = (bf16[784,256]{1,0:T(8,128)(2,1)S(1)}, bf16[784,256]{1,0:T(8,128)(2,1)S(1)}, u32[]{:S(2)}, u32[]{:S(2)}) collective-permute-start(bf16[784,256]{1,0:T(8,128)(2,1)S(1)} %get-tuple-element.31), channel_id=1, source_target_pairs={{0,28},{4,24},{8,20},{12,16},{16,12},{20,8},{24,4},{28,0},{1,29},{... | collective-permute-start | bytes 1204232 | tf_op jit(solution)/shard_map/ppermute | solution.py:33
  60.6 0.8 copy-start.9
  68.2 0.8 copy-start.10
  68.9 21.1 %copy-start.5 = (f32[2,512,384]{2,1,0:T(8,128)S(1)}, f32[2,512,384]{2,1,0:T(8,128)}, u32[]{:S(2)}) copy-start(f32[2,512,384]{2,1,0:T(8,128)} %tile.1) | copy-start | bytes 4718596
  77.5 16.3 %copy-start.6 = (f32[2,256,256]{2,1,0:T(8,128)S(1)}, f32[2,256,256]{2,1,0:T(8,128)}, u32[]{:S(2)}) copy-start(f32[2,256,256]{2,1,0:T(8,128)} %get-tuple-element.45) | copy-start | bytes 1572868
  79.3 10.2 %collective-permute-start.17 = (f32[2,32,256]{2,1,0:T(8,128)S(1)}, f32[2,32,256]{2,1,0:T(8,128)S(1)}, u32[]{:S(2)}, u32[]{:S(2)}) collective-permute-start(f32[2,32,256]{2,1,0:T(8,128)S(1)} %get-tuple-element.53), channel_id=1, source_target_pairs={{0,28},{4,24},{8,20},{12,16},{16,12},{20,8},{24,4},{28,0},{1,29},{... | collective-permute-start | bytes 196616 | tf_op jit(solution)/shard_map/ppermute | solution.py:33
  79.3 10.2 %collective-permute-start.16 = (f32[2,32,256]{2,1,0:T(8,128)S(1)}, f32[2,32,256]{2,1,0:T(8,128)S(1)}, u32[]{:S(2)}, u32[]{:S(2)}) collective-permute-start(f32[2,32,256]{2,1,0:T(8,128)S(1)} %get-tuple-element.54), channel_id=1, source_target_pairs={{0,24},{4,28},{8,16},{12,20},{16,8},{20,12},{24,0},{28,4},{1,25},{... | collective-permute-start | bytes 196616 | tf_op jit(solution)/shard_map/ppermute | solution.py:33
  81.0 9.2 %collective-permute-start.15 = (f32[2,32,256]{2,1,0:T(8,128)}, f32[2,32,256]{2,1,0:T(8,128)S(1)}, u32[]{:S(2)}, u32[]{:S(2)}) collective-permute-start(f32[2,32,256]{2,1,0:T(8,128)} %get-tuple-element.55), channel_id=1, source_target_pairs={{0,20},{4,16},{8,28},{12,24},{16,4},{20,0},{24,12},{28,8},{1,21},{... | collective-permute-start | bytes 196616 | tf_op jit(solution)/shard_map/ppermute | solution.py:33
  86.3 5.3 %collective-permute-start.14 = (f32[2,32,256]{2,1,0:T(8,128)}, f32[2,32,256]{2,1,0:T(8,128)}, u32[]{:S(2)}, u32[]{:S(2)}) collective-permute-start(f32[2,32,256]{2,1,0:T(8,128)} %get-tuple-element.56), channel_id=1, source_target_pairs={{0,16},{4,20},{8,24},{12,28},{16,0},{20,4},{24,8},{28,12},{1,17},{... | collective-permute-start | bytes 196616 | tf_op jit(solution)/shard_map/ppermute | solution.py:33
  86.6 5.3 %collective-permute-start.13 = (f32[2,32,256]{2,1,0:T(8,128)S(1)}, f32[2,32,256]{2,1,0:T(8,128)}, u32[]{:S(2)}, u32[]{:S(2)}) collective-permute-start(f32[2,32,256]{2,1,0:T(8,128)S(1)} %get-tuple-element.57), channel_id=1, source_target_pairs={{0,12},{4,8},{8,4},{12,0},{16,28},{20,24},{24,20},{28,16},{1,13},{... | collective-permute-start | bytes 196616 | tf_op jit(solution)/shard_map/ppermute | solution.py:33
  89.5 4.4 %collective-permute-start.12 = (f32[2,32,256]{2,1,0:T(8,128)S(1)}, f32[2,32,256]{2,1,0:T(8,128)}, u32[]{:S(2)}, u32[]{:S(2)}) collective-permute-start(f32[2,32,256]{2,1,0:T(8,128)S(1)} %get-tuple-element.58), channel_id=1, source_target_pairs={{0,8},{4,12},{8,0},{12,4},{16,24},{20,28},{24,16},{28,20},{1,9},{5... | collective-permute-start | bytes 196616 | tf_op jit(solution)/shard_map/ppermute | solution.py:33
  89.5 4.4 %collective-permute-start.11 = (f32[2,32,256]{2,1,0:T(8,128)S(1)}, f32[2,32,256]{2,1,0:T(8,128)}, u32[]{:S(2)}, u32[]{:S(2)}) collective-permute-start(f32[2,32,256]{2,1,0:T(8,128)S(1)} %get-tuple-element.52), channel_id=1, source_target_pairs={{0,4},{4,0},{8,12},{12,8},{16,20},{20,16},{24,28},{28,24},{1,5},{5... | collective-permute-start | bytes 196616 | tf_op jit(solution)/shard_map/ppermute | solution.py:33
  90.3 14.4 %collective-permute-start.3 = (f32[2,512,1]{2,1,0:T(8,128)S(1)}, f32[2,512,1]{2,1,0:T(8,128)S(1)}, u32[]{:S(2)}, u32[]{:S(2)}) collective-permute-start(f32[2,512,1]{2,1,0:T(8,128)S(1)} %get-tuple-element.51), channel_id=1, source_target_pairs={{4,0},{8,4},{12,8},{16,12},{20,16},{24,20},{28,24},{0,28},{5,1},{9... | collective-permute-start | bytes 12296 | tf_op jit(solution)/shard_map/ppermute | solution.py:269
  91.6 14.8 %collective-permute-start.2 = (f32[2,512,1]{2,1,0:T(8,128)S(1)}, f32[2,512,1]{2,1,0:T(8,128)S(1)}, u32[]{:S(2)}, u32[]{:S(2)}) collective-permute-start(f32[2,512,1]{2,1,0:T(8,128)S(1)} %get-tuple-element.50), channel_id=1, source_target_pairs={{0,4},{4,8},{8,12},{12,16},{16,20},{20,24},{24,28},{28,0},{1,5},{5... | collective-permute-start | bytes 12296 | tf_op jit(solution)/shard_map/ppermute | solution.py:268
  94.8 5.7 %collective-permute-start.18 = (f32[2,32,256]{2,1,0:T(8,128)S(1)}, f32[2,32,256]{2,1,0:T(8,128)S(1)}, u32[]{:S(2)}, u32[]{:S(2)}) collective-permute-start(f32[2,32,256]{2,1,0:T(8,128)S(1)} %add_add_fusion), channel_id=1, source_target_pairs={{0,1},{1,0},{2,3},{3,2},{4,5},{5,4},{6,7},{7,6},{8,9},{9,8},{10,11... | collective-permute-start | bytes 196616 | tf_op jit(solution)/shard_map/ppermute | solution.py:33
  95.7 6.4 %collective-permute-start.1 = (f32[2,1,384]{2,1,0:T(1,128)S(1)}, f32[2,1,384]{2,1,0:T(1,128)S(1)}, u32[]{:S(2)}, u32[]{:S(2)}) collective-permute-start(f32[2,1,384]{2,1,0:T(1,128)S(1)} %get-tuple-element.49), channel_id=1, source_target_pairs={{1,0},{2,1},{3,2},{0,3},{5,4},{6,5},{7,6},{4,7},{9,8},{10,9},{11,1... | collective-permute-start | bytes 9224 | tf_op jit(solution)/shard_map/ppermute | solution.py:269
  99.2 5.4 %collective-permute-start = (f32[2,1,384]{2,1,0:T(1,128)S(1)}, f32[2,1,384]{2,1,0:T(1,128)S(1)}, u32[]{:S(2)}, u32[]{:S(2)}) collective-permute-start(f32[2,1,384]{2,1,0:T(1,128)S(1)} %get-tuple-element.48), channel_id=1, source_target_pairs={{0,1},{1,2},{2,3},{3,0},{4,5},{5,6},{6,7},{7,4},{8,9},{9,10},{10,1... | collective-permute-start | bytes 9224 | tf_op jit(solution)/shard_map/ppermute | solution.py:268
  100.6 17.1 %collective-permute-start.19 = (f32[2,32,256]{2,1,0:T(8,128)S(1)}, f32[2,32,256]{2,1,0:T(8,128)S(1)}, u32[]{:S(2)}, u32[]{:S(2)}) collective-permute-start(f32[2,32,256]{2,1,0:T(8,128)S(1)} %add.86), channel_id=1, source_target_pairs={{0,2},{1,3},{2,0},{3,1},{4,6},{5,7},{6,4},{7,5},{8,10},{9,11},{10,... | collective-permute-start | bytes 196616 | tf_op jit(solution)/shard_map/ppermute | solution.py:33
  117.7 12.2 %collective-permute-start.20 = (f32[2,32,256]{2,1,0:T(8,128)S(1)}, f32[2,32,256]{2,1,0:T(8,128)S(1)}, u32[]{:S(2)}, u32[]{:S(2)}) collective-permute-start(f32[2,32,256]{2,1,0:T(8,128)S(1)} %get-tuple-element.47), channel_id=1, source_target_pairs={{0,4},{4,0},{8,12},{12,8},{16,20},{20,16},{24,28},{28,24},{1,5},{5... | collective-permute-start | bytes 196616 | tf_op jit(solution)/shard_map/ppermute | solution.py:33
  117.8 19.2 %copy-start.7 = (f32[2,256,256]{2,1,0:T(8,128)S(1)}, f32[2,256,256]{2,1,0:T(8,128)}, u32[]{:S(2)}) copy-start(f32[2,256,256]{2,1,0:T(8,128)} %probe.11) | copy-start | bytes 1572868
  126.1 5.5 %collective-permute-start.21 = (f32[2,32,256]{2,1,0:T(8,128)S(1)}, f32[2,32,256]{2,1,0:T(8,128)S(1)}, u32[]{:S(2)}, u32[]{:S(2)}) collective-permute-start(f32[2,32,256]{2,1,0:T(8,128)S(1)} %get-tuple-element.47), channel_id=1, source_target_pairs={{0,8},{4,12},{8,0},{12,4},{16,24},{20,28},{24,16},{28,20},{1,9},{5... | collective-permute-start | bytes 196616 | tf_op jit(solution)/shard_map/ppermute | solution.py:33
  127.4 5.6 %collective-permute-start.22 = (f32[2,32,256]{2,1,0:T(8,128)S(1)}, f32[2,32,256]{2,1,0:T(8,128)S(1)}, u32[]{:S(2)}, u32[]{:S(2)}) collective-permute-start(f32[2,32,256]{2,1,0:T(8,128)S(1)} %get-tuple-element.47), channel_id=1, source_target_pairs={{0,12},{4,8},{8,4},{12,0},{16,28},{20,24},{24,20},{28,16},{1,13},{... | collective-permute-start | bytes 196616 | tf_op jit(solution)/shard_map/ppermute | solution.py:33
  128.5 4.8 %collective-permute-start.23 = (f32[2,32,256]{2,1,0:T(8,128)S(1)}, f32[2,32,256]{2,1,0:T(8,128)S(1)}, u32[]{:S(2)}, u32[]{:S(2)}) collective-permute-start(f32[2,32,256]{2,1,0:T(8,128)S(1)} %get-tuple-element.47), channel_id=1, source_target_pairs={{0,16},{4,20},{8,24},{12,28},{16,0},{20,4},{24,8},{28,12},{1,17},{... | collective-permute-start | bytes 196616 | tf_op jit(solution)/shard_map/ppermute | solution.py:33
  128.5 4.7 %collective-permute-start.24 = (f32[2,32,256]{2,1,0:T(8,128)S(1)}, f32[2,32,256]{2,1,0:T(8,128)S(1)}, u32[]{:S(2)}, u32[]{:S(2)}) collective-permute-start(f32[2,32,256]{2,1,0:T(8,128)S(1)} %get-tuple-element.47), channel_id=1, source_target_pairs={{0,20},{4,16},{8,28},{12,24},{16,4},{20,0},{24,12},{28,8},{1,21},{... | collective-permute-start | bytes 196616 | tf_op jit(solution)/shard_map/ppermute | solution.py:33
  129.9 5.6 %collective-permute-start.25 = (f32[2,32,256]{2,1,0:T(8,128)S(1)}, f32[2,32,256]{2,1,0:T(8,128)S(1)}, u32[]{:S(2)}, u32[]{:S(2)}) collective-permute-start(f32[2,32,256]{2,1,0:T(8,128)S(1)} %get-tuple-element.47), channel_id=1, source_target_pairs={{0,24},{4,28},{8,16},{12,20},{16,8},{20,12},{24,0},{28,4},{1,25},{... | collective-permute-start | bytes 196616 | tf_op jit(solution)/shard_map/ppermute | solution.py:33
  131.6 5.3 %collective-permute-start.26 = (f32[2,32,256]{2,1,0:T(8,128)S(1)}, f32[2,32,256]{2,1,0:T(8,128)S(1)}, u32[]{:S(2)}, u32[]{:S(2)}) collective-permute-start(f32[2,32,256]{2,1,0:T(8,128)S(1)} %get-tuple-element.47), channel_id=1, source_target_pairs={{0,28},{4,24},{8,20},{12,16},{16,12},{20,8},{24,4},{28,0},{1,29},{... | collective-permute-start | bytes 196616 | tf_op jit(solution)/shard_map/ppermute | solution.py:33

commit v2 on v0

v2 whole, which is shorter than its diff:
```python
import functools
import math

import jax
import jax.numpy as jnp
import numpy as np
from jax import lax
from jax.experimental import pallas as pl
from jax.experimental.pallas import tpu as pltpu
from jax.sharding import PartitionSpec as P

LANES = 128
INFO_ROWS = 16
SUBLANES = 8
PACK_VMEM = 60 * 2**20
SMALL_VMEM = 16 * 2**20
TERMS_VMEM = 32 * 2**20
bf16 = jnp.bfloat16
f32 = jnp.float32


def dft_blocks(size):
    index = np.arange(size, dtype=np.int32)
    product = index[:, None] * index[None, :] % size
    angle = product.astype(np.float32) * np.float32(2.0 * math.pi / size)
    scale = np.float32(1.0 / math.sqrt(size))
    real_part = (np.cos(angle) * scale).astype(bf16)
    imag_part = (-np.sin(angle) * scale).astype(bf16)
    left = np.block([[real_part, -imag_part], [imag_part, real_part]])
    right = np.block([[real_part, imag_part], [-imag_part, real_part]])
    return left, right


def exchange(value, axis, distance):
    count = lax.axis_size(axis)
    return lax.ppermute(value, axis, [(i, i ^ distance) for i in range(count)])


def dot(a, b):
    return jnp.dot(a, b, preferred_element_type=f32)


def rim_width(cols, size):
    return -(-cols // size)


def pack_kernel(n_pos, capacity, order, owner_in, row_in, col_in, amp_in, tile, *rest):
    outs, rim = rest[:n_pos], rest[n_pos]
    owner, row, col, counts, source, amp, sides, ends, edges, info, rim_rows = rest[n_pos + 1 : n_pos + 12]
    int_sems, amp_sem, side_sems, end_sems, out_sems, info_sems = rest[n_pos + 12 :]
    pos_dev, size, _ = amp_in.shape
    _, rows, cols = tile.shape
    int_loads = [
        pltpu.make_async_copy(src, dst, int_sems.at[i])
        for i, (src, dst) in enumerate(((owner_in, owner), (row_in, row), (col_in, col)))
    ]
    amp_load = pltpu.make_async_copy(amp_in, amp, amp_sem)
    side_loads = [
        pltpu.make_async_copy(tile.at[:, :, pl.ds(first, LANES)], sides.at[i], side_sems.at[i])
        for i, first in enumerate((0, cols - LANES))
    ]
    end_loads = [
        pltpu.make_async_copy(tile.at[:, pl.ds(first, SUBLANES), :], ends.at[i], end_sems.at[i])
        for i, first in enumerate((0, rows - SUBLANES))
    ]
    for load in int_loads + [amp_load] + end_loads + side_loads:
        load.start()
    me = lax.axis_index("pos")
    for slot in range(n_pos * capacity):
        source[slot] = 0
    for q in range(n_pos):
        counts[q] = 0
    for load in int_loads:
        load.wait()
    for item in range(pos_dev):
        who = owner[item]
        rank = counts[who]
        source[who * capacity + rank] = item
        counts[who] = rank + 1
    stores = []
    amp_load.wait()
    for d in order:
        partner = jnp.bitwise_xor(me, d)
        for k in range(capacity):
            item = source[partner * capacity + k]
            store = pltpu.make_async_copy(amp.at[item], outs[d].at[pl.ds(k * size, size)], out_sems.at[d, k])
            store.start()
            stores.append(store)
    edges[...] = jnp.zeros(edges.shape, f32)
    place = 1
    for i, lane_of_edge in enumerate((0, LANES - 1)):
        pick = (lax.broadcasted_iota(jnp.int32, (SUBLANES, LANES), 1) == lane_of_edge).astype(bf16)
        side_loads[i].wait()
        for plane in range(2):
            turned = lax.dot_general(
                pick, sides[i, plane].astype(bf16), (((1,), (1,)), ((), ())), preferred_element_type=f32
            )
            for part in range(rows // size):
                edges[place : place + 1, :] = turned[0:1, part * size : (part + 1) * size]
                place += 1
    edge_block = edges[...]
    lane = lax.broadcasted_iota(jnp.int32, (INFO_ROWS, size), 1)
    at_info = lax.broadcasted_iota(jnp.int32, (INFO_ROWS, size), 0) == 0
    for d in order:
        partner = jnp.bitwise_xor(me, d)
        held = counts[partner]
        block = jnp.zeros((INFO_ROWS, size), f32)
        for k in range(capacity):
            item = source[partner * capacity + k]
            for j, number in enumerate((row[item], col[item], (k < held).astype(jnp.int32))):
                block = jnp.where(lane == 3 * k + j, number.astype(f32), block)
        info[d] = jnp.where(at_info, block, edge_block).astype(bf16)
        store = pltpu.make_async_copy(info.at[d], outs[d].at[pl.ds(capacity * size, INFO_ROWS)], info_sems.at[d])
        store.start()
        stores.append(store)
    rim_rows[...] = jnp.zeros(rim_rows.shape, f32)
    for i, at in enumerate((0, SUBLANES - 1)):
        end_loads[i].wait()
        for plane in range(2):
            for part, first in enumerate(range(0, cols, size)):
                width = min(size, cols - first)
                place = i * rim_width(cols, size) + part
                rim_rows[plane, place : place + 1, :width] = ends[i, plane, at : at + 1, first : first + width]
    store = pltpu.make_async_copy(rim_rows, rim, end_sems.at[2])
    store.start()
    stores.append(store)
    for store in stores:
        store.wait()


def pack(owner, row, col, amplitude, tile, n_pos, capacity, order):
    pos_dev, size, _ = amplitude.shape
    _, rows, cols = tile.shape
    far = pl.BlockSpec(memory_space=pltpu.HBM)
    ints = pltpu.SMEM((pos_dev,), jnp.int32)
    return pl.pallas_call(
        functools.partial(pack_kernel, n_pos, capacity, order),
        in_specs=[far] * 5,
        out_specs=[far] * (n_pos + 1),
        out_shape=[jax.ShapeDtypeStruct((capacity * size + INFO_ROWS, size), bf16)] * n_pos
        + [jax.ShapeDtypeStruct((2, SUBLANES, size), f32)],
        scratch_shapes=[
            ints,
            ints,
            ints,
            pltpu.SMEM((n_pos,), jnp.int32),
            pltpu.SMEM((n_pos * capacity,), jnp.int32),
            pltpu.VMEM(amplitude.shape, bf16),
            pltpu.VMEM((2, 2, rows, LANES), f32),
            pltpu.VMEM((2, 2, SUBLANES, cols), f32),
            pltpu.VMEM((INFO_ROWS, size), f32),
            pltpu.VMEM((n_pos, INFO_ROWS, size), bf16),
            pltpu.VMEM((2, SUBLANES, size), f32),
            pltpu.SemaphoreType.DMA((3,)),
            pltpu.SemaphoreType.DMA,
            pltpu.SemaphoreType.DMA((2,)),
            pltpu.SemaphoreType.DMA((3,)),
            pltpu.SemaphoreType.DMA((n_pos, capacity)),
            pltpu.SemaphoreType.DMA((n_pos,)),
        ],
        compiler_params=pltpu.CompilerParams(vmem_limit_bytes=PACK_VMEM),
        cost_estimate=pl.CostEstimate(flops=2**20, bytes_accessed=2**20, transcendentals=0),
        name="pack",
    )(owner, row, col, amplitude, tile)


def read_info(block, count):
    lane = lax.broadcasted_iota(jnp.int32, block.shape, 1)
    first = lax.broadcasted_iota(jnp.int32, block.shape, 0) == 0
    values = block.astype(f32)
    return [jnp.sum(jnp.where(first & (lane == j), values, 0.0)).astype(jnp.int32) for j in range(count)]


def window(tile, plane, row, col, size, parts):
    shift = lax.rem(LANES - col, LANES)
    keep = lax.broadcasted_iota(jnp.int32, (size, LANES), 1) < LANES - col
    rolled = [pltpu.roll(tile[plane * parts + k, pl.ds(row, size), :], shift, 1) for k in range(size // LANES + 1)]
    return jnp.concatenate([jnp.where(keep, rolled[k], rolled[k + 1]) for k in range(size // LANES)], axis=1)


def add_window(acc, plane, row, col, value, size, parts):
    inner = size // LANES
    keep = lax.broadcasted_iota(jnp.int32, (size, LANES), 1) >= col
    zero = jnp.zeros((size, LANES), f32)
    rolled = [pltpu.roll(value[:, k * LANES : (k + 1) * LANES], lax.rem(col, LANES), 1) for k in range(inner)]
    for k in range(inner + 1):
        here = rolled[k] if k < inner else zero
        before = rolled[k - 1] if k > 0 else zero
        acc[plane * parts + k, pl.ds(row, size), :] += jnp.where(keep, here, before)


def side_by_side(stacked, size):
    return jnp.concatenate([stacked[:size], stacked[size:]], axis=1)


def buffer_terms(amp, amp_load, info, tile, probe, left, right, acc, term, capacity, size, parts):
    numbers = read_info(info, 3 * capacity)
    slots = [tuple(numbers[3 * k : 3 * k + 3]) for k in range(capacity)]
    probe_re = probe[0]
    probe_im = probe[1]
    patches, psis = [], []
    for row, col, _ in slots:
        patch_re = window(tile, 0, row, col, size, parts)
        patch_im = window(tile, 1, row, col, size, parts)
        patches.append((patch_re.astype(bf16), patch_im.astype(bf16)))
        psi_re = (probe_re * patch_re - probe_im * patch_im).astype(bf16)
        psi_im = (probe_re * patch_im + probe_im * patch_re).astype(bf16)
        psis.append(jnp.concatenate([psi_re, psi_im], axis=0))
    halves = [side_by_side(dot(left[...], psi).astype(bf16), size) for psi in psis]
    waves = [dot(half, right[...]) for half in halves]
    diffs = []
    amp_load.wait()
    for k, wave in enumerate(waves):
        wave_re = wave[:, :size]
        wave_im = wave[:, size:]
        square = wave_re * wave_re + wave_im * wave_im
        measured = amp[k * size : (k + 1) * size, :].astype(f32)
        factor = 1.0 - measured * lax.rsqrt(jnp.maximum(square, 0.25))
        diffs.append(jnp.concatenate([(wave_re * factor).astype(bf16), (wave_im * factor).astype(bf16)], axis=0))
    backs = [side_by_side(dot(right[...], diff).astype(bf16), size) for diff in diffs]
    chis = [dot(back, left[...]) for back in backs]
    sum_re = sum_im = 0.0
    for (row, col, valid), (patch_re, patch_im), chi in zip(slots, patches, chis):
        weight = valid.astype(f32)
        chi_re = chi[:, :size] * weight
        chi_im = chi[:, size:] * weight
        grad_re = (probe_re * chi_re + probe_im * chi_im).astype(bf16).astype(f32)
        grad_im = (probe_re * chi_im - probe_im * chi_re).astype(bf16).astype(f32)
        add_window(acc, 0, row, col, grad_re, size, parts)
        add_window(acc, 1, row, col, grad_im, size, parts)
        patch_re = patch_re.astype(f32)
        patch_im = patch_im.astype(f32)
        sum_re += patch_re * chi_re + patch_im * chi_im
        sum_im += patch_re * chi_im - patch_im * chi_re
    term[0] += sum_re
    term[1] += sum_im


def terms_kernel(count, capacity, first, last, probe, left, right, *rest):
    size = probe.shape[1]
    held, infos, sems = rest[-3:]
    messages, rest = rest[:count], rest[count:-3]
    info_loads, amp_loads = [], []
    for i, message in enumerate(messages):
        info_rows = pl.ds(capacity * size, INFO_ROWS)
        amp_rows = pl.ds(0, capacity * size)
        info_loads.append(pltpu.make_async_copy(message.at[info_rows], infos.at[i], sems.at[i, 0]))
        amp_loads.append(pltpu.make_async_copy(message.at[amp_rows], held.at[i], sems.at[i, 1]))
    for load in info_loads + amp_loads:
        load.start()
    if first:
        source, tile, acc, term = rest
        parts = tile.shape[0] // 2
        for plane in range(2):
            for k in range(parts):
                block = source[plane, :, k * LANES : (k + 1) * LANES]
                tile[plane * parts + k] = block.astype(bf16).astype(f32)
        acc[...] = jnp.zeros(acc.shape, f32)
        term[...] = jnp.zeros(term.shape, f32)
    else:
        tile, acc_in, term_in, acc = rest[:4]
        term = rest[-1]
        parts = tile.shape[0] // 2
        acc[...] = acc_in[...]
        term[...] = term_in[...]
    for i in range(count):
        info_loads[i].wait()
        buffer_terms(
            held.at[i], amp_loads[i], infos[i], tile, probe, left, right, acc, term, capacity, size, parts
        )
    if last:
        keep, send = rest[4:6]
        half = size // 2
        odd = lax.rem(lax.axis_index("pos"), 2)
        keep[...] = term[:, pl.ds(pl.multiple_of(odd * half, half), half), :]
        send[...] = term[:, pl.ds(pl.multiple_of((1 - odd) * half, half), half), :]


def terms(probe, left, right, messages, capacity, source=None, state=None, last=False):
    size = probe.shape[1]
    count = len(messages)
    full = pl.BlockSpec(memory_space=pltpu.VMEM)
    far = pl.BlockSpec(memory_space=pltpu.HBM)
    scratch = [
        pltpu.VMEM((count, capacity * size, size), bf16),
        pltpu.VMEM((count, INFO_ROWS, size), bf16),
        pltpu.SemaphoreType.DMA((count, 2)),
    ]
    if state is None:
        _, rows, cols = source.shape
        blocks = jax.ShapeDtypeStruct((2 * cols // LANES, rows, LANES), f32)
        operands = (source,)
        shapes = [blocks, blocks, jax.ShapeDtypeStruct(probe.shape, f32)]
        aliases = {}
    else:
        operands = state
        tile, acc, term = state
        shapes = [jax.ShapeDtypeStruct(acc.shape, f32)]
        aliases = {4 + count: 0}
        if last:
            shapes += [jax.ShapeDtypeStruct((2, size // 2, size), f32)] * 2
            scratch = [pltpu.VMEM(term.shape, f32)] + scratch
        else:
            shapes += [jax.ShapeDtypeStruct(term.shape, f32)]
            aliases[5 + count] = 1
    results = pl.pallas_call(
        functools.partial(terms_kernel, count, capacity, state is None, last),
        in_specs=[full] * 3 + [far] * count + [full] * len(operands),
        out_specs=[full] * len(shapes),
        out_shape=shapes,
        scratch_shapes=scratch,
        input_output_aliases=aliases,
        compiler_params=pltpu.CompilerParams(vmem_limit_bytes=TERMS_VMEM),
        cost_estimate=pl.CostEstimate(
            flops=2 * size**3 * capacity * count, bytes_accessed=2**18, transcendentals=0
        ),
        name="terms",
    )(probe, left, right, *messages, *operands)
    return tuple(results) if state is None or last else (state[0], *results)


def finish_kernel(n_pos, n_obj, ring, steps, capacity, size, tile, acc, *rest):
    ends, rest = rest[: len(steps)], rest[len(steps) :]
    messages, (out, infos, chosen, sems) = rest[: len(ring)], rest[len(ring) :]
    loads = [
        pltpu.make_async_copy(message.at[pl.ds(capacity * size, INFO_ROWS)], infos.at[i], sems.at[i])
        for i, message in enumerate(messages)
    ]
    for load in loads:
        load.start()
    for load in loads:
        load.wait()
    _, rows, cols = tile.shape
    parts = cols // LANES
    each = rows // size
    me = lax.axis_index("pos")
    for side, neighbour in enumerate((lax.rem(me + n_pos - 1, n_pos), lax.rem(me + 1, n_pos))):
        block = jnp.zeros((INFO_ROWS, size), f32)
        for i, d in enumerate(ring):
            block = jnp.where(jnp.bitwise_xor(me, neighbour) == d, infos[i].astype(f32), block)
        chosen[side] = block

    def edge(side, plane):
        place = 1 + (2 * each if side == 0 else 0) + plane * each
        values = [chosen[side, place + i : place + i + 1, :] for i in range(each)]
        return jnp.concatenate([jnp.transpose(jnp.broadcast_to(v, (LANES, size))) for v in values], axis=0)

    level = lax.axis_index("obj")
    rim_at = ends[0].shape[1] - SUBLANES

    def end_row(side, plane, k):
        neighbour = lax.rem(level + (n_obj - 1 if side == 0 else 1), n_obj)
        place = rim_at + (rim_width(cols, size) if side == 0 else 0) + k * LANES // size
        lanes = slice(k * LANES % size, k * LANES % size + LANES)
        value = jnp.zeros((1, LANES), f32)
        for block, step in zip(ends, steps):
            value = jnp.where(jnp.bitwise_xor(level, neighbour) == step, block[plane, place : place + 1, lanes], value)
        return value

    lane = lax.broadcasted_iota(jnp.int32, (rows, LANES), 1)
    line = lax.broadcasted_iota(jnp.int32, (rows, LANES), 0)
    for plane in range(2):
        blocks = [tile[plane, :, k * LANES : (k + 1) * LANES] for k in range(parts)]
        to_right = [pltpu.roll(block, 1, 1) for block in blocks]
        to_left = [pltpu.roll(block, LANES - 1, 1) for block in blocks]
        low, high = edge(0, plane), edge(1, plane)
        for k in range(parts):
            here = slice(k * LANES, (k + 1) * LANES)
            block = blocks[k]
            near = jnp.where(lane == 0, to_right[k - 1] if k > 0 else low, to_right[k])
            near += jnp.where(lane == LANES - 1, to_left[k + 1] if k + 1 < parts else high, to_left[k])
            near += jnp.where(line == 0, end_row(0, plane, k), pltpu.roll(block, 1, 0))
            near += jnp.where(line == rows - 1, end_row(1, plane, k), pltpu.roll(block, rows - 1, 0))
            smooth = 4.0 * block - near
            out[plane, :, here] = block - 0.25 * (acc[plane * parts + k] + 0.5 * smooth)


def finish(tile, acc, steps, ends, ring, messages, n_pos, n_obj, capacity, size):
    full = pl.BlockSpec(memory_space=pltpu.VMEM)
    far = pl.BlockSpec(memory_space=pltpu.HBM)
    return pl.pallas_call(
        functools.partial(finish_kernel, n_pos, n_obj, ring, steps, capacity, size),
        in_specs=[full] * (2 + len(ends)) + [far] * len(ring),
        out_specs=full,
        out_shape=jax.ShapeDtypeStruct(tile.shape, f32),
        scratch_shapes=[
            pltpu.VMEM((len(ring), INFO_ROWS, size), bf16),
            pltpu.VMEM((2, INFO_ROWS, size), f32),
            pltpu.SemaphoreType.DMA((len(ring),)),
        ],
        compiler_params=pltpu.CompilerParams(vmem_limit_bytes=SMALL_VMEM),
        cost_estimate=pl.CostEstimate(flops=2**24, bytes_accessed=2**23, transcendentals=0),
        name="finish",
    )(tile, acc, *ends, *messages)


def small_call(body, name, operands, shapes):
    return pl.pallas_call(
        body,
        out_shape=shapes,
        compiler_params=pltpu.CompilerParams(vmem_limit_bytes=SMALL_VMEM),
        name=name,
    )(*operands)


def split_kernel(pairs, keep, got, *pieces):
    rows = pieces[0].shape[1]
    pair = lax.axis_index("pos") // 2
    for d in range(pairs):
        here = pl.ds(pl.multiple_of(jnp.bitwise_xor(pair, d) * rows, rows), rows)
        pieces[d][...] = keep[:, here, :] + got[:, here, :]


def join_kernel(pairs, scale, probe, *rest):
    pieces, out = rest[:pairs], rest[pairs]
    rows = pieces[0].shape[1]
    half = out.shape[1]
    me = lax.axis_index("pos")
    for d in range(pairs):
        start = jnp.bitwise_xor(me // 2, d) * rows
        old = probe[:, pl.ds(pl.multiple_of(lax.rem(me, 2) * half + start, rows), rows), :]
        out[:, pl.ds(pl.multiple_of(start, rows), rows), :] = old - pieces[d][...] * scale


def whole_kernel(mine, other, out):
    half = mine.shape[1]
    odd = lax.rem(lax.axis_index("pos"), 2)
    out[:, pl.ds(pl.multiple_of(odd * half, half), half), :] = mine[...]
    out[:, pl.ds(pl.multiple_of((1 - odd) * half, half), half), :] = other[...]


def step_probe(probe, keep, send, scale, rim, beside):
    n_pos = lax.axis_size("pos")
    n_obj = lax.axis_size("obj")
    pairs = n_pos // 2
    planes, half, size = keep.shape
    rows = half // pairs
    shape = jax.ShapeDtypeStruct((planes, rows, size), f32)
    got = exchange(send, "pos", 1)
    pieces = small_call(functools.partial(split_kernel, pairs), "split", (keep, got), [shape] * pairs)
    total = pieces[0]
    for d in range(1, pairs):
        total = total + exchange(pieces[d], "pos", 2 * d)
    steps, ends = [], []
    while 2 ** len(steps) < n_obj:
        step = 2 ** (len(steps) + 1) - 1
        got = exchange(jnp.concatenate([total, rim], axis=1), "obj", step)
        total = total + got[:, :rows]
        steps.append(step)
        ends.append(got)
    gathered = [total] + [exchange(total, "pos", 2 * d) for d in range(1, pairs)]
    gathered, result = lax.optimization_barrier((gathered, beside(steps, ends)))
    mine = small_call(
        functools.partial(join_kernel, pairs, scale),
        "join",
        (probe, *gathered),
        jax.ShapeDtypeStruct(keep.shape, f32),
    )
    other = exchange(mine, "pos", 1)
    new_probe = small_call(whole_kernel, "whole", (mine, other), jax.ShapeDtypeStruct(probe.shape, f32))
    return new_probe, result


def shards(object_field, probe, amplitude, row_offset, col_offset, owner):
    n_pos = lax.axis_size("pos")
    n_obj = lax.axis_size("obj")
    pos_dev, size, _ = amplitude.shape
    capacity = max(2, pos_dev // n_pos + 1)
    left, right = (jnp.asarray(table) for table in dft_blocks(size))
    if n_pos == 8:
        early, later = [1, 2, 4, 3, 5], {4: [6], 3: [7]}
        order = [0, 1, 2, 4, 3, 5, 6, 7]
    else:
        window = 4
        order = list(range(n_pos))
        early, later = order[1 : 1 + window], {d: [d + window] for d in order[1 : n_pos - window]}
    *packed, rim = pack(
        owner, row_offset, col_offset, amplitude, object_field, n_pos, capacity, order[1:] + order[:1]
    )
    received = {d: exchange(packed[d], "pos", d) for d in early}
    received[0] = packed[0]
    state = terms(probe, left, right, [received[0]], capacity, source=object_field)
    for d in order[1:-1]:
        state = terms(probe, left, right, [received[d]], capacity, state=state)
        for e in later.get(d, []):
            state, sending = lax.optimization_barrier((state, packed[e]))
            received[e] = exchange(sending, "pos", e)
    acc, keep, send = terms(probe, left, right, [received[order[-1]]], capacity, state=state, last=True)
    ring = sorted({i ^ ((i + 1) % n_pos) for i in range(n_pos)})
    near = [received[d] for d in ring]

    def object_step(steps, ends):
        return finish(object_field, acc, steps, ends, ring, near, n_pos, n_obj, capacity, size)

    scale = 1.0 / math.sqrt(pos_dev * n_pos * n_obj)
    new_probe, new_object = step_probe(probe, keep, send, scale, rim, object_step)
    return (new_object, new_probe)


def solution(mesh):
    placed = (
        P(None, "obj", "pos"),
        P(),
        P(("pos", "obj"), None, None),
        P(("pos", "obj")),
        P(("pos", "obj")),
        P(("pos", "obj")),
    )
    return jax.shard_map(
        shards, mesh=mesh, in_specs=placed, out_specs=(P(None, "obj", "pos"), P()), check_vma=False
    )
```

time: 507 us -> 80 us (0.16)
  the two profiles are of different devices: /device:TPU:12 before, /device:TPU:0 now
where the time goes in v2:
time: 80 us; the launch traced here: 79.8 us
  Pallas kernels  37.9 us (47%)
  starting transfers between devices  20.9 us (26%)
  waiting for transfers between devices  19 us (24%)
  local copies, waits for them, and re-layouts  1.03 us (1%)
  between operations  0.91 us (1%)
    pallas_call x8, Pallas kernels, terms(): pl.pallas_call(functools.partial(terms_kernel, count, capacity, state is...  30.3 us
    ppermute x17, starting transfers between devices, exchange(): return lax.ppermute(value, axis, [(i, i ^ distance) for i in range(count)])  20.9 us
    ppermute x17, waiting for transfers between devices, exchange(): return lax.ppermute(value, axis, [(i, i ^ distance) for i in range(count)])  19 us
    pallas_call x1, Pallas kernels, pack(): pl.pallas_call(functools.partial(pack_kernel, n_pos, capacity, order), in...  3.95 us
    pallas_call x1, Pallas kernels, finish(): pl.pallas_call(functools.partial(finish_kernel, n_pos, n_obj, ring, steps...  2.77 us
  transfers between devices with their start and end apart: 17, of which 9 were waited for; matrix products, arithmetic and copies ran while one was open for 0% of the time, Pallas kernels for 37%

profile of v2, /device:TPU:0, one launch (start us, length us, event | category | flops | bytes accessed | tf_op | source)
XLA Modules:
  0.0 79.8 jit_solution(13335632083683527884)
XLA Ops:
  0.6 0.0 copy-start.1
  0.6 0.0 copy-start.2
  0.7 0.0 copy-start.3
  0.7 0.0 copy-start
  0.7 4.0 %pack.1 = (bf16[784,256]{1,0:T(8,128)(2,1)}, bf16[784,256]{1,0:T(8,128)(2,1)}, bf16[784,256]{1,0:T(8,128)(2,1)}, bf16[784,256]{1,0:T(8,128)(2,1)}, bf16[784,256]...) custom-call(s32[16]{0:T(128)} %owner_in.1, ...), custom_call_target="tpu_custom_call" | custom-call | flops 1048576 | bytes 1048576 | tf_op jit(solution)/shard_map/pack/pallas_call | solution.py:136
  4.6 0.5 collective-permute-start.2
  5.2 2.6 %collective-permute-start.1 = (bf16[784,256]{1,0:T(8,128)(2,1)}, bf16[784,256]{1,0:T(8,128)(2,1)S(1)}, u32[]{:S(2)}, u32[]{:S(2)}) collective-permute-start(bf16[784,256]{1,0:T(8,128)(2,1)} %get-tuple-element.49), channel_id=1, source_target_pairs={{0,8},{4,12},{8,0},{12,4},{16,24},{20,28},{24,16},{28,20},{1,9},{5... | collective-permute-start | bytes 1204232 | tf_op jit(solution)/shard_map/ppermute | solution.py:36
  7.7 1.5 %collective-permute-start = (bf16[784,256]{1,0:T(8,128)(2,1)}, bf16[784,256]{1,0:T(8,128)(2,1)S(1)}, u32[]{:S(2)}, u32[]{:S(2)}) collective-permute-start(bf16[784,256]{1,0:T(8,128)(2,1)} %get-tuple-element.48), channel_id=1, source_target_pairs={{0,16},{4,20},{8,24},{12,28},{16,0},{20,4},{24,8},{28,12},{1,17},{... | collective-permute-start | bytes 1204232 | tf_op jit(solution)/shard_map/ppermute | solution.py:36
  9.2 0.0 collective-permute-start.3
  9.3 0.3 collective-permute-start.6
  9.6 0.0 copy-done.1
  9.6 0.0 copy-done.2
  9.6 0.0 copy-done.3
  9.6 0.0 copy-done
  9.6 0.0 copy-start.4
  9.6 1.0 %copy-done.4 = bf16[784,256]{1,0:T(8,128)(2,1)S(1)} copy-done((bf16[784,256]{1,0:T(8,128)(2,1)S(1)}, bf16[784,256]{1,0:T(8,128)(2,1)}, u32[]{:S(2)}) %copy-start.4) | copy-done | bytes 401432
  10.6 3.7 %terms.8 = (f32[6,512,128]{2,1,0:T(8,128)S(1)}, f32[6,512,128]{2,1,0:T(8,128)S(1)}, f32[2,256,256]{2,1,0:T(8,128)S(1)}) custom-call(f32[2,256,256]{2,1,0:T(8,128)S(1)} %copy-done, bf16[512,512]{1,0:T(8,128)(2,1)S(1)} %copy-done.2, bf16[512,512]{1,0:T(8,128)(2,1)S(1)} %copy-done.1, bf16[784,256]{1,0:T(8,128)(2,1)S(1)} %copy-done.4, f32[2,512,384]{2,1,0:T(8,128)S(1)} %copy-done.3), custom_call_target="tpu_custom_call" | custom-call | flops 100663296 | bytes 262144 | tf_op jit(solution)/shard_map/terms/pallas_call | solution.py:306
  14.3 0.0 collective-permute-done.2.rest_0_.rest_2_
  14.3 3.7 %terms.9 = (f32[6,512,128]{2,1,0:T(8,128)S(1)}, f32[2,256,256]{2,1,0:T(8,128)S(1)}) custom-call(f32[2,256,256]{2,1,0:T(8,128)S(1)} %copy-done, bf16[512,512]{1,0:T(8,128)(2,1)S(1)} %copy-done.2, bf16[512,512]{1,0:T(8,128)(2,1)S(1)} %copy-done.1, ...), custom_call_target="tpu_custom_call", output_to_operand_aliasing={{0}: (5, {}), {1}: (6, {})} | custom-call | flops 100663296 | bytes 262144 | tf_op jit(solution)/shard_map/terms/pallas_call | solution.py:306
  18.0 0.0 collective-permute-done.1.rest_0_
  18.1 3.7 %terms.10 = (f32[6,512,128]{2,1,0:T(8,128)S(1)}, f32[2,256,256]{2,1,0:T(8,128)S(1)}) custom-call(f32[2,256,256]{2,1,0:T(8,128)S(1)} %copy-done, bf16[512,512]{1,0:T(8,128)(2,1)S(1)} %copy-done.2, bf16[512,512]{1,0:T(8,128)(2,1)S(1)} %copy-done.1, bf16[784,256]{1,0:T(8,128)(2,1)S(1)} %collective-permute-done.1.rest_0_, ...), custom_call_target="tpu_custom_call", output_to_operand_aliasing={{0}: (5, {}), {1}: (6, {})} | custom-call | flops 100663296 | bytes 262144 | tf_op jit(solution)/shard_map/terms/pallas_call | solution.py:306
  21.8 0.0 collective-permute-done.rest_0_
  21.8 0.0 copy-start.7
  21.8 3.9 %terms.11 = (f32[6,512,128]{2,1,0:T(8,128)S(1)}, f32[2,256,256]{2,1,0:T(8,128)S(1)}) custom-call(f32[2,256,256]{2,1,0:T(8,128)S(1)} %copy-done, bf16[512,512]{1,0:T(8,128)(2,1)S(1)} %copy-done.2, bf16[512,512]{1,0:T(8,128)(2,1)S(1)} %copy-done.1, bf16[784,256]{1,0:T(8,128)(2,1)S(1)} %collective-permute-done.rest_0_, ...), custom_call_target="tpu_custom_call", output_to_operand_aliasing={{0}: (5, {}), {1}: (6, {})} | custom-call | flops 100663296 | bytes 262144 | tf_op jit(solution)/shard_map/terms/pallas_call | solution.py:306
  25.7 0.0 copy-done.7
  25.8 0.0 copy-start.6
  25.8 3.0 %collective-permute-start.5 = (bf16[784,256]{1,0:T(8,128)(2,1)S(1)}, bf16[784,256]{1,0:T(8,128)(2,1)S(1)}, u32[]{:S(2)}, u32[]{:S(2)}) collective-permute-start(bf16[784,256]{1,0:T(8,128)(2,1)S(1)} %copy-done.7), channel_id=1, source_target_pairs={{0,24},{4,28},{8,16},{12,20},{16,8},{20,12},{24,0},{28,4},{1,25},{... | collective-permute-start | bytes 1204232 | tf_op jit(solution)/shard_map/ppermute | solution.py:36
  28.7 0.0 collective-permute-done.3.rest_0_.rest_3_
  28.7 3.7 %terms.12 = (f32[6,512,128]{2,1,0:T(8,128)S(1)}, f32[2,256,256]{2,1,0:T(8,128)S(1)}) custom-call(f32[2,256,256]{2,1,0:T(8,128)S(1)} %copy-done, bf16[512,512]{1,0:T(8,128)(2,1)S(1)} %copy-done.2, bf16[512,512]{1,0:T(8,128)(2,1)S(1)} %copy-done.1, ...), custom_call_target="tpu_custom_call", output_to_operand_aliasing={{0}: (5, {}), {1}: (6, {})} | custom-call | flops 100663296 | bytes 262144 | tf_op jit(solution)/shard_map/terms/pallas_call | solution.py:306
  32.5 0.0 copy-done.6
  32.5 0.1 collective-permute-start.4
  32.6 0.0 collective-permute-done.6.rest_0_
  32.6 3.7 %terms.13 = (f32[6,512,128]{2,1,0:T(8,128)S(1)}, f32[2,256,256]{2,1,0:T(8,128)S(1)}) custom-call(f32[2,256,256]{2,1,0:T(8,128)S(1)} %copy-done, bf16[512,512]{1,0:T(8,128)(2,1)S(1)} %copy-done.2, bf16[512,512]{1,0:T(8,128)(2,1)S(1)} %copy-done.1, bf16[784,256]{1,0:T(8,128)(2,1)S(1)} %collective-permute-done.6.rest_0_, ...), custom_call_target="tpu_custom_call", output_to_operand_aliasing={{0}: (5, {}), {1}: (6, {})} | custom-call | flops 100663296 | bytes 262144 | tf_op jit(solution)/shard_map/terms/pallas_call | solution.py:306
  36.3 2.5 %collective-permute-done.5.rest_0_ = bf16[784,256]{1,0:T(8,128)(2,1)S(1)} collective-permute-done((bf16[784,256]{1,0:T(8,128)(2,1)S(1)}, bf16[784,256]{1,0:T(8,128)(2,1)S(1)}, u32[]{:S(2)}, u32[]{:S(2)}) %collective-permute-start.5) | collective-permute-done | bytes 401440 | tf_op jit(solution)/shard_map/ppermute | solution.py:36
  38.9 4.0 %terms.14 = (f32[6,512,128]{2,1,0:T(8,128)S(1)}, f32[2,256,256]{2,1,0:T(8,128)S(1)}) custom-call(f32[2,256,256]{2,1,0:T(8,128)S(1)} %copy-done, bf16[512,512]{1,0:T(8,128)(2,1)S(1)} %copy-done.2, bf16[512,512]{1,0:T(8,128)(2,1)S(1)} %copy-done.1, bf16[784,256]{1,0:T(8,128)(2,1)S(1)} %collective-permute-done.5.rest_0_, ...), custom_call_target="tpu_custom_call", output_to_operand_aliasing={{0}: (5, {}), {1}: (6, {})} | custom-call | flops 100663296 | bytes 262144 | tf_op jit(solution)/shard_map/terms/pallas_call | solution.py:306
  42.8 3.5 %collective-permute-done.4.rest_0_.rest_4_ = bf16[784,256]{1,0:T(8,128)(2,1)S(1)} collective-permute-done((bf16[784,256]{1,0:T(8,128)(2,1)S(1)}, bf16[784,256]{1,0:T(8,128)(2,1)S(1)}, u32[]{:S(2)}, u32[]{:S(2)}) %collective-permute-start.4) | collective-permute-done | bytes 401440 | tf_op jit(solution)/shard_map/ppermute | solution.py:36
  46.3 0.0 copy-start.5
  46.3 3.8 %terms.15 = (f32[6,512,128]{2,1,0:T(8,128)S(1)}, f32[2,128,256]{2,1,0:T(8,128)S(1)}, f32[2,128,256]{2,1,0:T(8,128)S(1)}) custom-call(f32[2,256,256]{2,1,0:T(8,128)S(1)} %copy-done, bf16[512,512]{1,0:T(8,128)(2,1)S(1)} %copy-done.2, bf16[512,512]{1,0:T(8,128)(2,1)S(1)} %copy-done.1, ...), custom_call_target="tpu_custom_call", output_to_operand_aliasing={{0}: (5, {})} | custom-call | flops 100663296 | bytes 262144 | tf_op jit(solution)/shard_map/terms/pallas_call | solution.py:306
  50.1 0.4 collective-permute-start.7
  50.6 1.2 %collective-permute-done.7.got = f32[2,128,256]{2,1,0:T(8,128)S(1)} collective-permute-done((f32[2,128,256]{2,1,0:T(8,128)S(1)}, f32[2,128,256]{2,1,0:T(8,128)S(1)}, u32[]{:S(2)}, u32[]{:S(2)}) %collective-permute-start.7) | collective-permute-done | bytes 262176 | tf_op jit(solution)/shard_map/ppermute | solution.py:36
  51.8 1.6 %collective-permute-start.8 = (f32[2,32,256]{2,1,0:T(8,128)S(1)}, f32[2,32,256]{2,1,0:T(8,128)S(1)}, u32[]{:S(2)}, u32[]{:S(2)}) collective-permute-start(f32[2,32,256]{2,1,0:T(8,128)S(1)} %get-tuple-element.80), channel_id=1, source_target_pairs={{0,8},{4,12},{8,0},{12,4},{16,24},{20,28},{24,16},{28,20},{1,9},{5... | collective-permute-start | bytes 196616 | tf_op jit(solution)/shard_map/ppermute | solution.py:36
  53.4 1.5 %collective-permute-start.9 = (f32[2,32,256]{2,1,0:T(8,128)S(1)}, f32[2,32,256]{2,1,0:T(8,128)S(1)}, u32[]{:S(2)}, u32[]{:S(2)}) collective-permute-start(f32[2,32,256]{2,1,0:T(8,128)S(1)} %get-tuple-element.81), channel_id=1, source_target_pairs={{0,16},{4,20},{8,24},{12,28},{16,0},{20,4},{24,8},{28,12},{1,17},{... | collective-permute-start | bytes 196616 | tf_op jit(solution)/shard_map/ppermute | solution.py:36
  54.8 0.5 collective-permute-start.10
  55.4 0.9 %collective-permute-done.8 = f32[2,32,256]{2,1,0:T(8,128)S(1)} collective-permute-done((f32[2,32,256]{2,1,0:T(8,128)S(1)}, f32[2,32,256]{2,1,0:T(8,128)S(1)}, u32[]{:S(2)}, u32[]{:S(2)}) %collective-permute-start.8) | collective-permute-done | bytes 65568 | tf_op jit(solution)/shard_map/ppermute | solution.py:36
  56.2 1.4 %collective-permute-done.9 = f32[2,32,256]{2,1,0:T(8,128)S(1)} collective-permute-done((f32[2,32,256]{2,1,0:T(8,128)S(1)}, f32[2,32,256]{2,1,0:T(8,128)S(1)}, u32[]{:S(2)}, u32[]{:S(2)}) %collective-permute-start.9) | collective-permute-done | bytes 65568 | tf_op jit(solution)/shard_map/ppermute | solution.py:36
  57.6 2.4 %collective-permute-done.10 = f32[2,32,256]{2,1,0:T(8,128)S(1)} collective-permute-done((f32[2,32,256]{2,1,0:T(8,128)S(1)}, f32[2,32,256]{2,1,0:T(8,128)S(1)}, u32[]{:S(2)}, u32[]{:S(2)}) %collective-permute-start.10) | collective-permute-done | bytes 65568 | tf_op jit(solution)/shard_map/ppermute | solution.py:36
  60.0 0.0 copy-done.5
  60.0 1.6 %collective-permute-start.11 = (f32[2,40,256]{2,1,0:T(8,128)S(1)}, f32[2,40,256]{2,1,0:T(8,128)S(1)}, u32[]{:S(2)}, u32[]{:S(2)}) collective-permute-start(f32[2,40,256]{2,1,0:T(8,128)S(1)} %pad_maximum_fusion.1), channel_id=1, source_target_pairs={{0,1},{1,0},{2,3},{3,2},{4,5},{5,4},{6,7},{7,6},{8,9},{9,8},{10,11... | collective-permute-start | bytes 245768 | tf_op jit(solution)/shard_map/ppermute | solution.py:36
  61.7 2.9 %collective-permute-done.11.rest_0_ = f32[2,40,256]{2,1,0:T(8,128)S(1)} collective-permute-done((f32[2,40,256]{2,1,0:T(8,128)S(1)}, f32[2,40,256]{2,1,0:T(8,128)S(1)}, u32[]{:S(2)}, u32[]{:S(2)}) %collective-permute-start.11) | collective-permute-done | bytes 81952 | tf_op jit(solution)/shard_map/ppermute | solution.py:36
  64.6 3.7 %collective-permute-start.12 = (f32[2,40,256]{2,1,0:T(8,128)S(1)}, f32[2,40,256]{2,1,0:T(8,128)S(1)}, u32[]{:S(2)}, u32[]{:S(2)}) collective-permute-start(f32[2,40,256]{2,1,0:T(8,128)S(1)} %pad_maximum_fusion), channel_id=1, source_target_pairs={{0,3},{1,2},{2,1},{3,0},{4,7},{5,6},{6,5},{7,4},{8,11},{9,10},{10,... | collective-permute-start | bytes 245768 | tf_op jit(solution)/shard_map/ppermute | solution.py:36
  68.3 2.7 %collective-permute-done.12.rest_1_ = f32[2,40,256]{2,1,0:T(8,128)S(1)} collective-permute-done((f32[2,40,256]{2,1,0:T(8,128)S(1)}, f32[2,40,256]{2,1,0:T(8,128)S(1)}, u32[]{:S(2)}, u32[]{:S(2)}) %collective-permute-start.12) | collective-permute-done | bytes 81952 | tf_op jit(solution)/shard_map/ppermute | solution.py:36
  71.0 0.6 collective-permute-start.15
  71.6 1.5 %collective-permute-start.14 = (f32[2,32,256]{2,1,0:T(8,128)S(1)}, f32[2,32,256]{2,1,0:T(8,128)S(1)}, u32[]{:S(2)}, u32[]{:S(2)}) collective-permute-start(f32[2,32,256]{2,1,0:T(8,128)S(1)} %slice_add_fusion.rest_0_), channel_id=1, source_target_pairs={{0,16},{4,20},{8,24},{12,28},{16,0},{20,4},{24,8},{28,12},{1,17},{... | collective-permute-start | bytes 196616 | tf_op jit(solution)/shard_map/ppermute | solution.py:36
  73.0 1.5 %collective-permute-start.13 = (f32[2,32,256]{2,1,0:T(8,128)S(1)}, f32[2,32,256]{2,1,0:T(8,128)S(1)}, u32[]{:S(2)}, u32[]{:S(2)}) collective-permute-start(f32[2,32,256]{2,1,0:T(8,128)S(1)} %slice_add_fusion.rest_0_), channel_id=1, source_target_pairs={{0,8},{4,12},{8,0},{12,4},{16,24},{20,28},{24,16},{28,20},{1,9},{5... | collective-permute-start | bytes 196616 | tf_op jit(solution)/shard_map/ppermute | solution.py:36
  74.5 2.8 %finish.1 = f32[2,512,384]{2,1,0:T(8,128)} custom-call(f32[2,512,384]{2,1,0:T(8,128)S(1)} %copy-done.3, f32[6,512,128]{2,1,0:T(8,128)S(1)} %get-tuple-element.84.acc, f32[2,40,256]{2,1,0:T(8,128)S(1)} %collective-permute-done.11.rest_0_, f32[2,40,256]{2,1,0:T(8,128)S(1)} %collective-permute-done.12.rest_1_, ...), custom_call_target="tpu_custom_call" | custom-call | flops 16777216 | bytes 8388608 | tf_op jit(solution)/shard_map/finish/pallas_call | solution.py:381
  77.3 0.0 collective-permute-done.15.rest_3_
  77.3 0.0 collective-permute-done.14.rest_2_
  77.3 0.0 collective-permute-done.13.rest_1_
  77.3 0.1 join.1.mine
  77.4 0.1 collective-permute-start.16
  77.5 1.5 %collective-permute-done.16.other = f32[2,128,256]{2,1,0:T(8,128)S(1)} collective-permute-done((f32[2,128,256]{2,1,0:T(8,128)S(1)}, f32[2,128,256]{2,1,0:T(8,128)S(1)}, u32[]{:S(2)}, u32[]{:S(2)}) %collective-permute-start.16) | collective-permute-done | bytes 262176 | tf_op jit(solution)/shard_map/ppermute | solution.py:36
  79.0 0.8 %whole.1 = f32[2,256,256]{2,1,0:T(8,128)} custom-call(f32[2,128,256]{2,1,0:T(8,128)S(1)} %join.1.mine, f32[2,128,256]{2,1,0:T(8,128)S(1)} %collective-permute-done.16.other), custom_call_target="tpu_custom_call" | custom-call | tf_op jit(solution)/shard_map/whole/pallas_call | solution.py:398
  (6 shorter events, 0.1 us)
Async XLA Ops:
  0.6 8.9 %copy-start.1 = (bf16[512,512]{1,0:T(8,128)(2,1)S(1)}, bf16[512,512]{1,0:T(8,128)(2,1)}, u32[]{:S(2)}) copy-start(bf16[512,512]{1,0:T(8,128)(2,1)} %constant.5.clone.right) | copy-start | bytes 1572868
  0.6 8.9 %copy-start.2 = (bf16[512,512]{1,0:T(8,128)(2,1)S(1)}, bf16[512,512]{1,0:T(8,128)(2,1)}, u32[]{:S(2)}) copy-start(bf16[512,512]{1,0:T(8,128)(2,1)} %constant.4.clone.left) | copy-start | bytes 1572868
  0.7 8.9 %copy-start.3 = (f32[2,512,384]{2,1,0:T(8,128)S(1)}, f32[2,512,384]{2,1,0:T(8,128)}, u32[]{:S(2)}) copy-start(f32[2,512,384]{2,1,0:T(8,128)} %tile.3) | copy-start | bytes 4718596
  0.7 8.9 %copy-start = (f32[2,256,256]{2,1,0:T(8,128)S(1)}, f32[2,256,256]{2,1,0:T(8,128)}, u32[]{:S(2)}) copy-start(f32[2,256,256]{2,1,0:T(8,128)} %probe.17) | copy-start | bytes 1572868
  4.6 9.7 %collective-permute-start.2 = (bf16[784,256]{1,0:T(8,128)(2,1)}, bf16[784,256]{1,0:T(8,128)(2,1)S(1)}, u32[]{:S(2)}, u32[]{:S(2)}) collective-permute-start(bf16[784,256]{1,0:T(8,128)(2,1)} %get-tuple-element.50), channel_id=1, source_target_pairs={{0,4},{4,0},{8,12},{12,8},{16,20},{20,16},{24,28},{28,24},{1,5},{5... | collective-permute-start | bytes 1204232 | tf_op jit(solution)/shard_map/ppermute | solution.py:36
  5.2 12.9 %collective-permute-start.1 = (bf16[784,256]{1,0:T(8,128)(2,1)}, bf16[784,256]{1,0:T(8,128)(2,1)S(1)}, u32[]{:S(2)}, u32[]{:S(2)}) collective-permute-start(bf16[784,256]{1,0:T(8,128)(2,1)} %get-tuple-element.49), channel_id=1, source_target_pairs={{0,8},{4,12},{8,0},{12,4},{16,24},{20,28},{24,16},{28,20},{1,9},{5... | collective-permute-start | bytes 1204232 | tf_op jit(solution)/shard_map/ppermute | solution.py:36
  7.7 14.1 %collective-permute-start = (bf16[784,256]{1,0:T(8,128)(2,1)}, bf16[784,256]{1,0:T(8,128)(2,1)S(1)}, u32[]{:S(2)}, u32[]{:S(2)}) collective-permute-start(bf16[784,256]{1,0:T(8,128)(2,1)} %get-tuple-element.48), channel_id=1, source_target_pairs={{0,16},{4,20},{8,24},{12,28},{16,0},{20,4},{24,8},{28,12},{1,17},{... | collective-permute-start | bytes 1204232 | tf_op jit(solution)/shard_map/ppermute | solution.py:36
  9.2 19.5 %collective-permute-start.3 = (bf16[784,256]{1,0:T(8,128)(2,1)}, bf16[784,256]{1,0:T(8,128)(2,1)S(1)}, u32[]{:S(2)}, u32[]{:S(2)}) collective-permute-start(bf16[784,256]{1,0:T(8,128)(2,1)} %get-tuple-element.61), channel_id=1, source_target_pairs={{0,12},{4,8},{8,4},{12,0},{16,28},{20,24},{24,20},{28,16},{1,13},{... | collective-permute-start | bytes 1204232 | tf_op jit(solution)/shard_map/ppermute | solution.py:36
  9.3 23.3 %collective-permute-start.6 = (bf16[784,256]{1,0:T(8,128)(2,1)}, bf16[784,256]{1,0:T(8,128)(2,1)S(1)}, u32[]{:S(2)}, u32[]{:S(2)}) collective-permute-start(bf16[784,256]{1,0:T(8,128)(2,1)} %get-tuple-element.70), channel_id=1, source_target_pairs={{0,20},{4,16},{8,28},{12,24},{16,4},{20,0},{24,12},{28,8},{1,21},{... | collective-permute-start | bytes 1204232 | tf_op jit(solution)/shard_map/ppermute | solution.py:36
  9.6 1.0 %copy-start.4 = (bf16[784,256]{1,0:T(8,128)(2,1)S(1)}, bf16[784,256]{1,0:T(8,128)(2,1)}, u32[]{:S(2)}) copy-start(bf16[784,256]{1,0:T(8,128)(2,1)} %get-tuple-element.46.rest_0_) | copy-start | bytes 1204228
  21.8 3.9 %copy-start.7 = (bf16[784,256]{1,0:T(8,128)(2,1)S(1)}, bf16[784,256]{1,0:T(8,128)(2,1)}, u32[]{:S(2)}) copy-start(bf16[784,256]{1,0:T(8,128)(2,1)} %get-tuple-element.69) | copy-start | bytes 1204228
  25.8 6.7 %copy-start.6 = (bf16[784,256]{1,0:T(8,128)(2,1)S(1)}, bf16[784,256]{1,0:T(8,128)(2,1)}, u32[]{:S(2)}) copy-start(bf16[784,256]{1,0:T(8,128)(2,1)} %get-tuple-element.67) | copy-start | bytes 1204228
  25.8 13.1 %collective-permute-start.5 = (bf16[784,256]{1,0:T(8,128)(2,1)S(1)}, bf16[784,256]{1,0:T(8,128)(2,1)S(1)}, u32[]{:S(2)}, u32[]{:S(2)}) collective-permute-start(bf16[784,256]{1,0:T(8,128)(2,1)S(1)} %copy-done.7), channel_id=1, source_target_pairs={{0,24},{4,28},{8,16},{12,20},{16,8},{20,12},{24,0},{28,4},{1,25},{... | collective-permute-start | bytes 1204232 | tf_op jit(solution)/shard_map/ppermute | solution.py:36
  32.5 13.9 %collective-permute-start.4 = (bf16[784,256]{1,0:T(8,128)(2,1)S(1)}, bf16[784,256]{1,0:T(8,128)(2,1)S(1)}, u32[]{:S(2)}, u32[]{:S(2)}) collective-permute-start(bf16[784,256]{1,0:T(8,128)(2,1)S(1)} %copy-done.6), channel_id=1, source_target_pairs={{0,28},{4,24},{8,20},{12,16},{16,12},{20,8},{24,4},{28,0},{1,29},{... | collective-permute-start | bytes 1204232 | tf_op jit(solution)/shard_map/ppermute | solution.py:36
  46.3 13.7 %copy-start.5 = (f32[2,8,256]{2,1,0:T(8,128)S(1)}, f32[2,8,256]{2,1,0:T(8,128)}, u32[]{:S(2)}) copy-start(f32[2,8,256]{2,1,0:T(8,128)} %get-tuple-element.83) | copy-start | bytes 49156
  50.1 1.6 %collective-permute-start.7 = (f32[2,128,256]{2,1,0:T(8,128)S(1)}, f32[2,128,256]{2,1,0:T(8,128)S(1)}, u32[]{:S(2)}, u32[]{:S(2)}) collective-permute-start(f32[2,128,256]{2,1,0:T(8,128)S(1)} %get-tuple-element.78), channel_id=1, source_target_pairs={{0,4},{4,0},{8,12},{12,8},{16,20},{20,16},{24,28},{28,24},{1,5},{5... | collective-permute-start | bytes 786440 | tf_op jit(solution)/shard_map/ppermute | solution.py:36
  51.8 4.4 %collective-permute-start.8 = (f32[2,32,256]{2,1,0:T(8,128)S(1)}, f32[2,32,256]{2,1,0:T(8,128)S(1)}, u32[]{:S(2)}, u32[]{:S(2)}) collective-permute-start(f32[2,32,256]{2,1,0:T(8,128)S(1)} %get-tuple-element.80), channel_id=1, source_target_pairs={{0,8},{4,12},{8,0},{12,4},{16,24},{20,28},{24,16},{28,20},{1,9},{5... | collective-permute-start | bytes 196616 | tf_op jit(solution)/shard_map/ppermute | solution.py:36
  53.4 4.3 %collective-permute-start.9 = (f32[2,32,256]{2,1,0:T(8,128)S(1)}, f32[2,32,256]{2,1,0:T(8,128)S(1)}, u32[]{:S(2)}, u32[]{:S(2)}) collective-permute-start(f32[2,32,256]{2,1,0:T(8,128)S(1)} %get-tuple-element.81), channel_id=1, source_target_pairs={{0,16},{4,20},{8,24},{12,28},{16,0},{20,4},{24,8},{28,12},{1,17},{... | collective-permute-start | bytes 196616 | tf_op jit(solution)/shard_map/ppermute | solution.py:36
  54.8 5.2 %collective-permute-start.10 = (f32[2,32,256]{2,1,0:T(8,128)S(1)}, f32[2,32,256]{2,1,0:T(8,128)S(1)}, u32[]{:S(2)}, u32[]{:S(2)}) collective-permute-start(f32[2,32,256]{2,1,0:T(8,128)S(1)} %get-tuple-element.82), channel_id=1, source_target_pairs={{0,24},{4,28},{8,16},{12,20},{16,8},{20,12},{24,0},{28,4},{1,25},{... | collective-permute-start | bytes 196616 | tf_op jit(solution)/shard_map/ppermute | solution.py:36
  60.0 4.5 %collective-permute-start.11 = (f32[2,40,256]{2,1,0:T(8,128)S(1)}, f32[2,40,256]{2,1,0:T(8,128)S(1)}, u32[]{:S(2)}, u32[]{:S(2)}) collective-permute-start(f32[2,40,256]{2,1,0:T(8,128)S(1)} %pad_maximum_fusion.1), channel_id=1, source_target_pairs={{0,1},{1,0},{2,3},{3,2},{4,5},{5,4},{6,7},{7,6},{8,9},{9,8},{10,11... | collective-permute-start | bytes 245768 | tf_op jit(solution)/shard_map/ppermute | solution.py:36
  64.6 6.4 %collective-permute-start.12 = (f32[2,40,256]{2,1,0:T(8,128)S(1)}, f32[2,40,256]{2,1,0:T(8,128)S(1)}, u32[]{:S(2)}, u32[]{:S(2)}) collective-permute-start(f32[2,40,256]{2,1,0:T(8,128)S(1)} %pad_maximum_fusion), channel_id=1, source_target_pairs={{0,3},{1,2},{2,1},{3,0},{4,7},{5,6},{6,5},{7,4},{8,11},{9,10},{10,... | collective-permute-start | bytes 245768 | tf_op jit(solution)/shard_map/ppermute | solution.py:36
  71.0 6.3 %collective-permute-start.15 = (f32[2,32,256]{2,1,0:T(8,128)S(1)}, f32[2,32,256]{2,1,0:T(8,128)S(1)}, u32[]{:S(2)}, u32[]{:S(2)}) collective-permute-start(f32[2,32,256]{2,1,0:T(8,128)S(1)} %slice_add_fusion.rest_0_), channel_id=1, source_target_pairs={{0,24},{4,28},{8,16},{12,20},{16,8},{20,12},{24,0},{28,4},{1,25},{... | collective-permute-start | bytes 196616 | tf_op jit(solution)/shard_map/ppermute | solution.py:36
  71.6 5.7 %collective-permute-start.14 = (f32[2,32,256]{2,1,0:T(8,128)S(1)}, f32[2,32,256]{2,1,0:T(8,128)S(1)}, u32[]{:S(2)}, u32[]{:S(2)}) collective-permute-start(f32[2,32,256]{2,1,0:T(8,128)S(1)} %slice_add_fusion.rest_0_), channel_id=1, source_target_pairs={{0,16},{4,20},{8,24},{12,28},{16,0},{20,4},{24,8},{28,12},{1,17},{... | collective-permute-start | bytes 196616 | tf_op jit(solution)/shard_map/ppermute | solution.py:36
  73.0 4.3 %collective-permute-start.13 = (f32[2,32,256]{2,1,0:T(8,128)S(1)}, f32[2,32,256]{2,1,0:T(8,128)S(1)}, u32[]{:S(2)}, u32[]{:S(2)}) collective-permute-start(f32[2,32,256]{2,1,0:T(8,128)S(1)} %slice_add_fusion.rest_0_), channel_id=1, source_target_pairs={{0,8},{4,12},{8,0},{12,4},{16,24},{20,28},{24,16},{28,20},{1,9},{5... | collective-permute-start | bytes 196616 | tf_op jit(solution)/shard_map/ppermute | solution.py:36
  77.4 1.6 %collective-permute-start.16 = (f32[2,128,256]{2,1,0:T(8,128)S(1)}, f32[2,128,256]{2,1,0:T(8,128)S(1)}, u32[]{:S(2)}, u32[]{:S(2)}) collective-permute-start(f32[2,128,256]{2,1,0:T(8,128)S(1)} %join.1.mine), channel_id=1, source_target_pairs={{0,4},{4,0},{8,12},{12,8},{16,20},{20,16},{24,28},{28,24},{1,5},{5... | collective-permute-start | bytes 786440 | tf_op jit(solution)/shard_map/ppermute | solution.py:36

commit v3 on v2

--- a/solution.py
+++ b/solution.py
@@ -443,10 +443,10 @@
         total = total + exchange(pieces[d], "pos", 2 * d)
     steps, ends = [], []
     while 2 ** len(steps) < n_obj:
-        step = 2 ** (len(steps) + 1) - 1
-        got = exchange(jnp.concatenate([total, rim], axis=1), "obj", step)
+        got = exchange(jnp.concatenate([total, rim], axis=1), "obj", 2 ** len(steps))
         total = total + got[:, :rows]
-        steps.append(step)
+        rim = got[:, rows:]
+        steps.append(2 ** (len(steps) + 1) - 1)
         ends.append(got)
     gathered = [total] + [exchange(total, "pos", 2 * d) for d in range(1, pairs)]
     gathered, result = lax.optimization_barrier((gathered, beside(steps, ends)))
@@ -469,19 +469,20 @@
     left, right = (jnp.asarray(table) for table in dft_blocks(size))
     if n_pos == 8:
         early, later = [1, 2, 4, 3, 5], {4: [6], 3: [7]}
-        order = [0, 1, 2, 4, 3, 5, 6, 7]
+        order = [1, 0, 2, 4, 3, 5, 6, 7]
     else:
         window = 4
-        order = list(range(n_pos))
-        early, later = order[1 : 1 + window], {d: [d + window] for d in order[1 : n_pos - window]}
+        order = [1, 0] + list(range(2, n_pos))
+        early, later = list(range(1, 1 + window)), {d: [d + window] for d in range(1, n_pos - window)}
     *packed, rim = pack(
-        owner, row_offset, col_offset, amplitude, object_field, n_pos, capacity, order[1:] + order[:1]
+        owner, row_offset, col_offset, amplitude, object_field, n_pos, capacity, early + [d for d in order if d not in early]
     )
     received = {d: exchange(packed[d], "pos", d) for d in early}
     received[0] = packed[0]
-    state = terms(probe, left, right, [received[0]], capacity, source=object_field)
-    for d in order[1:-1]:
-        state = terms(probe, left, right, [received[d]], capacity, state=state)
+    state = terms(probe, left, right, [received[order[0]]], capacity, source=object_field)
+    for d in order[:-1]:
+        if d != order[0]:
+            state = terms(probe, left, right, [received[d]], capacity, state=state)
         for e in later.get(d, []):
             state, sending = lax.optimization_barrier((state, packed[e]))
             received[e] = exchange(sending, "pos", e)

time: 80 us -> 78.3 us (0.979)
  local copies, waits for them, and re-layouts: 1.03 us -> 0.04 us
    unnamed x16, local copies, waits for them, and re-layouts: 1.03 us -> 0.04 us
  transfers between devices with their start and end apart: 17 -> 17, of which waited for: 9 -> 10; matrix products, arithmetic and copies ran while one was open for 0% -> 0% of each run, Pallas kernels for 37% -> 37%
where the time goes in v3:
time: 78.3 us; the launch traced here: 78.2 us
  Pallas kernels  38 us (49%)
  starting transfers between devices  20.2 us (26%)
  waiting for transfers between devices  19 us (24%)
  between operations  0.93 us (1%)
    pallas_call x8, Pallas kernels, terms(): pl.pallas_call(functools.partial(terms_kernel, count, capacity, state is...  30.3 us
    ppermute x17, starting transfers between devices, exchange(): return lax.ppermute(value, axis, [(i, i ^ distance) for i in range(count)])  20.2 us
    ppermute x17, waiting for transfers between devices, exchange(): return lax.ppermute(value, axis, [(i, i ^ distance) for i in range(count)])  19 us
    pallas_call x1, Pallas kernels, pack(): pl.pallas_call(functools.partial(pack_kernel, n_pos, capacity, order), in...  3.95 us
    pallas_call x1, Pallas kernels, finish(): pl.pallas_call(functools.partial(finish_kernel, n_pos, n_obj, ring, steps...  2.77 us
  transfers between devices with their start and end apart: 17, of which 10 were waited for; matrix products, arithmetic and copies ran while one was open for 0% of the time, Pallas kernels for 37%

profile of v3, /device:TPU:0, one launch (start us, length us, event | category | flops | bytes accessed | tf_op | source)
XLA Modules:
  0.0 78.2 jit_solution(12126602737053364437)
XLA Ops:
  0.6 0.0 copy-start.1
  0.6 0.0 copy-start.2
  0.7 0.0 copy-start.3
  0.7 0.0 copy-start
  0.7 4.0 %pack.1 = (bf16[784,256]{1,0:T(8,128)(2,1)}, bf16[784,256]{1,0:T(8,128)(2,1)}, bf16[784,256]{1,0:T(8,128)(2,1)}, bf16[784,256]{1,0:T(8,128)(2,1)}, bf16[784,256]...) custom-call(s32[16]{0:T(128)} %owner_in.1, ...), custom_call_target="tpu_custom_call" | custom-call | flops 1048576 | bytes 1048576 | tf_op jit(solution)/shard_map/pack/pallas_call | solution.py:136
  4.6 0.5 collective-permute-start
  5.2 2.6 %collective-permute-start.2 = (bf16[784,256]{1,0:T(8,128)(2,1)}, bf16[784,256]{1,0:T(8,128)(2,1)S(1)}, u32[]{:S(2)}, u32[]{:S(2)}) collective-permute-start(bf16[784,256]{1,0:T(8,128)(2,1)} %get-tuple-element.49), channel_id=1, source_target_pairs={{0,8},{4,12},{8,0},{12,4},{16,24},{20,28},{24,16},{28,20},{1,9},{5... | collective-permute-start | bytes 1204232 | tf_op jit(solution)/shard_map/ppermute | solution.py:36
  7.7 1.5 %collective-permute-start.1 = (bf16[784,256]{1,0:T(8,128)(2,1)}, bf16[784,256]{1,0:T(8,128)(2,1)S(1)}, u32[]{:S(2)}, u32[]{:S(2)}) collective-permute-start(bf16[784,256]{1,0:T(8,128)(2,1)} %get-tuple-element.48), channel_id=1, source_target_pairs={{0,16},{4,20},{8,24},{12,28},{16,0},{20,4},{24,8},{28,12},{1,17},{... | collective-permute-start | bytes 1204232 | tf_op jit(solution)/shard_map/ppermute | solution.py:36
  9.2 0.0 collective-permute-start.3
  9.3 0.0 copy-start.4
  9.3 0.3 collective-permute-start.6
  9.6 0.0 collective-permute-done.rest_0_.rest_2_
  9.6 0.0 copy-done.1
  9.6 0.0 copy-done.2
  9.6 0.0 copy-done.3
  9.6 0.0 copy-done
  9.6 3.7 %terms.8 = (f32[6,512,128]{2,1,0:T(8,128)S(1)}, f32[6,512,128]{2,1,0:T(8,128)S(1)}, f32[2,256,256]{2,1,0:T(8,128)S(1)}) custom-call(f32[2,256,256]{2,1,0:T(8,128)S(1)} %copy-done, bf16[512,512]{1,0:T(8,128)(2,1)S(1)} %copy-done.2, bf16[512,512]{1,0:T(8,128)(2,1)S(1)} %copy-done.1, bf16[784,256]{1,0:T(8,128)(2,1)S(1)} %collective-permute-done.rest_0_.rest_2_, ...), custom_call_target="tpu_custom_call" | custom-call | flops 100663296 | bytes 262144 | tf_op jit(solution)/shard_map/terms/pallas_call | solution.py:306
  13.3 0.0 copy-done.4
  13.3 3.8 %terms.9 = (f32[6,512,128]{2,1,0:T(8,128)S(1)}, f32[2,256,256]{2,1,0:T(8,128)S(1)}) custom-call(f32[2,256,256]{2,1,0:T(8,128)S(1)} %copy-done, bf16[512,512]{1,0:T(8,128)(2,1)S(1)} %copy-done.2, bf16[512,512]{1,0:T(8,128)(2,1)S(1)} %copy-done.1, bf16[784,256]{1,0:T(8,128)(2,1)S(1)} %copy-done.4, ...), custom_call_target="tpu_custom_call", output_to_operand_aliasing={{0}: (5, {}), {1}: (6, {})} | custom-call | flops 100663296 | bytes 262144 | tf_op jit(solution)/shard_map/terms/pallas_call | solution.py:306
  17.1 1.0 %collective-permute-done.2.rest_0_ = bf16[784,256]{1,0:T(8,128)(2,1)S(1)} collective-permute-done((bf16[784,256]{1,0:T(8,128)(2,1)}, bf16[784,256]{1,0:T(8,128)(2,1)S(1)}, u32[]{:S(2)}, u32[]{:S(2)}) %collective-permute-start.2) | collective-permute-done | bytes 401440 | tf_op jit(solution)/shard_map/ppermute | solution.py:36
  18.1 3.7 %terms.10 = (f32[6,512,128]{2,1,0:T(8,128)S(1)}, f32[2,256,256]{2,1,0:T(8,128)S(1)}) custom-call(f32[2,256,256]{2,1,0:T(8,128)S(1)} %copy-done, bf16[512,512]{1,0:T(8,128)(2,1)S(1)} %copy-done.2, bf16[512,512]{1,0:T(8,128)(2,1)S(1)} %copy-done.1, bf16[784,256]{1,0:T(8,128)(2,1)S(1)} %collective-permute-done.2.rest_0_, ...), custom_call_target="tpu_custom_call", output_to_operand_aliasing={{0}: (5, {}), {1}: (6, {})} | custom-call | flops 100663296 | bytes 262144 | tf_op jit(solution)/shard_map/terms/pallas_call | solution.py:306
  21.8 0.0 collective-permute-done.1.rest_0_
  21.8 0.0 copy-start.7
  21.8 3.9 %terms.11 = (f32[6,512,128]{2,1,0:T(8,128)S(1)}, f32[2,256,256]{2,1,0:T(8,128)S(1)}) custom-call(f32[2,256,256]{2,1,0:T(8,128)S(1)} %copy-done, bf16[512,512]{1,0:T(8,128)(2,1)S(1)} %copy-done.2, bf16[512,512]{1,0:T(8,128)(2,1)S(1)} %copy-done.1, bf16[784,256]{1,0:T(8,128)(2,1)S(1)} %collective-permute-done.1.rest_0_, ...), custom_call_target="tpu_custom_call", output_to_operand_aliasing={{0}: (5, {}), {1}: (6, {})} | custom-call | flops 100663296 | bytes 262144 | tf_op jit(solution)/shard_map/terms/pallas_call | solution.py:306
  25.8 0.0 copy-done.7
  25.8 0.0 copy-start.6
  25.8 3.0 %collective-permute-start.5 = (bf16[784,256]{1,0:T(8,128)(2,1)S(1)}, bf16[784,256]{1,0:T(8,128)(2,1)S(1)}, u32[]{:S(2)}, u32[]{:S(2)}) collective-permute-start(bf16[784,256]{1,0:T(8,128)(2,1)S(1)} %copy-done.7), channel_id=1, source_target_pairs={{0,24},{4,28},{8,16},{12,20},{16,8},{20,12},{24,0},{28,4},{1,25},{... | collective-permute-start | bytes 1204232 | tf_op jit(solution)/shard_map/ppermute | solution.py:36
  28.8 0.0 collective-permute-done.3.rest_0_.rest_3_
  28.8 3.7 %terms.12 = (f32[6,512,128]{2,1,0:T(8,128)S(1)}, f32[2,256,256]{2,1,0:T(8,128)S(1)}) custom-call(f32[2,256,256]{2,1,0:T(8,128)S(1)} %copy-done, bf16[512,512]{1,0:T(8,128)(2,1)S(1)} %copy-done.2, bf16[512,512]{1,0:T(8,128)(2,1)S(1)} %copy-done.1, ...), custom_call_target="tpu_custom_call", output_to_operand_aliasing={{0}: (5, {}), {1}: (6, {})} | custom-call | flops 100663296 | bytes 262144 | tf_op jit(solution)/shard_map/terms/pallas_call | solution.py:306
  32.5 0.0 copy-done.6
  32.5 0.1 collective-permute-start.4
  32.6 0.0 collective-permute-done.6.rest_0_
  32.6 3.7 %terms.13 = (f32[6,512,128]{2,1,0:T(8,128)S(1)}, f32[2,256,256]{2,1,0:T(8,128)S(1)}) custom-call(f32[2,256,256]{2,1,0:T(8,128)S(1)} %copy-done, bf16[512,512]{1,0:T(8,128)(2,1)S(1)} %copy-done.2, bf16[512,512]{1,0:T(8,128)(2,1)S(1)} %copy-done.1, bf16[784,256]{1,0:T(8,128)(2,1)S(1)} %collective-permute-done.6.rest_0_, ...), custom_call_target="tpu_custom_call", output_to_operand_aliasing={{0}: (5, {}), {1}: (6, {})} | custom-call | flops 100663296 | bytes 262144 | tf_op jit(solution)/shard_map/terms/pallas_call | solution.py:306
  36.3 2.2 %collective-permute-done.5.rest_0_ = bf16[784,256]{1,0:T(8,128)(2,1)S(1)} collective-permute-done((bf16[784,256]{1,0:T(8,128)(2,1)S(1)}, bf16[784,256]{1,0:T(8,128)(2,1)S(1)}, u32[]{:S(2)}, u32[]{:S(2)}) %collective-permute-start.5) | collective-permute-done | bytes 401440 | tf_op jit(solution)/shard_map/ppermute | solution.py:36
  38.5 4.0 %terms.14 = (f32[6,512,128]{2,1,0:T(8,128)S(1)}, f32[2,256,256]{2,1,0:T(8,128)S(1)}) custom-call(f32[2,256,256]{2,1,0:T(8,128)S(1)} %copy-done, bf16[512,512]{1,0:T(8,128)(2,1)S(1)} %copy-done.2, bf16[512,512]{1,0:T(8,128)(2,1)S(1)} %copy-done.1, bf16[784,256]{1,0:T(8,128)(2,1)S(1)} %collective-permute-done.5.rest_0_, ...), custom_call_target="tpu_custom_call", output_to_operand_aliasing={{0}: (5, {}), {1}: (6, {})} | custom-call | flops 100663296 | bytes 262144 | tf_op jit(solution)/shard_map/terms/pallas_call | solution.py:306
  42.5 2.7 %collective-permute-done.4.rest_0_.rest_4_ = bf16[784,256]{1,0:T(8,128)(2,1)S(1)} collective-permute-done((bf16[784,256]{1,0:T(8,128)(2,1)S(1)}, bf16[784,256]{1,0:T(8,128)(2,1)S(1)}, u32[]{:S(2)}, u32[]{:S(2)}) %collective-permute-start.4) | collective-permute-done | bytes 401440 | tf_op jit(solution)/shard_map/ppermute | solution.py:36
  45.3 0.0 copy-start.5
  45.3 3.8 %terms.15 = (f32[6,512,128]{2,1,0:T(8,128)S(1)}, f32[2,128,256]{2,1,0:T(8,128)S(1)}, f32[2,128,256]{2,1,0:T(8,128)S(1)}) custom-call(f32[2,256,256]{2,1,0:T(8,128)S(1)} %copy-done, bf16[512,512]{1,0:T(8,128)(2,1)S(1)} %copy-done.2, bf16[512,512]{1,0:T(8,128)(2,1)S(1)} %copy-done.1, ...), custom_call_target="tpu_custom_call", output_to_operand_aliasing={{0}: (5, {})} | custom-call | flops 100663296 | bytes 262144 | tf_op jit(solution)/shard_map/terms/pallas_call | solution.py:306
  49.1 0.8 collective-permute-start.7
  49.8 1.2 %collective-permute-done.7.got = f32[2,128,256]{2,1,0:T(8,128)S(1)} collective-permute-done((f32[2,128,256]{2,1,0:T(8,128)S(1)}, f32[2,128,256]{2,1,0:T(8,128)S(1)}, u32[]{:S(2)}, u32[]{:S(2)}) %collective-permute-start.7) | collective-permute-done | bytes 262176 | tf_op jit(solution)/shard_map/ppermute | solution.py:36
  51.0 1.6 %collective-permute-start.8 = (f32[2,32,256]{2,1,0:T(8,128)S(1)}, f32[2,32,256]{2,1,0:T(8,128)S(1)}, u32[]{:S(2)}, u32[]{:S(2)}) collective-permute-start(f32[2,32,256]{2,1,0:T(8,128)S(1)} %get-tuple-element.80), channel_id=1, source_target_pairs={{0,8},{4,12},{8,0},{12,4},{16,24},{20,28},{24,16},{28,20},{1,9},{5... | collective-permute-start | bytes 196616 | tf_op jit(solution)/shard_map/ppermute | solution.py:36
  52.6 1.5 %collective-permute-start.9 = (f32[2,32,256]{2,1,0:T(8,128)S(1)}, f32[2,32,256]{2,1,0:T(8,128)S(1)}, u32[]{:S(2)}, u32[]{:S(2)}) collective-permute-start(f32[2,32,256]{2,1,0:T(8,128)S(1)} %get-tuple-element.81), channel_id=1, source_target_pairs={{0,16},{4,20},{8,24},{12,28},{16,0},{20,4},{24,8},{28,12},{1,17},{... | collective-permute-start | bytes 196616 | tf_op jit(solution)/shard_map/ppermute | solution.py:36
  54.2 0.4 collective-permute-start.10
  54.6 0.9 %collective-permute-done.8 = f32[2,32,256]{2,1,0:T(8,128)S(1)} collective-permute-done((f32[2,32,256]{2,1,0:T(8,128)S(1)}, f32[2,32,256]{2,1,0:T(8,128)S(1)}, u32[]{:S(2)}, u32[]{:S(2)}) %collective-permute-start.8) | collective-permute-done | bytes 65568 | tf_op jit(solution)/shard_map/ppermute | solution.py:36
  55.5 1.4 %collective-permute-done.9 = f32[2,32,256]{2,1,0:T(8,128)S(1)} collective-permute-done((f32[2,32,256]{2,1,0:T(8,128)S(1)}, f32[2,32,256]{2,1,0:T(8,128)S(1)}, u32[]{:S(2)}, u32[]{:S(2)}) %collective-permute-start.9) | collective-permute-done | bytes 65568 | tf_op jit(solution)/shard_map/ppermute | solution.py:36
  56.9 2.4 %collective-permute-done.10 = f32[2,32,256]{2,1,0:T(8,128)S(1)} collective-permute-done((f32[2,32,256]{2,1,0:T(8,128)S(1)}, f32[2,32,256]{2,1,0:T(8,128)S(1)}, u32[]{:S(2)}, u32[]{:S(2)}) %collective-permute-start.10) | collective-permute-done | bytes 65568 | tf_op jit(solution)/shard_map/ppermute | solution.py:36
  59.3 0.0 copy-done.5
  59.4 1.6 %collective-permute-start.11 = (f32[2,40,256]{2,1,0:T(8,128)S(1)}, f32[2,40,256]{2,1,0:T(8,128)S(1)}, u32[]{:S(2)}, u32[]{:S(2)}) collective-permute-start(f32[2,40,256]{2,1,0:T(8,128)S(1)} %pad_maximum_fusion), channel_id=1, source_target_pairs={{0,1},{1,0},{2,3},{3,2},{4,5},{5,4},{6,7},{7,6},{8,9},{9,8},{10,11... | collective-permute-start | bytes 245768 | tf_op jit(solution)/shard_map/ppermute | solution.py:36
  61.0 2.9 %collective-permute-done.11.rest_0_ = f32[2,40,256]{2,1,0:T(8,128)S(1)} collective-permute-done((f32[2,40,256]{2,1,0:T(8,128)S(1)}, f32[2,40,256]{2,1,0:T(8,128)S(1)}, u32[]{:S(2)}, u32[]{:S(2)}) %collective-permute-start.11) | collective-permute-done | bytes 81952 | tf_op jit(solution)/shard_map/ppermute | solution.py:36
  63.9 2.7 %collective-permute-start.12 = (f32[2,40,256]{2,1,0:T(8,128)S(1)}, f32[2,40,256]{2,1,0:T(8,128)S(1)}, u32[]{:S(2)}, u32[]{:S(2)}) collective-permute-start(f32[2,40,256]{2,1,0:T(8,128)S(1)} %pad_maximum_fusion.1), channel_id=1, source_target_pairs={{0,2},{1,3},{2,0},{3,1},{4,6},{5,7},{6,4},{7,5},{8,10},{9,11},{10,... | collective-permute-start | bytes 245768 | tf_op jit(solution)/shard_map/ppermute | solution.py:36
  66.6 2.7 %collective-permute-done.12.rest_1_ = f32[2,40,256]{2,1,0:T(8,128)S(1)} collective-permute-done((f32[2,40,256]{2,1,0:T(8,128)S(1)}, f32[2,40,256]{2,1,0:T(8,128)S(1)}, u32[]{:S(2)}, u32[]{:S(2)}) %collective-permute-start.12) | collective-permute-done | bytes 81952 | tf_op jit(solution)/shard_map/ppermute | solution.py:36
  69.3 0.5 collective-permute-start.15
  69.9 1.5 %collective-permute-start.14 = (f32[2,32,256]{2,1,0:T(8,128)S(1)}, f32[2,32,256]{2,1,0:T(8,128)S(1)}, u32[]{:S(2)}, u32[]{:S(2)}) collective-permute-start(f32[2,32,256]{2,1,0:T(8,128)S(1)} %slice_add_fusion.rest_0_), channel_id=1, source_target_pairs={{0,16},{4,20},{8,24},{12,28},{16,0},{20,4},{24,8},{28,12},{1,17},{... | collective-permute-start | bytes 196616 | tf_op jit(solution)/shard_map/ppermute | solution.py:36
  71.4 1.5 %collective-permute-start.13 = (f32[2,32,256]{2,1,0:T(8,128)S(1)}, f32[2,32,256]{2,1,0:T(8,128)S(1)}, u32[]{:S(2)}, u32[]{:S(2)}) collective-permute-start(f32[2,32,256]{2,1,0:T(8,128)S(1)} %slice_add_fusion.rest_0_), channel_id=1, source_target_pairs={{0,8},{4,12},{8,0},{12,4},{16,24},{20,28},{24,16},{28,20},{1,9},{5... | collective-permute-start | bytes 196616 | tf_op jit(solution)/shard_map/ppermute | solution.py:36
  72.9 2.8 %finish.1 = f32[2,512,384]{2,1,0:T(8,128)} custom-call(f32[2,512,384]{2,1,0:T(8,128)S(1)} %copy-done.3, f32[6,512,128]{2,1,0:T(8,128)S(1)} %get-tuple-element.84.acc, f32[2,40,256]{2,1,0:T(8,128)S(1)} %collective-permute-done.11.rest_0_, f32[2,40,256]{2,1,0:T(8,128)S(1)} %collective-permute-done.12.rest_1_, ...), custom_call_target="tpu_custom_call" | custom-call | flops 16777216 | bytes 8388608 | tf_op jit(solution)/shard_map/finish/pallas_call | solution.py:381
  75.7 0.0 collective-permute-done.15.rest_3_
  75.7 0.0 collective-permute-done.14.rest_2_
  75.7 0.0 collective-permute-done.13.rest_1_
  75.7 0.1 join.1.mine
  75.8 0.1 collective-permute-start.16
  75.8 1.5 %collective-permute-done.16.other = f32[2,128,256]{2,1,0:T(8,128)S(1)} collective-permute-done((f32[2,128,256]{2,1,0:T(8,128)S(1)}, f32[2,128,256]{2,1,0:T(8,128)S(1)}, u32[]{:S(2)}, u32[]{:S(2)}) %collective-permute-start.16) | collective-permute-done | bytes 262176 | tf_op jit(solution)/shard_map/ppermute | solution.py:36
  77.4 0.8 %whole.1 = f32[2,256,256]{2,1,0:T(8,128)} custom-call(f32[2,128,256]{2,1,0:T(8,128)S(1)} %join.1.mine, f32[2,128,256]{2,1,0:T(8,128)S(1)} %collective-permute-done.16.other), custom_call_target="tpu_custom_call" | custom-call | tf_op jit(solution)/shard_map/whole/pallas_call | solution.py:398
  (7 shorter events, 0.1 us)
Async XLA Ops:
  0.6 8.9 %copy-start.1 = (bf16[512,512]{1,0:T(8,128)(2,1)S(1)}, bf16[512,512]{1,0:T(8,128)(2,1)}, u32[]{:S(2)}) copy-start(bf16[512,512]{1,0:T(8,128)(2,1)} %constant.5.clone.right) | copy-start | bytes 1572868
  0.6 8.9 %copy-start.2 = (bf16[512,512]{1,0:T(8,128)(2,1)S(1)}, bf16[512,512]{1,0:T(8,128)(2,1)}, u32[]{:S(2)}) copy-start(bf16[512,512]{1,0:T(8,128)(2,1)} %constant.4.clone.left) | copy-start | bytes 1572868
  0.7 8.9 %copy-start.3 = (f32[2,512,384]{2,1,0:T(8,128)S(1)}, f32[2,512,384]{2,1,0:T(8,128)}, u32[]{:S(2)}) copy-start(f32[2,512,384]{2,1,0:T(8,128)} %tile.3) | copy-start | bytes 4718596
  0.7 8.9 %copy-start = (f32[2,256,256]{2,1,0:T(8,128)S(1)}, f32[2,256,256]{2,1,0:T(8,128)}, u32[]{:S(2)}) copy-start(f32[2,256,256]{2,1,0:T(8,128)} %probe.17) | copy-start | bytes 1572868
  4.6 4.9 %collective-permute-start = (bf16[784,256]{1,0:T(8,128)(2,1)}, bf16[784,256]{1,0:T(8,128)(2,1)S(1)}, u32[]{:S(2)}, u32[]{:S(2)}) collective-permute-start(bf16[784,256]{1,0:T(8,128)(2,1)} %get-tuple-element.46), channel_id=1, source_target_pairs={{0,4},{4,0},{8,12},{12,8},{16,20},{20,16},{24,28},{28,24},{1,5},{5... | collective-permute-start | bytes 1204232 | tf_op jit(solution)/shard_map/ppermute | solution.py:36
  5.2 12.9 %collective-permute-start.2 = (bf16[784,256]{1,0:T(8,128)(2,1)}, bf16[784,256]{1,0:T(8,128)(2,1)S(1)}, u32[]{:S(2)}, u32[]{:S(2)}) collective-permute-start(bf16[784,256]{1,0:T(8,128)(2,1)} %get-tuple-element.49), channel_id=1, source_target_pairs={{0,8},{4,12},{8,0},{12,4},{16,24},{20,28},{24,16},{28,20},{1,9},{5... | collective-permute-start | bytes 1204232 | tf_op jit(solution)/shard_map/ppermute | solution.py:36
  7.7 14.1 %collective-permute-start.1 = (bf16[784,256]{1,0:T(8,128)(2,1)}, bf16[784,256]{1,0:T(8,128)(2,1)S(1)}, u32[]{:S(2)}, u32[]{:S(2)}) collective-permute-start(bf16[784,256]{1,0:T(8,128)(2,1)} %get-tuple-element.48), channel_id=1, source_target_pairs={{0,16},{4,20},{8,24},{12,28},{16,0},{20,4},{24,8},{28,12},{1,17},{... | collective-permute-start | bytes 1204232 | tf_op jit(solution)/shard_map/ppermute | solution.py:36
  9.2 19.5 %collective-permute-start.3 = (bf16[784,256]{1,0:T(8,128)(2,1)}, bf16[784,256]{1,0:T(8,128)(2,1)S(1)}, u32[]{:S(2)}, u32[]{:S(2)}) collective-permute-start(bf16[784,256]{1,0:T(8,128)(2,1)} %get-tuple-element.61), channel_id=1, source_target_pairs={{0,12},{4,8},{8,4},{12,0},{16,28},{20,24},{24,20},{28,16},{1,13},{... | collective-permute-start | bytes 1204232 | tf_op jit(solution)/shard_map/ppermute | solution.py:36
  9.3 4.0 %copy-start.4 = (bf16[784,256]{1,0:T(8,128)(2,1)S(1)}, bf16[784,256]{1,0:T(8,128)(2,1)}, u32[]{:S(2)}) copy-start(bf16[784,256]{1,0:T(8,128)(2,1)} %get-tuple-element.50.rest_0_) | copy-start | bytes 1204228
  9.3 23.3 %collective-permute-start.6 = (bf16[784,256]{1,0:T(8,128)(2,1)}, bf16[784,256]{1,0:T(8,128)(2,1)S(1)}, u32[]{:S(2)}, u32[]{:S(2)}) collective-permute-start(bf16[784,256]{1,0:T(8,128)(2,1)} %get-tuple-element.70), channel_id=1, source_target_pairs={{0,20},{4,16},{8,28},{12,24},{16,4},{20,0},{24,12},{28,8},{1,21},{... | collective-permute-start | bytes 1204232 | tf_op jit(solution)/shard_map/ppermute | solution.py:36
  21.8 3.9 %copy-start.7 = (bf16[784,256]{1,0:T(8,128)(2,1)S(1)}, bf16[784,256]{1,0:T(8,128)(2,1)}, u32[]{:S(2)}) copy-start(bf16[784,256]{1,0:T(8,128)(2,1)} %get-tuple-element.69) | copy-start | bytes 1204228
  25.8 6.7 %copy-start.6 = (bf16[784,256]{1,0:T(8,128)(2,1)S(1)}, bf16[784,256]{1,0:T(8,128)(2,1)}, u32[]{:S(2)}) copy-start(bf16[784,256]{1,0:T(8,128)(2,1)} %get-tuple-element.67) | copy-start | bytes 1204228
  25.8 12.8 %collective-permute-start.5 = (bf16[784,256]{1,0:T(8,128)(2,1)S(1)}, bf16[784,256]{1,0:T(8,128)(2,1)S(1)}, u32[]{:S(2)}, u32[]{:S(2)}) collective-permute-start(bf16[784,256]{1,0:T(8,128)(2,1)S(1)} %copy-done.7), channel_id=1, source_target_pairs={{0,24},{4,28},{8,16},{12,20},{16,8},{20,12},{24,0},{28,4},{1,25},{... | collective-permute-start | bytes 1204232 | tf_op jit(solution)/shard_map/ppermute | solution.py:36
  32.5 12.8 %collective-permute-start.4 = (bf16[784,256]{1,0:T(8,128)(2,1)S(1)}, bf16[784,256]{1,0:T(8,128)(2,1)S(1)}, u32[]{:S(2)}, u32[]{:S(2)}) collective-permute-start(bf16[784,256]{1,0:T(8,128)(2,1)S(1)} %copy-done.6), channel_id=1, source_target_pairs={{0,28},{4,24},{8,20},{12,16},{16,12},{20,8},{24,4},{28,0},{1,29},{... | collective-permute-start | bytes 1204232 | tf_op jit(solution)/shard_map/ppermute | solution.py:36
  45.3 14.1 %copy-start.5 = (f32[2,8,256]{2,1,0:T(8,128)S(1)}, f32[2,8,256]{2,1,0:T(8,128)}, u32[]{:S(2)}) copy-start(f32[2,8,256]{2,1,0:T(8,128)} %get-tuple-element.83) | copy-start | bytes 49156
  49.1 1.9 %collective-permute-start.7 = (f32[2,128,256]{2,1,0:T(8,128)S(1)}, f32[2,128,256]{2,1,0:T(8,128)S(1)}, u32[]{:S(2)}, u32[]{:S(2)}) collective-permute-start(f32[2,128,256]{2,1,0:T(8,128)S(1)} %get-tuple-element.78), channel_id=1, source_target_pairs={{0,4},{4,0},{8,12},{12,8},{16,20},{20,16},{24,28},{28,24},{1,5},{5... | collective-permute-start | bytes 786440 | tf_op jit(solution)/shard_map/ppermute | solution.py:36
  51.0 4.4 %collective-permute-start.8 = (f32[2,32,256]{2,1,0:T(8,128)S(1)}, f32[2,32,256]{2,1,0:T(8,128)S(1)}, u32[]{:S(2)}, u32[]{:S(2)}) collective-permute-start(f32[2,32,256]{2,1,0:T(8,128)S(1)} %get-tuple-element.80), channel_id=1, source_target_pairs={{0,8},{4,12},{8,0},{12,4},{16,24},{20,28},{24,16},{28,20},{1,9},{5... | collective-permute-start | bytes 196616 | tf_op jit(solution)/shard_map/ppermute | solution.py:36
  52.6 4.3 %collective-permute-start.9 = (f32[2,32,256]{2,1,0:T(8,128)S(1)}, f32[2,32,256]{2,1,0:T(8,128)S(1)}, u32[]{:S(2)}, u32[]{:S(2)}) collective-permute-start(f32[2,32,256]{2,1,0:T(8,128)S(1)} %get-tuple-element.81), channel_id=1, source_target_pairs={{0,16},{4,20},{8,24},{12,28},{16,0},{20,4},{24,8},{28,12},{1,17},{... | collective-permute-start | bytes 196616 | tf_op jit(solution)/shard_map/ppermute | solution.py:36
  54.2 5.2 %collective-permute-start.10 = (f32[2,32,256]{2,1,0:T(8,128)S(1)}, f32[2,32,256]{2,1,0:T(8,128)S(1)}, u32[]{:S(2)}, u32[]{:S(2)}) collective-permute-start(f32[2,32,256]{2,1,0:T(8,128)S(1)} %get-tuple-element.82), channel_id=1, source_target_pairs={{0,24},{4,28},{8,16},{12,20},{16,8},{20,12},{24,0},{28,4},{1,25},{... | collective-permute-start | bytes 196616 | tf_op jit(solution)/shard_map/ppermute | solution.py:36
  59.4 4.5 %collective-permute-start.11 = (f32[2,40,256]{2,1,0:T(8,128)S(1)}, f32[2,40,256]{2,1,0:T(8,128)S(1)}, u32[]{:S(2)}, u32[]{:S(2)}) collective-permute-start(f32[2,40,256]{2,1,0:T(8,128)S(1)} %pad_maximum_fusion), channel_id=1, source_target_pairs={{0,1},{1,0},{2,3},{3,2},{4,5},{5,4},{6,7},{7,6},{8,9},{9,8},{10,11... | collective-permute-start | bytes 245768 | tf_op jit(solution)/shard_map/ppermute | solution.py:36
  63.9 5.4 %collective-permute-start.12 = (f32[2,40,256]{2,1,0:T(8,128)S(1)}, f32[2,40,256]{2,1,0:T(8,128)S(1)}, u32[]{:S(2)}, u32[]{:S(2)}) collective-permute-start(f32[2,40,256]{2,1,0:T(8,128)S(1)} %pad_maximum_fusion.1), channel_id=1, source_target_pairs={{0,2},{1,3},{2,0},{3,1},{4,6},{5,7},{6,4},{7,5},{8,10},{9,11},{10,... | collective-permute-start | bytes 245768 | tf_op jit(solution)/shard_map/ppermute | solution.py:36
  69.3 6.3 %collective-permute-start.15 = (f32[2,32,256]{2,1,0:T(8,128)S(1)}, f32[2,32,256]{2,1,0:T(8,128)S(1)}, u32[]{:S(2)}, u32[]{:S(2)}) collective-permute-start(f32[2,32,256]{2,1,0:T(8,128)S(1)} %slice_add_fusion.rest_0_), channel_id=1, source_target_pairs={{0,24},{4,28},{8,16},{12,20},{16,8},{20,12},{24,0},{28,4},{1,25},{... | collective-permute-start | bytes 196616 | tf_op jit(solution)/shard_map/ppermute | solution.py:36
  69.9 5.8 %collective-permute-start.14 = (f32[2,32,256]{2,1,0:T(8,128)S(1)}, f32[2,32,256]{2,1,0:T(8,128)S(1)}, u32[]{:S(2)}, u32[]{:S(2)}) collective-permute-start(f32[2,32,256]{2,1,0:T(8,128)S(1)} %slice_add_fusion.rest_0_), channel_id=1, source_target_pairs={{0,16},{4,20},{8,24},{12,28},{16,0},{20,4},{24,8},{28,12},{1,17},{... | collective-permute-start | bytes 196616 | tf_op jit(solution)/shard_map/ppermute | solution.py:36
  71.4 4.3 %collective-permute-start.13 = (f32[2,32,256]{2,1,0:T(8,128)S(1)}, f32[2,32,256]{2,1,0:T(8,128)S(1)}, u32[]{:S(2)}, u32[]{:S(2)}) collective-permute-start(f32[2,32,256]{2,1,0:T(8,128)S(1)} %slice_add_fusion.rest_0_), channel_id=1, source_target_pairs={{0,8},{4,12},{8,0},{12,4},{16,24},{20,28},{24,16},{28,20},{1,9},{5... | collective-permute-start | bytes 196616 | tf_op jit(solution)/shard_map/ppermute | solution.py:36
  75.8 1.6 %collective-permute-start.16 = (f32[2,128,256]{2,1,0:T(8,128)S(1)}, f32[2,128,256]{2,1,0:T(8,128)S(1)}, u32[]{:S(2)}, u32[]{:S(2)}) collective-permute-start(f32[2,128,256]{2,1,0:T(8,128)S(1)} %join.1.mine), channel_id=1, source_target_pairs={{0,4},{4,0},{8,12},{12,8},{16,20},{20,16},{24,28},{28,24},{1,5},{5... | collective-permute-start | bytes 786440 | tf_op jit(solution)/shard_map/ppermute | solution.py:36

commit v4 on v3

--- a/solution.py
+++ b/solution.py
@@ -193,7 +193,7 @@
     return jnp.concatenate([stacked[:size], stacked[size:]], axis=1)
 
 
-def buffer_terms(amp, amp_load, info, tile, probe, left, right, acc, term, capacity, size, parts):
+def buffer_terms(amp, amp_load, info, tile, probe, left, right, emit, term, capacity, size, parts):
     numbers = read_info(info, 3 * capacity)
     slots = [tuple(numbers[3 * k : 3 * k + 3]) for k in range(capacity)]
     probe_re = probe[0]
@@ -220,14 +220,12 @@
     backs = [side_by_side(dot(right[...], diff).astype(bf16), size) for diff in diffs]
     chis = [dot(back, left[...]) for back in backs]
     sum_re = sum_im = 0.0
-    for (row, col, valid), (patch_re, patch_im), chi in zip(slots, patches, chis):
+    for slot, ((row, col, valid), (patch_re, patch_im), chi) in enumerate(zip(slots, patches, chis)):
         weight = valid.astype(f32)
         chi_re = chi[:, :size] * weight
         chi_im = chi[:, size:] * weight
-        grad_re = (probe_re * chi_re + probe_im * chi_im).astype(bf16).astype(f32)
-        grad_im = (probe_re * chi_im - probe_im * chi_re).astype(bf16).astype(f32)
-        add_window(acc, 0, row, col, grad_re, size, parts)
-        add_window(acc, 1, row, col, grad_im, size, parts)
+        emit(slot, 0, row, col, (probe_re * chi_re + probe_im * chi_im).astype(bf16))
+        emit(slot, 1, row, col, (probe_re * chi_im - probe_im * chi_re).astype(bf16))
         patch_re = patch_re.astype(f32)
         patch_im = patch_im.astype(f32)
         sum_re += patch_re * chi_re + patch_im * chi_im
@@ -257,19 +255,28 @@
                 tile[plane * parts + k] = block.astype(bf16).astype(f32)
         acc[...] = jnp.zeros(acc.shape, f32)
         term[...] = jnp.zeros(term.shape, f32)
+    elif last:
+        tile, term_in, grads, keep, send, term = rest
+        parts = tile.shape[0] // 2
+        term[...] = term_in[...]
     else:
-        tile, acc_in, term_in, acc = rest[:4]
-        term = rest[-1]
+        tile, acc_in, term_in, acc, term = rest
         parts = tile.shape[0] // 2
         acc[...] = acc_in[...]
         term[...] = term_in[...]
+
+    def emit(slot, plane, row, col, grad):
+        if last:
+            grads[slot, plane] = grad
+        else:
+            add_window(acc, plane, row, col, grad.astype(f32), size, parts)
+
     for i in range(count):
         info_loads[i].wait()
         buffer_terms(
-            held.at[i], amp_loads[i], infos[i], tile, probe, left, right, acc, term, capacity, size, parts
+            held.at[i], amp_loads[i], infos[i], tile, probe, left, right, emit, term, capacity, size, parts
         )
     if last:
-        keep, send = rest[4:6]
         half = size // 2
         odd = lax.rem(lax.axis_index("pos"), 2)
         keep[...] = term[:, pl.ds(pl.multiple_of(odd * half, half), half), :]
@@ -293,16 +300,17 @@
         shapes = [blocks, blocks, jax.ShapeDtypeStruct(probe.shape, f32)]
         aliases = {}
     else:
-        operands = state
         tile, acc, term = state
-        shapes = [jax.ShapeDtypeStruct(acc.shape, f32)]
-        aliases = {4 + count: 0}
         if last:
+            operands = (tile, term)
+            shapes = [jax.ShapeDtypeStruct((capacity, 2, size, size), bf16)]
             shapes += [jax.ShapeDtypeStruct((2, size // 2, size), f32)] * 2
             scratch = [pltpu.VMEM(term.shape, f32)] + scratch
+            aliases = {}
         else:
-            shapes += [jax.ShapeDtypeStruct(term.shape, f32)]
-            aliases[5 + count] = 1
+            operands = state
+            shapes = [jax.ShapeDtypeStruct(acc.shape, f32), jax.ShapeDtypeStruct(term.shape, f32)]
+            aliases = {4 + count: 0, 5 + count: 1}
     results = pl.pallas_call(
         functools.partial(terms_kernel, count, capacity, state is None, last),
         in_specs=[full] * 3 + [far] * count + [full] * len(operands),
@@ -317,6 +325,35 @@
         name="terms",
     )(probe, left, right, *messages, *operands)
     return tuple(results) if state is None or last else (state[0], *results)
+
+
+def add_kernel(capacity, message, grads, acc_in, acc, info, sem):
+    _, _, size, _ = grads.shape
+    parts = acc.shape[0] // 2
+    load = pltpu.make_async_copy(message.at[pl.ds(capacity * size, INFO_ROWS)], info, sem)
+    load.start()
+    acc[...] = acc_in[...]
+    load.wait()
+    numbers = read_info(info[...], 3 * capacity)
+    for slot in range(capacity):
+        for plane in range(2):
+            add_window(acc, plane, numbers[3 * slot], numbers[3 * slot + 1], grads[slot, plane].astype(f32), size, parts)
+
+
+def add_grads(message, grads, acc):
+    capacity, _, size, _ = grads.shape
+    full = pl.BlockSpec(memory_space=pltpu.VMEM)
+    return pl.pallas_call(
+        functools.partial(add_kernel, capacity),
+        in_specs=[pl.BlockSpec(memory_space=pltpu.HBM), full, full],
+        out_specs=full,
+        out_shape=jax.ShapeDtypeStruct(acc.shape, f32),
+        scratch_shapes=[pltpu.VMEM((INFO_ROWS, size), bf16), pltpu.SemaphoreType.DMA],
+        input_output_aliases={2: 0},
+        compiler_params=pltpu.CompilerParams(vmem_limit_bytes=SMALL_VMEM),
+        cost_estimate=pl.CostEstimate(flops=2**20, bytes_accessed=2**18, transcendentals=0),
+        name="add",
+    )(message, grads, acc)
 
 
 def finish_kernel(n_pos, n_obj, ring, steps, capacity, size, tile, acc, *rest):
@@ -429,7 +466,7 @@
     out[:, pl.ds(pl.multiple_of((1 - odd) * half, half), half), :] = other[...]
 
 
-def step_probe(probe, keep, send, scale, rim, beside):
+def step_probe(probe, keep, send, scale, rim, acc, beside):
     n_pos = lax.axis_size("pos")
     n_obj = lax.axis_size("obj")
     pairs = n_pos // 2
@@ -439,17 +476,19 @@
     got = exchange(send, "pos", 1)
     pieces = small_call(functools.partial(split_kernel, pairs), "split", (keep, got), [shape] * pairs)
     total = pieces[0]
-    for d in range(1, pairs):
+    for d in reversed(range(1, pairs)):
         total = total + exchange(pieces[d], "pos", 2 * d)
     steps, ends = [], []
     while 2 ** len(steps) < n_obj:
         got = exchange(jnp.concatenate([total, rim], axis=1), "obj", 2 ** len(steps))
+        if not steps:
+            got, acc = lax.optimization_barrier((got, acc))
         total = total + got[:, :rows]
         rim = got[:, rows:]
         steps.append(2 ** (len(steps) + 1) - 1)
         ends.append(got)
     gathered = [total] + [exchange(total, "pos", 2 * d) for d in range(1, pairs)]
-    gathered, result = lax.optimization_barrier((gathered, beside(steps, ends)))
+    gathered, result = lax.optimization_barrier((gathered, beside(acc, steps, ends)))
     mine = small_call(
         functools.partial(join_kernel, pairs, scale),
         "join",
@@ -486,15 +525,16 @@
         for e in later.get(d, []):
             state, sending = lax.optimization_barrier((state, packed[e]))
             received[e] = exchange(sending, "pos", e)
-    acc, keep, send = terms(probe, left, right, [received[order[-1]]], capacity, state=state, last=True)
+    grads, keep, send = terms(probe, left, right, [received[order[-1]]], capacity, state=state, last=True)
+    acc = add_grads(received[order[-1]], grads, state[1])
     ring = sorted({i ^ ((i + 1) % n_pos) for i in range(n_pos)})
     near = [received[d] for d in ring]
 
-    def object_step(steps, ends):
+    def object_step(acc, steps, ends):
         return finish(object_field, acc, steps, ends, ring, near, n_pos, n_obj, capacity, size)
 
     scale = 1.0 / math.sqrt(pos_dev * n_pos * n_obj)
-    new_probe, new_object = step_probe(probe, keep, send, scale, rim, object_step)
+    new_probe, new_object = step_probe(probe, keep, send, scale, rim, acc, object_step)
     return (new_object, new_probe)
 
 

time: 78.3 us -> 77.3 us (0.987)
  waiting for transfers between devices: 19 us -> 17.9 us
    ppermute x17, waiting for transfers between devices: 19 us -> 17.9 us  [exchange(): return lax.ppermute(value, axis, [(i, i ^ distance) for i in range(count)])]
  transfers between devices with their start and end apart: 17 -> 17, of which waited for: 10 -> 11; matrix products, arithmetic and copies ran while one was open for 0% -> 0% of each run, Pallas kernels for 37% -> 39%
where the time goes in v4:
time: 77.3 us; the launch traced here: 77.2 us
  Pallas kernels  38.1 us (49%)
  starting transfers between devices  20.2 us (26%)
  waiting for transfers between devices  17.9 us (23%)
  between operations  0.93 us (1%)
    pallas_call x8, Pallas kernels, terms(): pl.pallas_call(functools.partial(terms_kernel, count, capacity, state is...  29.7 us
    ppermute x17, starting transfers between devices, exchange(): return lax.ppermute(value, axis, [(i, i ^ distance) for i in range(count)])  20.2 us
    ppermute x17, waiting for transfers between devices, exchange(): return lax.ppermute(value, axis, [(i, i ^ distance) for i in range(count)])  17.9 us
    pallas_call x1, Pallas kernels, pack(): pl.pallas_call(functools.partial(pack_kernel, n_pos, capacity, order), in...  3.95 us
    pallas_call x1, Pallas kernels, finish(): pl.pallas_call(functools.partial(finish_kernel, n_pos, n_obj, ring, steps...  2.77 us
  transfers between devices with their start and end apart: 17, of which 11 were waited for; matrix products, arithmetic and copies ran while one was open for 0% of the time, Pallas kernels for 39%

profile of v4, /device:TPU:0, one launch (start us, length us, event | category | flops | bytes accessed | tf_op | source)
XLA Modules:
  0.0 77.2 jit_solution(5407166513392778785)
XLA Ops:
  0.6 0.0 copy-start.1
  0.6 0.0 copy-start.2
  0.7 0.0 copy-start.3
  0.7 0.0 copy-start
  0.7 4.0 %pack.1 = (bf16[784,256]{1,0:T(8,128)(2,1)}, bf16[784,256]{1,0:T(8,128)(2,1)}, bf16[784,256]{1,0:T(8,128)(2,1)}, bf16[784,256]{1,0:T(8,128)(2,1)}, bf16[784,256]...) custom-call(s32[16]{0:T(128)} %owner_in.1, ...), custom_call_target="tpu_custom_call" | custom-call | flops 1048576 | bytes 1048576 | tf_op jit(solution)/shard_map/pack/pallas_call | solution.py:136
  4.6 0.5 collective-permute-start
  5.2 2.6 %collective-permute-start.2 = (bf16[784,256]{1,0:T(8,128)(2,1)}, bf16[784,256]{1,0:T(8,128)(2,1)S(1)}, u32[]{:S(2)}, u32[]{:S(2)}) collective-permute-start(bf16[784,256]{1,0:T(8,128)(2,1)} %get-tuple-element.51), channel_id=1, source_target_pairs={{0,8},{4,12},{8,0},{12,4},{16,24},{20,28},{24,16},{28,20},{1,9},{5... | collective-permute-start | bytes 1204232 | tf_op jit(solution)/shard_map/ppermute | solution.py:36
  7.7 1.5 %collective-permute-start.1 = (bf16[784,256]{1,0:T(8,128)(2,1)}, bf16[784,256]{1,0:T(8,128)(2,1)S(1)}, u32[]{:S(2)}, u32[]{:S(2)}) collective-permute-start(bf16[784,256]{1,0:T(8,128)(2,1)} %get-tuple-element.50), channel_id=1, source_target_pairs={{0,16},{4,20},{8,24},{12,28},{16,0},{20,4},{24,8},{28,12},{1,17},{... | collective-permute-start | bytes 1204232 | tf_op jit(solution)/shard_map/ppermute | solution.py:36
  9.2 0.0 collective-permute-start.3
  9.3 0.0 copy-start.4
  9.3 0.3 collective-permute-start.6
  9.6 0.0 collective-permute-done.rest_0_.rest_2_
  9.6 0.0 copy-done.1
  9.6 0.0 copy-done.2
  9.6 0.0 copy-done.3
  9.6 0.0 copy-done
  9.6 3.7 %terms.8 = (f32[6,512,128]{2,1,0:T(8,128)S(1)}, f32[6,512,128]{2,1,0:T(8,128)S(1)}, f32[2,256,256]{2,1,0:T(8,128)S(1)}) custom-call(f32[2,256,256]{2,1,0:T(8,128)S(1)} %copy-done, bf16[512,512]{1,0:T(8,128)(2,1)S(1)} %copy-done.2, bf16[512,512]{1,0:T(8,128)(2,1)S(1)} %copy-done.1, bf16[784,256]{1,0:T(8,128)(2,1)S(1)} %collective-permute-done.rest_0_.rest_2_, ...), custom_call_target="tpu_custom_call" | custom-call | flops 100663296 | bytes 262144 | tf_op jit(solution)/shard_map/terms/pallas_call | solution.py:314
  13.3 0.0 copy-done.4
  13.3 3.7 %terms.9 = (f32[6,512,128]{2,1,0:T(8,128)S(1)}, f32[2,256,256]{2,1,0:T(8,128)S(1)}) custom-call(f32[2,256,256]{2,1,0:T(8,128)S(1)} %copy-done, bf16[512,512]{1,0:T(8,128)(2,1)S(1)} %copy-done.2, bf16[512,512]{1,0:T(8,128)(2,1)S(1)} %copy-done.1, bf16[784,256]{1,0:T(8,128)(2,1)S(1)} %copy-done.4, ...), custom_call_target="tpu_custom_call", output_to_operand_aliasing={{0}: (5, {}), {1}: (6, {})} | custom-call | flops 100663296 | bytes 262144 | tf_op jit(solution)/shard_map/terms/pallas_call | solution.py:314
  17.0 1.0 %collective-permute-done.2.rest_0_ = bf16[784,256]{1,0:T(8,128)(2,1)S(1)} collective-permute-done((bf16[784,256]{1,0:T(8,128)(2,1)}, bf16[784,256]{1,0:T(8,128)(2,1)S(1)}, u32[]{:S(2)}, u32[]{:S(2)}) %collective-permute-start.2) | collective-permute-done | bytes 401440 | tf_op jit(solution)/shard_map/ppermute | solution.py:36
  18.1 3.7 %terms.10 = (f32[6,512,128]{2,1,0:T(8,128)S(1)}, f32[2,256,256]{2,1,0:T(8,128)S(1)}) custom-call(f32[2,256,256]{2,1,0:T(8,128)S(1)} %copy-done, bf16[512,512]{1,0:T(8,128)(2,1)S(1)} %copy-done.2, bf16[512,512]{1,0:T(8,128)(2,1)S(1)} %copy-done.1, bf16[784,256]{1,0:T(8,128)(2,1)S(1)} %collective-permute-done.2.rest_0_, ...), custom_call_target="tpu_custom_call", output_to_operand_aliasing={{0}: (5, {}), {1}: (6, {})} | custom-call | flops 100663296 | bytes 262144 | tf_op jit(solution)/shard_map/terms/pallas_call | solution.py:314
  21.8 0.0 collective-permute-done.1.rest_0_
  21.8 0.0 copy-start.7
  21.8 3.9 %terms.11 = (f32[6,512,128]{2,1,0:T(8,128)S(1)}, f32[2,256,256]{2,1,0:T(8,128)S(1)}) custom-call(f32[2,256,256]{2,1,0:T(8,128)S(1)} %copy-done, bf16[512,512]{1,0:T(8,128)(2,1)S(1)} %copy-done.2, bf16[512,512]{1,0:T(8,128)(2,1)S(1)} %copy-done.1, bf16[784,256]{1,0:T(8,128)(2,1)S(1)} %collective-permute-done.1.rest_0_, ...), custom_call_target="tpu_custom_call", output_to_operand_aliasing={{0}: (5, {}), {1}: (6, {})} | custom-call | flops 100663296 | bytes 262144 | tf_op jit(solution)/shard_map/terms/pallas_call | solution.py:314
  25.7 0.0 copy-done.7
  25.7 0.0 copy-start.6
  25.7 3.0 %collective-permute-start.5 = (bf16[784,256]{1,0:T(8,128)(2,1)S(1)}, bf16[784,256]{1,0:T(8,128)(2,1)S(1)}, u32[]{:S(2)}, u32[]{:S(2)}) collective-permute-start(bf16[784,256]{1,0:T(8,128)(2,1)S(1)} %copy-done.7), channel_id=1, source_target_pairs={{0,24},{4,28},{8,16},{12,20},{16,8},{20,12},{24,0},{28,4},{1,25},{... | collective-permute-start | bytes 1204232 | tf_op jit(solution)/shard_map/ppermute | solution.py:36
  28.7 0.0 collective-permute-done.3.rest_0_.rest_3_
  28.7 3.7 %terms.12 = (f32[6,512,128]{2,1,0:T(8,128)S(1)}, f32[2,256,256]{2,1,0:T(8,128)S(1)}) custom-call(f32[2,256,256]{2,1,0:T(8,128)S(1)} %copy-done, bf16[512,512]{1,0:T(8,128)(2,1)S(1)} %copy-done.2, bf16[512,512]{1,0:T(8,128)(2,1)S(1)} %copy-done.1, ...), custom_call_target="tpu_custom_call", output_to_operand_aliasing={{0}: (5, {}), {1}: (6, {})} | custom-call | flops 100663296 | bytes 262144 | tf_op jit(solution)/shard_map/terms/pallas_call | solution.py:314
  32.4 0.0 copy-done.6
  32.4 0.1 collective-permute-start.4
  32.5 0.0 collective-permute-done.6.rest_0_
  32.5 3.7 %terms.13 = (f32[6,512,128]{2,1,0:T(8,128)S(1)}, f32[2,256,256]{2,1,0:T(8,128)S(1)}) custom-call(f32[2,256,256]{2,1,0:T(8,128)S(1)} %copy-done, bf16[512,512]{1,0:T(8,128)(2,1)S(1)} %copy-done.2, bf16[512,512]{1,0:T(8,128)(2,1)S(1)} %copy-done.1, bf16[784,256]{1,0:T(8,128)(2,1)S(1)} %collective-permute-done.6.rest_0_, ...), custom_call_target="tpu_custom_call", output_to_operand_aliasing={{0}: (5, {}), {1}: (6, {})} | custom-call | flops 100663296 | bytes 262144 | tf_op jit(solution)/shard_map/terms/pallas_call | solution.py:314
  36.2 2.3 %collective-permute-done.5.rest_0_ = bf16[784,256]{1,0:T(8,128)(2,1)S(1)} collective-permute-done((bf16[784,256]{1,0:T(8,128)(2,1)S(1)}, bf16[784,256]{1,0:T(8,128)(2,1)S(1)}, u32[]{:S(2)}, u32[]{:S(2)}) %collective-permute-start.5) | collective-permute-done | bytes 401440 | tf_op jit(solution)/shard_map/ppermute | solution.py:36
  38.5 3.9 %terms.14 = (f32[6,512,128]{2,1,0:T(8,128)S(1)}, f32[2,256,256]{2,1,0:T(8,128)S(1)}) custom-call(f32[2,256,256]{2,1,0:T(8,128)S(1)} %copy-done, bf16[512,512]{1,0:T(8,128)(2,1)S(1)} %copy-done.2, bf16[512,512]{1,0:T(8,128)(2,1)S(1)} %copy-done.1, bf16[784,256]{1,0:T(8,128)(2,1)S(1)} %collective-permute-done.5.rest_0_, ...), custom_call_target="tpu_custom_call", output_to_operand_aliasing={{0}: (5, {}), {1}: (6, {})} | custom-call | flops 100663296 | bytes 262144 | tf_op jit(solution)/shard_map/terms/pallas_call | solution.py:314
  42.5 2.7 %collective-permute-done.4.rest_0_.message.rest_4_ = bf16[784,256]{1,0:T(8,128)(2,1)S(1)} collective-permute-done((bf16[784,256]{1,0:T(8,128)(2,1)S(1)}, bf16[784,256]{1,0:T(8,128)(2,1)S(1)}, u32[]{:S(2)}, u32[]{:S(2)}) %collective-permute-start.4) | collective-permute-done | bytes 401440 | tf_op jit(solution)/shard_map/ppermute | solution.py:36
  45.2 0.0 copy-start.5
  45.2 3.3 %terms.15 = (bf16[3,2,256,256]{3,2,1,0:T(8,128)(2,1)S(1)}, f32[2,128,256]{2,1,0:T(8,128)S(1)}, f32[2,128,256]{2,1,0:T(8,128)S(1)}) custom-call(f32[2,256,256]{2,1,0:T(8,128)S(1)} %copy-done, bf16[512,512]{1,0:T(8,128)(2,1)S(1)} %copy-done.2, bf16[512,512]{1,0:T(8,128)(2,1)S(1)} %copy-done.1, ...), custom_call_target="tpu_custom_call" | custom-call | flops 100663296 | bytes 262144 | tf_op jit(solution)/shard_map/terms/pallas_call | solution.py:314
  48.6 0.8 collective-permute-start.7
  49.3 1.2 %collective-permute-done.7.got = f32[2,128,256]{2,1,0:T(8,128)S(1)} collective-permute-done((f32[2,128,256]{2,1,0:T(8,128)S(1)}, f32[2,128,256]{2,1,0:T(8,128)S(1)}, u32[]{:S(2)}, u32[]{:S(2)}) %collective-permute-start.7) | collective-permute-done | bytes 262176 | tf_op jit(solution)/shard_map/ppermute | solution.py:36
  50.5 2.6 %collective-permute-start.8 = (f32[2,32,256]{2,1,0:T(8,128)S(1)}, f32[2,32,256]{2,1,0:T(8,128)S(1)}, u32[]{:S(2)}, u32[]{:S(2)}) collective-permute-start(f32[2,32,256]{2,1,0:T(8,128)S(1)} %get-tuple-element.81), channel_id=1, source_target_pairs={{0,24},{4,28},{8,16},{12,20},{16,8},{20,12},{24,0},{28,4},{1,25},{... | collective-permute-start | bytes 196616 | tf_op jit(solution)/shard_map/ppermute | solution.py:36
  53.1 0.5 collective-permute-start.9
  53.6 0.5 collective-permute-start.10
  54.1 1.8 %collective-permute-done.8 = f32[2,32,256]{2,1,0:T(8,128)S(1)} collective-permute-done((f32[2,32,256]{2,1,0:T(8,128)S(1)}, f32[2,32,256]{2,1,0:T(8,128)S(1)}, u32[]{:S(2)}, u32[]{:S(2)}) %collective-permute-start.8) | collective-permute-done | bytes 65568 | tf_op jit(solution)/shard_map/ppermute | solution.py:36
  55.9 1.5 %collective-permute-done.9 = f32[2,32,256]{2,1,0:T(8,128)S(1)} collective-permute-done((f32[2,32,256]{2,1,0:T(8,128)S(1)}, f32[2,32,256]{2,1,0:T(8,128)S(1)}, u32[]{:S(2)}, u32[]{:S(2)}) %collective-permute-start.9) | collective-permute-done | bytes 65568 | tf_op jit(solution)/shard_map/ppermute | solution.py:36
  57.4 0.5 collective-permute-done.10
  57.9 0.0 copy-done.5
  57.9 1.7 %collective-permute-start.11 = (f32[2,40,256]{2,1,0:T(8,128)S(1)}, f32[2,40,256]{2,1,0:T(8,128)S(1)}, u32[]{:S(2)}, u32[]{:S(2)}) collective-permute-start(f32[2,40,256]{2,1,0:T(8,128)S(1)} %pad_maximum_fusion), channel_id=1, source_target_pairs={{0,1},{1,0},{2,3},{3,2},{4,5},{5,4},{6,7},{7,6},{8,9},{9,8},{10,11... | collective-permute-start | bytes 245768 | tf_op jit(solution)/shard_map/ppermute | solution.py:36
  59.6 0.7 add.26.acc
  60.3 2.1 %collective-permute-done.11.rest_0_ = f32[2,40,256]{2,1,0:T(8,128)S(1)} collective-permute-done((f32[2,40,256]{2,1,0:T(8,128)S(1)}, f32[2,40,256]{2,1,0:T(8,128)S(1)}, u32[]{:S(2)}, u32[]{:S(2)}) %collective-permute-start.11) | collective-permute-done | bytes 81952 | tf_op jit(solution)/shard_map/ppermute | solution.py:36
  62.5 2.7 %collective-permute-start.12 = (f32[2,40,256]{2,1,0:T(8,128)S(1)}, f32[2,40,256]{2,1,0:T(8,128)S(1)}, u32[]{:S(2)}, u32[]{:S(2)}) collective-permute-start(f32[2,40,256]{2,1,0:T(8,128)S(1)} %pad_maximum_fusion.1), channel_id=1, source_target_pairs={{0,2},{1,3},{2,0},{3,1},{4,6},{5,7},{6,4},{7,5},{8,10},{9,11},{10,... | collective-permute-start | bytes 245768 | tf_op jit(solution)/shard_map/ppermute | solution.py:36
  65.1 2.7 %collective-permute-done.12.rest_1_ = f32[2,40,256]{2,1,0:T(8,128)S(1)} collective-permute-done((f32[2,40,256]{2,1,0:T(8,128)S(1)}, f32[2,40,256]{2,1,0:T(8,128)S(1)}, u32[]{:S(2)}, u32[]{:S(2)}) %collective-permute-start.12) | collective-permute-done | bytes 81952 | tf_op jit(solution)/shard_map/ppermute | solution.py:36
  67.9 1.5 %collective-permute-start.15 = (f32[2,32,256]{2,1,0:T(8,128)S(1)}, f32[2,32,256]{2,1,0:T(8,128)S(1)}, u32[]{:S(2)}, u32[]{:S(2)}) collective-permute-start(f32[2,32,256]{2,1,0:T(8,128)S(1)} %slice_add_fusion.rest_0_), channel_id=1, source_target_pairs={{0,24},{4,28},{8,16},{12,20},{16,8},{20,12},{24,0},{28,4},{1,25},{... | collective-permute-start | bytes 196616 | tf_op jit(solution)/shard_map/ppermute | solution.py:36
  69.4 1.0 %collective-permute-start.14 = (f32[2,32,256]{2,1,0:T(8,128)S(1)}, f32[2,32,256]{2,1,0:T(8,128)S(1)}, u32[]{:S(2)}, u32[]{:S(2)}) collective-permute-start(f32[2,32,256]{2,1,0:T(8,128)S(1)} %slice_add_fusion.rest_0_), channel_id=1, source_target_pairs={{0,16},{4,20},{8,24},{12,28},{16,0},{20,4},{24,8},{28,12},{1,17},{... | collective-permute-start | bytes 196616 | tf_op jit(solution)/shard_map/ppermute | solution.py:36
  70.4 1.0 %collective-permute-start.13 = (f32[2,32,256]{2,1,0:T(8,128)S(1)}, f32[2,32,256]{2,1,0:T(8,128)S(1)}, u32[]{:S(2)}, u32[]{:S(2)}) collective-permute-start(f32[2,32,256]{2,1,0:T(8,128)S(1)} %slice_add_fusion.rest_0_), channel_id=1, source_target_pairs={{0,8},{4,12},{8,0},{12,4},{16,24},{20,28},{24,16},{28,20},{1,9},{5... | collective-permute-start | bytes 196616 | tf_op jit(solution)/shard_map/ppermute | solution.py:36
  71.5 2.8 %finish.1 = f32[2,512,384]{2,1,0:T(8,128)} custom-call(f32[2,512,384]{2,1,0:T(8,128)S(1)} %copy-done.3, f32[6,512,128]{2,1,0:T(8,128)S(1)} %add.26.acc, f32[2,40,256]{2,1,0:T(8,128)S(1)} %collective-permute-done.11.rest_0_, f32[2,40,256]{2,1,0:T(8,128)S(1)} %collective-permute-done.12.rest_1_, bf16[784,256]{1,0:T(8,128)(2,1)S(1)} %collective-permute-done.rest_0_.rest_2_, ...), custom_call_target="tpu_custom_call" | custom-call | flops 16777216 | bytes 8388608 | tf_op jit(solution)/shard_map/finish/pallas_call | solution.py:418
  74.2 0.0 collective-permute-done.15.rest_3_
  74.2 0.0 collective-permute-done.14.rest_2_
  74.2 0.4 collective-permute-done.13.rest_1_
  74.7 0.1 collective-permute-start.16
  74.8 1.5 %collective-permute-done.16.other = f32[2,128,256]{2,1,0:T(8,128)S(1)} collective-permute-done((f32[2,128,256]{2,1,0:T(8,128)S(1)}, f32[2,128,256]{2,1,0:T(8,128)S(1)}, u32[]{:S(2)}, u32[]{:S(2)}) %collective-permute-start.16) | collective-permute-done | bytes 262176 | tf_op jit(solution)/shard_map/ppermute | solution.py:36
  76.3 0.8 %whole.1 = f32[2,256,256]{2,1,0:T(8,128)} custom-call(f32[2,128,256]{2,1,0:T(8,128)S(1)} %join.1.mine, f32[2,128,256]{2,1,0:T(8,128)S(1)} %collective-permute-done.16.other), custom_call_target="tpu_custom_call" | custom-call | tf_op jit(solution)/shard_map/whole/pallas_call | solution.py:435
  (8 shorter events, 0.1 us)
Async XLA Ops:
  0.6 8.9 %copy-start.1 = (bf16[512,512]{1,0:T(8,128)(2,1)S(1)}, bf16[512,512]{1,0:T(8,128)(2,1)}, u32[]{:S(2)}) copy-start(bf16[512,512]{1,0:T(8,128)(2,1)} %constant.5.clone.right) | copy-start | bytes 1572868
  0.6 8.9 %copy-start.2 = (bf16[512,512]{1,0:T(8,128)(2,1)S(1)}, bf16[512,512]{1,0:T(8,128)(2,1)}, u32[]{:S(2)}) copy-start(bf16[512,512]{1,0:T(8,128)(2,1)} %constant.4.clone.left) | copy-start | bytes 1572868
  0.7 8.9 %copy-start.3 = (f32[2,512,384]{2,1,0:T(8,128)S(1)}, f32[2,512,384]{2,1,0:T(8,128)}, u32[]{:S(2)}) copy-start(f32[2,512,384]{2,1,0:T(8,128)} %tile.3) | copy-start | bytes 4718596
  0.7 8.9 %copy-start = (f32[2,256,256]{2,1,0:T(8,128)S(1)}, f32[2,256,256]{2,1,0:T(8,128)}, u32[]{:S(2)}) copy-start(f32[2,256,256]{2,1,0:T(8,128)} %probe.17) | copy-start | bytes 1572868
  4.6 4.9 %collective-permute-start = (bf16[784,256]{1,0:T(8,128)(2,1)}, bf16[784,256]{1,0:T(8,128)(2,1)S(1)}, u32[]{:S(2)}, u32[]{:S(2)}) collective-permute-start(bf16[784,256]{1,0:T(8,128)(2,1)} %get-tuple-element.48), channel_id=1, source_target_pairs={{0,4},{4,0},{8,12},{12,8},{16,20},{20,16},{24,28},{28,24},{1,5},{5... | collective-permute-start | bytes 1204232 | tf_op jit(solution)/shard_map/ppermute | solution.py:36
  5.2 12.9 %collective-permute-start.2 = (bf16[784,256]{1,0:T(8,128)(2,1)}, bf16[784,256]{1,0:T(8,128)(2,1)S(1)}, u32[]{:S(2)}, u32[]{:S(2)}) collective-permute-start(bf16[784,256]{1,0:T(8,128)(2,1)} %get-tuple-element.51), channel_id=1, source_target_pairs={{0,8},{4,12},{8,0},{12,4},{16,24},{20,28},{24,16},{28,20},{1,9},{5... | collective-permute-start | bytes 1204232 | tf_op jit(solution)/shard_map/ppermute | solution.py:36
  7.7 14.1 %collective-permute-start.1 = (bf16[784,256]{1,0:T(8,128)(2,1)}, bf16[784,256]{1,0:T(8,128)(2,1)S(1)}, u32[]{:S(2)}, u32[]{:S(2)}) collective-permute-start(bf16[784,256]{1,0:T(8,128)(2,1)} %get-tuple-element.50), channel_id=1, source_target_pairs={{0,16},{4,20},{8,24},{12,28},{16,0},{20,4},{24,8},{28,12},{1,17},{... | collective-permute-start | bytes 1204232 | tf_op jit(solution)/shard_map/ppermute | solution.py:36
  9.2 19.5 %collective-permute-start.3 = (bf16[784,256]{1,0:T(8,128)(2,1)}, bf16[784,256]{1,0:T(8,128)(2,1)S(1)}, u32[]{:S(2)}, u32[]{:S(2)}) collective-permute-start(bf16[784,256]{1,0:T(8,128)(2,1)} %get-tuple-element.63), channel_id=1, source_target_pairs={{0,12},{4,8},{8,4},{12,0},{16,28},{20,24},{24,20},{28,16},{1,13},{... | collective-permute-start | bytes 1204232 | tf_op jit(solution)/shard_map/ppermute | solution.py:36
  9.3 4.0 %copy-start.4 = (bf16[784,256]{1,0:T(8,128)(2,1)S(1)}, bf16[784,256]{1,0:T(8,128)(2,1)}, u32[]{:S(2)}) copy-start(bf16[784,256]{1,0:T(8,128)(2,1)} %get-tuple-element.52.rest_0_) | copy-start | bytes 1204228
  9.3 23.2 %collective-permute-start.6 = (bf16[784,256]{1,0:T(8,128)(2,1)}, bf16[784,256]{1,0:T(8,128)(2,1)S(1)}, u32[]{:S(2)}, u32[]{:S(2)}) collective-permute-start(bf16[784,256]{1,0:T(8,128)(2,1)} %get-tuple-element.72), channel_id=1, source_target_pairs={{0,20},{4,16},{8,28},{12,24},{16,4},{20,0},{24,12},{28,8},{1,21},{... | collective-permute-start | bytes 1204232 | tf_op jit(solution)/shard_map/ppermute | solution.py:36
  21.8 3.9 %copy-start.7 = (bf16[784,256]{1,0:T(8,128)(2,1)S(1)}, bf16[784,256]{1,0:T(8,128)(2,1)}, u32[]{:S(2)}) copy-start(bf16[784,256]{1,0:T(8,128)(2,1)} %get-tuple-element.71) | copy-start | bytes 1204228
  25.7 6.7 %copy-start.6 = (bf16[784,256]{1,0:T(8,128)(2,1)S(1)}, bf16[784,256]{1,0:T(8,128)(2,1)}, u32[]{:S(2)}) copy-start(bf16[784,256]{1,0:T(8,128)(2,1)} %get-tuple-element.69) | copy-start | bytes 1204228
  25.7 12.8 %collective-permute-start.5 = (bf16[784,256]{1,0:T(8,128)(2,1)S(1)}, bf16[784,256]{1,0:T(8,128)(2,1)S(1)}, u32[]{:S(2)}, u32[]{:S(2)}) collective-permute-start(bf16[784,256]{1,0:T(8,128)(2,1)S(1)} %copy-done.7), channel_id=1, source_target_pairs={{0,24},{4,28},{8,16},{12,20},{16,8},{20,12},{24,0},{28,4},{1,25},{... | collective-permute-start | bytes 1204232 | tf_op jit(solution)/shard_map/ppermute | solution.py:36
  32.4 12.8 %collective-permute-start.4 = (bf16[784,256]{1,0:T(8,128)(2,1)S(1)}, bf16[784,256]{1,0:T(8,128)(2,1)S(1)}, u32[]{:S(2)}, u32[]{:S(2)}) collective-permute-start(bf16[784,256]{1,0:T(8,128)(2,1)S(1)} %copy-done.6), channel_id=1, source_target_pairs={{0,28},{4,24},{8,20},{12,16},{16,12},{20,8},{24,4},{28,0},{1,29},{... | collective-permute-start | bytes 1204232 | tf_op jit(solution)/shard_map/ppermute | solution.py:36
  45.2 12.7 %copy-start.5 = (f32[2,8,256]{2,1,0:T(8,128)S(1)}, f32[2,8,256]{2,1,0:T(8,128)}, u32[]{:S(2)}) copy-start(f32[2,8,256]{2,1,0:T(8,128)} %get-tuple-element.84) | copy-start | bytes 49156
  48.6 1.9 %collective-permute-start.7 = (f32[2,128,256]{2,1,0:T(8,128)S(1)}, f32[2,128,256]{2,1,0:T(8,128)S(1)}, u32[]{:S(2)}, u32[]{:S(2)}) collective-permute-start(f32[2,128,256]{2,1,0:T(8,128)S(1)} %get-tuple-element.79), channel_id=1, source_target_pairs={{0,4},{4,0},{8,12},{12,8},{16,20},{20,16},{24,28},{28,24},{1,5},{5... | collective-permute-start | bytes 786440 | tf_op jit(solution)/shard_map/ppermute | solution.py:36
  50.5 5.3 %collective-permute-start.8 = (f32[2,32,256]{2,1,0:T(8,128)S(1)}, f32[2,32,256]{2,1,0:T(8,128)S(1)}, u32[]{:S(2)}, u32[]{:S(2)}) collective-permute-start(f32[2,32,256]{2,1,0:T(8,128)S(1)} %get-tuple-element.81), channel_id=1, source_target_pairs={{0,24},{4,28},{8,16},{12,20},{16,8},{20,12},{24,0},{28,4},{1,25},{... | collective-permute-start | bytes 196616 | tf_op jit(solution)/shard_map/ppermute | solution.py:36
  53.1 4.3 %collective-permute-start.9 = (f32[2,32,256]{2,1,0:T(8,128)S(1)}, f32[2,32,256]{2,1,0:T(8,128)S(1)}, u32[]{:S(2)}, u32[]{:S(2)}) collective-permute-start(f32[2,32,256]{2,1,0:T(8,128)S(1)} %get-tuple-element.82), channel_id=1, source_target_pairs={{0,16},{4,20},{8,24},{12,28},{16,0},{20,4},{24,8},{28,12},{1,17},{... | collective-permute-start | bytes 196616 | tf_op jit(solution)/shard_map/ppermute | solution.py:36
  53.6 4.3 %collective-permute-start.10 = (f32[2,32,256]{2,1,0:T(8,128)S(1)}, f32[2,32,256]{2,1,0:T(8,128)S(1)}, u32[]{:S(2)}, u32[]{:S(2)}) collective-permute-start(f32[2,32,256]{2,1,0:T(8,128)S(1)} %get-tuple-element.83), channel_id=1, source_target_pairs={{0,8},{4,12},{8,0},{12,4},{16,24},{20,28},{24,16},{28,20},{1,9},{5... | collective-permute-start | bytes 196616 | tf_op jit(solution)/shard_map/ppermute | solution.py:36
  57.9 4.5 %collective-permute-start.11 = (f32[2,40,256]{2,1,0:T(8,128)S(1)}, f32[2,40,256]{2,1,0:T(8,128)S(1)}, u32[]{:S(2)}, u32[]{:S(2)}) collective-permute-start(f32[2,40,256]{2,1,0:T(8,128)S(1)} %pad_maximum_fusion), channel_id=1, source_target_pairs={{0,1},{1,0},{2,3},{3,2},{4,5},{5,4},{6,7},{7,6},{8,9},{9,8},{10,11... | collective-permute-start | bytes 245768 | tf_op jit(solution)/shard_map/ppermute | solution.py:36
  62.5 5.4 %collective-permute-start.12 = (f32[2,40,256]{2,1,0:T(8,128)S(1)}, f32[2,40,256]{2,1,0:T(8,128)S(1)}, u32[]{:S(2)}, u32[]{:S(2)}) collective-permute-start(f32[2,40,256]{2,1,0:T(8,128)S(1)} %pad_maximum_fusion.1), channel_id=1, source_target_pairs={{0,2},{1,3},{2,0},{3,1},{4,6},{5,7},{6,4},{7,5},{8,10},{9,11},{10,... | collective-permute-start | bytes 245768 | tf_op jit(solution)/shard_map/ppermute | solution.py:36
  67.9 6.3 %collective-permute-start.15 = (f32[2,32,256]{2,1,0:T(8,128)S(1)}, f32[2,32,256]{2,1,0:T(8,128)S(1)}, u32[]{:S(2)}, u32[]{:S(2)}) collective-permute-start(f32[2,32,256]{2,1,0:T(8,128)S(1)} %slice_add_fusion.rest_0_), channel_id=1, source_target_pairs={{0,24},{4,28},{8,16},{12,20},{16,8},{20,12},{24,0},{28,4},{1,25},{... | collective-permute-start | bytes 196616 | tf_op jit(solution)/shard_map/ppermute | solution.py:36
  69.4 4.8 %collective-permute-start.14 = (f32[2,32,256]{2,1,0:T(8,128)S(1)}, f32[2,32,256]{2,1,0:T(8,128)S(1)}, u32[]{:S(2)}, u32[]{:S(2)}) collective-permute-start(f32[2,32,256]{2,1,0:T(8,128)S(1)} %slice_add_fusion.rest_0_), channel_id=1, source_target_pairs={{0,16},{4,20},{8,24},{12,28},{16,0},{20,4},{24,8},{28,12},{1,17},{... | collective-permute-start | bytes 196616 | tf_op jit(solution)/shard_map/ppermute | solution.py:36
  70.4 4.3 %collective-permute-start.13 = (f32[2,32,256]{2,1,0:T(8,128)S(1)}, f32[2,32,256]{2,1,0:T(8,128)S(1)}, u32[]{:S(2)}, u32[]{:S(2)}) collective-permute-start(f32[2,32,256]{2,1,0:T(8,128)S(1)} %slice_add_fusion.rest_0_), channel_id=1, source_target_pairs={{0,8},{4,12},{8,0},{12,4},{16,24},{20,28},{24,16},{28,20},{1,9},{5... | collective-permute-start | bytes 196616 | tf_op jit(solution)/shard_map/ppermute | solution.py:36
  74.7 1.6 %collective-permute-start.16 = (f32[2,128,256]{2,1,0:T(8,128)S(1)}, f32[2,128,256]{2,1,0:T(8,128)S(1)}, u32[]{:S(2)}, u32[]{:S(2)}) collective-permute-start(f32[2,128,256]{2,1,0:T(8,128)S(1)} %join.1.mine), channel_id=1, source_target_pairs={{0,4},{4,0},{8,12},{12,8},{16,20},{20,16},{24,28},{28,24},{1,5},{5... | collective-permute-start | bytes 786440 | tf_op jit(solution)/shard_map/ppermute | solution.py:36

commit v5 on v4

--- a/solution.py
+++ b/solution.py
@@ -119,8 +119,8 @@
         for plane in range(2):
             for part, first in enumerate(range(0, cols, size)):
                 width = min(size, cols - first)
-                place = i * rim_width(cols, size) + part
-                rim_rows[plane, place : place + 1, :width] = ends[i, plane, at : at + 1, first : first + width]
+                place = (2 * i + plane) * rim_width(cols, size) + part
+                rim_rows[place : place + 1, :width] = ends[i, plane, at : at + 1, first : first + width]
     store = pltpu.make_async_copy(rim_rows, rim, end_sems.at[2])
     store.start()
     stores.append(store)
@@ -133,12 +133,13 @@
     _, rows, cols = tile.shape
     far = pl.BlockSpec(memory_space=pltpu.HBM)
     ints = pltpu.SMEM((pos_dev,), jnp.int32)
+    rim_shape = (-(-4 * rim_width(cols, size) // SUBLANES) * SUBLANES, size)
     return pl.pallas_call(
         functools.partial(pack_kernel, n_pos, capacity, order),
         in_specs=[far] * 5,
         out_specs=[far] * (n_pos + 1),
         out_shape=[jax.ShapeDtypeStruct((capacity * size + INFO_ROWS, size), bf16)] * n_pos
-        + [jax.ShapeDtypeStruct((2, SUBLANES, size), f32)],
+        + [jax.ShapeDtypeStruct(rim_shape, f32)],
         scratch_shapes=[
             ints,
             ints,
@@ -150,7 +151,7 @@
             pltpu.VMEM((2, 2, SUBLANES, cols), f32),
             pltpu.VMEM((INFO_ROWS, size), f32),
             pltpu.VMEM((n_pos, INFO_ROWS, size), bf16),
-            pltpu.VMEM((2, SUBLANES, size), f32),
+            pltpu.VMEM(rim_shape, f32),
             pltpu.SemaphoreType.DMA((3,)),
             pltpu.SemaphoreType.DMA,
             pltpu.SemaphoreType.DMA((2,)),
@@ -193,8 +194,8 @@
     return jnp.concatenate([stacked[:size], stacked[size:]], axis=1)
 
 
-def buffer_terms(amp, amp_load, info, tile, probe, left, right, emit, term, capacity, size, parts):
-    numbers = read_info(info, 3 * capacity)
+def buffer_terms(amp, tile, probe, left, right, emit, term, capacity, size, parts):
+    numbers = read_info(amp[capacity * size :, :], 3 * capacity)
     slots = [tuple(numbers[3 * k : 3 * k + 3]) for k in range(capacity)]
     probe_re = probe[0]
     probe_im = probe[1]
@@ -209,7 +210,6 @@
     halves = [side_by_side(dot(left[...], psi).astype(bf16), size) for psi in psis]
     waves = [dot(half, right[...]) for half in halves]
     diffs = []
-    amp_load.wait()
     for k, wave in enumerate(waves):
         wave_re = wave[:, :size]
         wave_im = wave[:, size:]
@@ -236,16 +236,7 @@
 
 def terms_kernel(count, capacity, first, last, probe, left, right, *rest):
     size = probe.shape[1]
-    held, infos, sems = rest[-3:]
-    messages, rest = rest[:count], rest[count:-3]
-    info_loads, amp_loads = [], []
-    for i, message in enumerate(messages):
-        info_rows = pl.ds(capacity * size, INFO_ROWS)
-        amp_rows = pl.ds(0, capacity * size)
-        info_loads.append(pltpu.make_async_copy(message.at[info_rows], infos.at[i], sems.at[i, 0]))
-        amp_loads.append(pltpu.make_async_copy(message.at[amp_rows], held.at[i], sems.at[i, 1]))
-    for load in info_loads + amp_loads:
-        load.start()
+    messages, rest = rest[:count], rest[count:]
     if first:
         source, tile, acc, term = rest
         parts = tile.shape[0] // 2
@@ -271,11 +262,8 @@
         else:
             add_window(acc, plane, row, col, grad.astype(f32), size, parts)
 
-    for i in range(count):
-        info_loads[i].wait()
-        buffer_terms(
-            held.at[i], amp_loads[i], infos[i], tile, probe, left, right, emit, term, capacity, size, parts
-        )
+    for message in messages:
+        buffer_terms(message, tile, probe, left, right, emit, term, capacity, size, parts)
     if last:
         half = size // 2
         odd = lax.rem(lax.axis_index("pos"), 2)
@@ -287,12 +275,7 @@
     size = probe.shape[1]
     count = len(messages)
     full = pl.BlockSpec(memory_space=pltpu.VMEM)
-    far = pl.BlockSpec(memory_space=pltpu.HBM)
-    scratch = [
-        pltpu.VMEM((count, capacity * size, size), bf16),
-        pltpu.VMEM((count, INFO_ROWS, size), bf16),
-        pltpu.SemaphoreType.DMA((count, 2)),
-    ]
+    scratch = []
     if state is None:
         _, rows, cols = source.shape
         blocks = jax.ShapeDtypeStruct((2 * cols // LANES, rows, LANES), f32)
@@ -305,7 +288,7 @@
             operands = (tile, term)
             shapes = [jax.ShapeDtypeStruct((capacity, 2, size, size), bf16)]
             shapes += [jax.ShapeDtypeStruct((2, size // 2, size), f32)] * 2
-            scratch = [pltpu.VMEM(term.shape, f32)] + scratch
+            scratch = [pltpu.VMEM(term.shape, f32)]
             aliases = {}
         else:
             operands = state
@@ -313,7 +296,7 @@
             aliases = {4 + count: 0, 5 + count: 1}
     results = pl.pallas_call(
         functools.partial(terms_kernel, count, capacity, state is None, last),
-        in_specs=[full] * 3 + [far] * count + [full] * len(operands),
+        in_specs=[full] * (3 + count + len(operands)),
         out_specs=[full] * len(shapes),
         out_shape=shapes,
         scratch_shapes=scratch,
@@ -383,15 +366,15 @@
         return jnp.concatenate([jnp.transpose(jnp.broadcast_to(v, (LANES, size))) for v in values], axis=0)
 
     level = lax.axis_index("obj")
-    rim_at = ends[0].shape[1] - SUBLANES
+    rim_at = 2 * size // n_pos
 
     def end_row(side, plane, k):
         neighbour = lax.rem(level + (n_obj - 1 if side == 0 else 1), n_obj)
-        place = rim_at + (rim_width(cols, size) if side == 0 else 0) + k * LANES // size
+        place = rim_at + (2 * (1 - side) + plane) * rim_width(cols, size) + k * LANES // size
         lanes = slice(k * LANES % size, k * LANES % size + LANES)
         value = jnp.zeros((1, LANES), f32)
         for block, step in zip(ends, steps):
-            value = jnp.where(jnp.bitwise_xor(level, neighbour) == step, block[plane, place : place + 1, lanes], value)
+            value = jnp.where(jnp.bitwise_xor(level, neighbour) == step, block[place : place + 1, lanes], value)
         return value
 
     lane = lax.broadcasted_iota(jnp.int32, (rows, LANES), 1)
@@ -459,11 +442,31 @@
         out[:, pl.ds(pl.multiple_of(start, rows), rows), :] = old - pieces[d][...] * scale
 
 
-def whole_kernel(mine, other, out):
+def whole_kernel(mine, other, out, sems):
     half = mine.shape[1]
     odd = lax.rem(lax.axis_index("pos"), 2)
-    out[:, pl.ds(pl.multiple_of(odd * half, half), half), :] = mine[...]
-    out[:, pl.ds(pl.multiple_of((1 - odd) * half, half), half), :] = other[...]
+    copies = [
+        pltpu.make_async_copy(value, out.at[:, pl.ds(pl.multiple_of(which * half, half), half), :], sems.at[i])
+        for i, (value, which) in enumerate(((mine, odd), (other, 1 - odd)))
+    ]
+    for copy in copies:
+        copy.start()
+    for copy in copies:
+        copy.wait()
+
+
+def whole(mine, other):
+    planes, half, size = mine.shape
+    full = pl.BlockSpec(memory_space=pltpu.VMEM)
+    return pl.pallas_call(
+        whole_kernel,
+        in_specs=[full, full],
+        out_specs=pl.BlockSpec(memory_space=pltpu.HBM),
+        out_shape=jax.ShapeDtypeStruct((planes, 2 * half, size), f32),
+        scratch_shapes=[pltpu.SemaphoreType.DMA((2,))],
+        compiler_params=pltpu.CompilerParams(vmem_limit_bytes=SMALL_VMEM),
+        name="whole",
+    )(mine, other)
 
 
 def step_probe(probe, keep, send, scale, rim, acc, beside):
@@ -480,11 +483,12 @@
         total = total + exchange(pieces[d], "pos", 2 * d)
     steps, ends = [], []
     while 2 ** len(steps) < n_obj:
-        got = exchange(jnp.concatenate([total, rim], axis=1), "obj", 2 ** len(steps))
+        flat = total.reshape(planes * rows, size)
+        got = exchange(jnp.concatenate([flat, rim]), "obj", 2 ** len(steps))
         if not steps:
             got, acc = lax.optimization_barrier((got, acc))
-        total = total + got[:, :rows]
-        rim = got[:, rows:]
+        total = total + got[: planes * rows].reshape(total.shape)
+        rim = got[planes * rows :]
         steps.append(2 ** (len(steps) + 1) - 1)
         ends.append(got)
     gathered = [total] + [exchange(total, "pos", 2 * d) for d in range(1, pairs)]
@@ -496,7 +500,7 @@
         jax.ShapeDtypeStruct(keep.shape, f32),
     )
     other = exchange(mine, "pos", 1)
-    new_probe = small_call(whole_kernel, "whole", (mine, other), jax.ShapeDtypeStruct(probe.shape, f32))
+    new_probe = whole(mine, other)
     return new_probe, result
 
 

time: 77.3 us -> 76.4 us (0.988)
  Pallas kernels: 38.1 us -> 35 us
  waiting for transfers between devices: 17.9 us -> 19.3 us
    pallas_call x8, Pallas kernels: 29.7 us -> 26.7 us  [terms(): pl.pallas_call(functools.partial(terms_kernel, count, capacity, state is...]
    ppermute x17, waiting for transfers between devices: 17.9 us -> 19.3 us  [exchange(): return lax.ppermute(value, axis, [(i, i ^ distance) for i in range(count)])]
    pallas_call x3 -> x2, Pallas kernels: 0.92 us -> 0.08 us  [small_call(): pl.pallas_call(body, out_shape=shapes, compiler_params=pltpu.CompilerPara...]
    pallas_call x0 -> x1, Pallas kernels: none -> 0.8 us  [whole(): pl.pallas_call(whole_kernel, in_specs=[full, full], out_specs=pl.BlockSpe...]
  transfers between devices with their start and end apart: 17 -> 17, of which waited for: 11 -> 11; matrix products, arithmetic and copies ran while one was open for 0% -> 0% of each run, Pallas kernels for 39% -> 35%
where the time goes in v5:
time: 76.4 us; the launch traced here: 76.3 us
  Pallas kernels  35 us (46%)
  starting transfers between devices  20.8 us (27%)
  waiting for transfers between devices  19.3 us (25%)
  between operations  1.07 us (1%)
    pallas_call x8, Pallas kernels, terms(): pl.pallas_call(functools.partial(terms_kernel, count, capacity, state is...  26.7 us
    ppermute x17, starting transfers between devices, exchange(): return lax.ppermute(value, axis, [(i, i ^ distance) for i in range(count)])  20.8 us
    ppermute x17, waiting for transfers between devices, exchange(): return lax.ppermute(value, axis, [(i, i ^ distance) for i in range(count)])  19.3 us
    pallas_call x1, Pallas kernels, pack(): pl.pallas_call(functools.partial(pack_kernel, n_pos, capacity, order), in...  3.95 us
    pallas_call x1, Pallas kernels, finish(): pl.pallas_call(functools.partial(finish_kernel, n_pos, n_obj, ring, steps...  2.77 us
  transfers between devices with their start and end apart: 17, of which 11 were waited for; matrix products, arithmetic and copies ran while one was open for 0% of the time, Pallas kernels for 35%

profile of v5, /device:TPU:0, one launch (start us, length us, event | category | flops | bytes accessed | tf_op | source)
XLA Modules:
  0.0 76.3 jit_solution(11332601767739547078)
XLA Ops:
  0.6 0.0 copy-start.1
  0.6 0.0 copy-start.2
  0.7 0.0 copy-start.3
  0.7 0.0 copy-start
  0.7 4.0 %pack.1 = (bf16[784,256]{1,0:T(8,128)(2,1)}, bf16[784,256]{1,0:T(8,128)(2,1)}, bf16[784,256]{1,0:T(8,128)(2,1)}, bf16[784,256]{1,0:T(8,128)(2,1)}, bf16[784,256]...) custom-call(s32[16]{0:T(128)} %owner_in.1, ...), custom_call_target="tpu_custom_call" | custom-call | flops 1048576 | bytes 1048576 | tf_op jit(solution)/shard_map/pack/pallas_call | solution.py:137
  4.6 0.5 collective-permute-start
  5.2 2.6 %collective-permute-start.2 = (bf16[784,256]{1,0:T(8,128)(2,1)}, bf16[784,256]{1,0:T(8,128)(2,1)S(1)}, u32[]{:S(2)}, u32[]{:S(2)}) collective-permute-start(bf16[784,256]{1,0:T(8,128)(2,1)} %get-tuple-element.51), channel_id=1, source_target_pairs={{0,8},{4,12},{8,0},{12,4},{16,24},{20,28},{24,16},{28,20},{1,9},{5... | collective-permute-start | bytes 1204232 | tf_op jit(solution)/shard_map/ppermute | solution.py:36
  7.7 1.5 %collective-permute-start.1 = (bf16[784,256]{1,0:T(8,128)(2,1)}, bf16[784,256]{1,0:T(8,128)(2,1)S(1)}, u32[]{:S(2)}, u32[]{:S(2)}) collective-permute-start(bf16[784,256]{1,0:T(8,128)(2,1)} %get-tuple-element.50), channel_id=1, source_target_pairs={{0,16},{4,20},{8,24},{12,28},{16,0},{20,4},{24,8},{28,12},{1,17},{... | collective-permute-start | bytes 1204232 | tf_op jit(solution)/shard_map/ppermute | solution.py:36
  9.2 0.0 collective-permute-start.3
  9.3 0.0 copy-start.4
  9.3 0.3 collective-permute-start.6
  9.6 0.0 collective-permute-done.rest_0_.rest_2_
  9.6 0.0 copy-done.1
  9.6 0.0 copy-done.2
  9.6 0.0 copy-done.3
  9.6 0.0 copy-done
  9.6 3.2 %terms.8 = (f32[6,512,128]{2,1,0:T(8,128)S(1)}, f32[6,512,128]{2,1,0:T(8,128)S(1)}, f32[2,256,256]{2,1,0:T(8,128)S(1)}) custom-call(f32[2,256,256]{2,1,0:T(8,128)S(1)} %copy-done, bf16[512,512]{1,0:T(8,128)(2,1)S(1)} %copy-done.2, bf16[512,512]{1,0:T(8,128)(2,1)S(1)} %copy-done.1, bf16[784,256]{1,0:T(8,128)(2,1)S(1)} %collective-permute-done.rest_0_.rest_2_, ...), custom_call_target="tpu_custom_call" | custom-call | flops 100663296 | bytes 262144 | tf_op jit(solution)/shard_map/terms/pallas_call | solution.py:297
  12.8 0.0 copy-done.4
  12.8 3.4 %terms.9 = (f32[6,512,128]{2,1,0:T(8,128)S(1)}, f32[2,256,256]{2,1,0:T(8,128)S(1)}) custom-call(f32[2,256,256]{2,1,0:T(8,128)S(1)} %copy-done, bf16[512,512]{1,0:T(8,128)(2,1)S(1)} %copy-done.2, bf16[512,512]{1,0:T(8,128)(2,1)S(1)} %copy-done.1, bf16[784,256]{1,0:T(8,128)(2,1)S(1)} %copy-done.4, ...), custom_call_target="tpu_custom_call", output_to_operand_aliasing={{0}: (5, {}), {1}: (6, {})} | custom-call | flops 100663296 | bytes 262144 | tf_op jit(solution)/shard_map/terms/pallas_call | solution.py:297
  16.2 1.9 %collective-permute-done.2.rest_0_ = bf16[784,256]{1,0:T(8,128)(2,1)S(1)} collective-permute-done((bf16[784,256]{1,0:T(8,128)(2,1)}, bf16[784,256]{1,0:T(8,128)(2,1)S(1)}, u32[]{:S(2)}, u32[]{:S(2)}) %collective-permute-start.2) | collective-permute-done | bytes 401440 | tf_op jit(solution)/shard_map/ppermute | solution.py:36
  18.1 3.4 %terms.10 = (f32[6,512,128]{2,1,0:T(8,128)S(1)}, f32[2,256,256]{2,1,0:T(8,128)S(1)}) custom-call(f32[2,256,256]{2,1,0:T(8,128)S(1)} %copy-done, bf16[512,512]{1,0:T(8,128)(2,1)S(1)} %copy-done.2, bf16[512,512]{1,0:T(8,128)(2,1)S(1)} %copy-done.1, bf16[784,256]{1,0:T(8,128)(2,1)S(1)} %collective-permute-done.2.rest_0_, ...), custom_call_target="tpu_custom_call", output_to_operand_aliasing={{0}: (5, {}), {1}: (6, {})} | custom-call | flops 100663296 | bytes 262144 | tf_op jit(solution)/shard_map/terms/pallas_call | solution.py:297
  21.4 0.0 collective-permute-done.1.rest_0_
  21.4 0.0 copy-start.7
  21.5 3.5 %terms.11 = (f32[6,512,128]{2,1,0:T(8,128)S(1)}, f32[2,256,256]{2,1,0:T(8,128)S(1)}) custom-call(f32[2,256,256]{2,1,0:T(8,128)S(1)} %copy-done, bf16[512,512]{1,0:T(8,128)(2,1)S(1)} %copy-done.2, bf16[512,512]{1,0:T(8,128)(2,1)S(1)} %copy-done.1, bf16[784,256]{1,0:T(8,128)(2,1)S(1)} %collective-permute-done.1.rest_0_, ...), custom_call_target="tpu_custom_call", output_to_operand_aliasing={{0}: (5, {}), {1}: (6, {})} | custom-call | flops 100663296 | bytes 262144 | tf_op jit(solution)/shard_map/terms/pallas_call | solution.py:297
  25.0 0.0 copy-done.7
  25.0 0.0 copy-start.6
  25.0 3.0 %collective-permute-start.5 = (bf16[784,256]{1,0:T(8,128)(2,1)S(1)}, bf16[784,256]{1,0:T(8,128)(2,1)S(1)}, u32[]{:S(2)}, u32[]{:S(2)}) collective-permute-start(bf16[784,256]{1,0:T(8,128)(2,1)S(1)} %copy-done.7), channel_id=1, source_target_pairs={{0,24},{4,28},{8,16},{12,20},{16,8},{20,12},{24,0},{28,4},{1,25},{... | collective-permute-start | bytes 1204232 | tf_op jit(solution)/shard_map/ppermute | solution.py:36
  28.0 0.0 collective-permute-done.3.rest_0_.rest_3_
  28.0 3.4 %terms.12 = (f32[6,512,128]{2,1,0:T(8,128)S(1)}, f32[2,256,256]{2,1,0:T(8,128)S(1)}) custom-call(f32[2,256,256]{2,1,0:T(8,128)S(1)} %copy-done, bf16[512,512]{1,0:T(8,128)(2,1)S(1)} %copy-done.2, bf16[512,512]{1,0:T(8,128)(2,1)S(1)} %copy-done.1, ...), custom_call_target="tpu_custom_call", output_to_operand_aliasing={{0}: (5, {}), {1}: (6, {})} | custom-call | flops 100663296 | bytes 262144 | tf_op jit(solution)/shard_map/terms/pallas_call | solution.py:297
  31.4 0.0 copy-done.6
  31.4 0.6 collective-permute-start.4
  32.0 0.0 collective-permute-done.6.rest_0_
  32.0 3.4 %terms.13 = (f32[6,512,128]{2,1,0:T(8,128)S(1)}, f32[2,256,256]{2,1,0:T(8,128)S(1)}) custom-call(f32[2,256,256]{2,1,0:T(8,128)S(1)} %copy-done, bf16[512,512]{1,0:T(8,128)(2,1)S(1)} %copy-done.2, bf16[512,512]{1,0:T(8,128)(2,1)S(1)} %copy-done.1, bf16[784,256]{1,0:T(8,128)(2,1)S(1)} %collective-permute-done.6.rest_0_, ...), custom_call_target="tpu_custom_call", output_to_operand_aliasing={{0}: (5, {}), {1}: (6, {})} | custom-call | flops 100663296 | bytes 262144 | tf_op jit(solution)/shard_map/terms/pallas_call | solution.py:297
  35.4 2.8 %collective-permute-done.5.rest_0_ = bf16[784,256]{1,0:T(8,128)(2,1)S(1)} collective-permute-done((bf16[784,256]{1,0:T(8,128)(2,1)S(1)}, bf16[784,256]{1,0:T(8,128)(2,1)S(1)}, u32[]{:S(2)}, u32[]{:S(2)}) %collective-permute-start.5) | collective-permute-done | bytes 401440 | tf_op jit(solution)/shard_map/ppermute | solution.py:36
  38.2 3.4 %terms.14 = (f32[6,512,128]{2,1,0:T(8,128)S(1)}, f32[2,256,256]{2,1,0:T(8,128)S(1)}) custom-call(f32[2,256,256]{2,1,0:T(8,128)S(1)} %copy-done, bf16[512,512]{1,0:T(8,128)(2,1)S(1)} %copy-done.2, bf16[512,512]{1,0:T(8,128)(2,1)S(1)} %copy-done.1, bf16[784,256]{1,0:T(8,128)(2,1)S(1)} %collective-permute-done.5.rest_0_, ...), custom_call_target="tpu_custom_call", output_to_operand_aliasing={{0}: (5, {}), {1}: (6, {})} | custom-call | flops 100663296 | bytes 262144 | tf_op jit(solution)/shard_map/terms/pallas_call | solution.py:297
  41.6 2.9 %collective-permute-done.4.rest_0_.message.rest_4_ = bf16[784,256]{1,0:T(8,128)(2,1)S(1)} collective-permute-done((bf16[784,256]{1,0:T(8,128)(2,1)S(1)}, bf16[784,256]{1,0:T(8,128)(2,1)S(1)}, u32[]{:S(2)}, u32[]{:S(2)}) %collective-permute-start.4) | collective-permute-done | bytes 401440 | tf_op jit(solution)/shard_map/ppermute | solution.py:36
  44.5 0.0 copy-start.5
  44.5 3.2 %terms.15 = (bf16[3,2,256,256]{3,2,1,0:T(8,128)(2,1)S(1)}, f32[2,128,256]{2,1,0:T(8,128)S(1)}, f32[2,128,256]{2,1,0:T(8,128)S(1)}) custom-call(f32[2,256,256]{2,1,0:T(8,128)S(1)} %copy-done, bf16[512,512]{1,0:T(8,128)(2,1)S(1)} %copy-done.2, bf16[512,512]{1,0:T(8,128)(2,1)S(1)} %copy-done.1, ...), custom_call_target="tpu_custom_call" | custom-call | flops 100663296 | bytes 262144 | tf_op jit(solution)/shard_map/terms/pallas_call | solution.py:297
  47.7 0.8 %collective-permute-start.7 = (f32[2,128,256]{2,1,0:T(8,128)S(1)}, f32[2,128,256]{2,1,0:T(8,128)S(1)}, u32[]{:S(2)}, u32[]{:S(2)}) collective-permute-start(f32[2,128,256]{2,1,0:T(8,128)S(1)} %get-tuple-element.79), channel_id=1, source_target_pairs={{0,4},{4,0},{8,12},{12,8},{16,20},{20,16},{24,28},{28,24},{1,5},{5... | collective-permute-start | bytes 786440 | tf_op jit(solution)/shard_map/ppermute | solution.py:36
  48.4 1.2 %collective-permute-done.7.got = f32[2,128,256]{2,1,0:T(8,128)S(1)} collective-permute-done((f32[2,128,256]{2,1,0:T(8,128)S(1)}, f32[2,128,256]{2,1,0:T(8,128)S(1)}, u32[]{:S(2)}, u32[]{:S(2)}) %collective-permute-start.7) | collective-permute-done | bytes 262176 | tf_op jit(solution)/shard_map/ppermute | solution.py:36
  49.6 2.6 %collective-permute-start.8 = (f32[2,32,256]{2,1,0:T(8,128)S(1)}, f32[2,32,256]{2,1,0:T(8,128)S(1)}, u32[]{:S(2)}, u32[]{:S(2)}) collective-permute-start(f32[2,32,256]{2,1,0:T(8,128)S(1)} %get-tuple-element.81), channel_id=1, source_target_pairs={{0,24},{4,28},{8,16},{12,20},{16,8},{20,12},{24,0},{28,4},{1,25},{... | collective-permute-start | bytes 196616 | tf_op jit(solution)/shard_map/ppermute | solution.py:36
  52.2 0.5 collective-permute-start.9
  52.7 0.5 collective-permute-start.10
  53.2 1.8 %collective-permute-done.8 = f32[2,32,256]{2,1,0:T(8,128)S(1)} collective-permute-done((f32[2,32,256]{2,1,0:T(8,128)S(1)}, f32[2,32,256]{2,1,0:T(8,128)S(1)}, u32[]{:S(2)}, u32[]{:S(2)}) %collective-permute-start.8) | collective-permute-done | bytes 65568 | tf_op jit(solution)/shard_map/ppermute | solution.py:36
  55.0 1.5 %collective-permute-done.9 = f32[2,32,256]{2,1,0:T(8,128)S(1)} collective-permute-done((f32[2,32,256]{2,1,0:T(8,128)S(1)}, f32[2,32,256]{2,1,0:T(8,128)S(1)}, u32[]{:S(2)}, u32[]{:S(2)}) %collective-permute-start.9) | collective-permute-done | bytes 65568 | tf_op jit(solution)/shard_map/ppermute | solution.py:36
  56.5 0.5 collective-permute-done.10
  57.0 0.0 copy-done.5
  57.1 1.7 %collective-permute-start.11 = (f32[72,256]{1,0:T(8,128)S(1)}, f32[72,256]{1,0:T(8,128)S(1)}, u32[]{:S(2)}, u32[]{:S(2)}) collective-permute-start(f32[72,256]{1,0:T(8,128)S(1)} %pad_maximum_fusion), channel_id=1, source_target_pairs={{0,1},{1,0},{2,3},{3,2},{4,5},{5,4},{6,7},{7,6},{8,9},{9,8},{10,11... | collective-permute-start | bytes 221192 | tf_op jit(solution)/shard_map/ppermute | solution.py:36
  58.7 0.7 add.24.acc
  59.4 2.1 %collective-permute-done.11.rest_0_ = f32[72,256]{1,0:T(8,128)S(1)} collective-permute-done((f32[72,256]{1,0:T(8,128)S(1)}, f32[72,256]{1,0:T(8,128)S(1)}, u32[]{:S(2)}, u32[]{:S(2)}) %collective-permute-start.11) | collective-permute-done | bytes 73760 | tf_op jit(solution)/shard_map/ppermute | solution.py:36
  61.5 2.6 %collective-permute-start.12 = (f32[72,256]{1,0:T(8,128)S(1)}, f32[72,256]{1,0:T(8,128)S(1)}, u32[]{:S(2)}, u32[]{:S(2)}) collective-permute-start(f32[72,256]{1,0:T(8,128)S(1)} %pad_maximum_fusion.1), channel_id=1, source_target_pairs={{0,2},{1,3},{2,0},{3,1},{4,6},{5,7},{6,4},{7,5},{8,10},{9,11},{10,... | collective-permute-start | bytes 221192 | tf_op jit(solution)/shard_map/ppermute | solution.py:36
  64.2 2.7 %collective-permute-done.12.rest_1_ = f32[72,256]{1,0:T(8,128)S(1)} collective-permute-done((f32[72,256]{1,0:T(8,128)S(1)}, f32[72,256]{1,0:T(8,128)S(1)}, u32[]{:S(2)}, u32[]{:S(2)}) %collective-permute-start.12) | collective-permute-done | bytes 73760 | tf_op jit(solution)/shard_map/ppermute | solution.py:36
  66.9 1.6 %collective-permute-start.15 = (f32[2,32,256]{2,1,0:T(8,128)S(1)}, f32[2,32,256]{2,1,0:T(8,128)S(1)}, u32[]{:S(2)}, u32[]{:S(2)}) collective-permute-start(f32[2,32,256]{2,1,0:T(8,128)S(1)} %add.20.rest_0_), channel_id=1, source_target_pairs={{0,24},{4,28},{8,16},{12,20},{16,8},{20,12},{24,0},{28,4},{1,25},{... | collective-permute-start | bytes 196616 | tf_op jit(solution)/shard_map/ppermute | solution.py:36
  68.4 0.9 %collective-permute-start.14 = (f32[2,32,256]{2,1,0:T(8,128)S(1)}, f32[2,32,256]{2,1,0:T(8,128)S(1)}, u32[]{:S(2)}, u32[]{:S(2)}) collective-permute-start(f32[2,32,256]{2,1,0:T(8,128)S(1)} %add.20.rest_0_), channel_id=1, source_target_pairs={{0,16},{4,20},{8,24},{12,28},{16,0},{20,4},{24,8},{28,12},{1,17},{... | collective-permute-start | bytes 196616 | tf_op jit(solution)/shard_map/ppermute | solution.py:36
  69.4 1.1 %collective-permute-start.13 = (f32[2,32,256]{2,1,0:T(8,128)S(1)}, f32[2,32,256]{2,1,0:T(8,128)S(1)}, u32[]{:S(2)}, u32[]{:S(2)}) collective-permute-start(f32[2,32,256]{2,1,0:T(8,128)S(1)} %add.20.rest_0_), channel_id=1, source_target_pairs={{0,8},{4,12},{8,0},{12,4},{16,24},{20,28},{24,16},{28,20},{1,9},{5... | collective-permute-start | bytes 196616 | tf_op jit(solution)/shard_map/ppermute | solution.py:36
  70.4 2.8 %finish.1 = f32[2,512,384]{2,1,0:T(8,128)} custom-call(f32[2,512,384]{2,1,0:T(8,128)S(1)} %copy-done.3, f32[6,512,128]{2,1,0:T(8,128)S(1)} %add.24.acc, f32[72,256]{1,0:T(8,128)S(1)} %collective-permute-done.11.rest_0_, f32[72,256]{1,0:T(8,128)S(1)} %collective-permute-done.12.rest_1_, bf16[784,256]{1,0:T(8,128)(2,1)S(1)} %collective-permute-done.rest_0_.rest_2_, ...), custom_call_target="tpu_custom_call" | custom-call | flops 16777216 | bytes 8388608 | tf_op jit(solution)/shard_map/finish/pallas_call | solution.py:401
  73.2 0.0 collective-permute-done.15.rest_3_
  73.2 0.0 collective-permute-done.14.rest_2_
  73.2 0.4 collective-permute-done.13.rest_1_
  73.7 0.1 collective-permute-start.16
  73.8 1.5 %collective-permute-done.16.other = f32[2,128,256]{2,1,0:T(8,128)S(1)} collective-permute-done((f32[2,128,256]{2,1,0:T(8,128)S(1)}, f32[2,128,256]{2,1,0:T(8,128)S(1)}, u32[]{:S(2)}, u32[]{:S(2)}) %collective-permute-start.16) | collective-permute-done | bytes 262176 | tf_op jit(solution)/shard_map/ppermute | solution.py:36
  75.3 0.8 %whole.1 = f32[2,256,256]{2,1,0:T(8,128)} custom-call(f32[2,128,256]{2,1,0:T(8,128)S(1)} %join.1.mine, f32[2,128,256]{2,1,0:T(8,128)S(1)} %collective-permute-done.16.other), custom_call_target="tpu_custom_call" | custom-call | tf_op jit(solution)/shard_map/whole/pallas_call | solution.py:461
  (10 shorter events, 0.1 us)
Async XLA Ops:
  0.6 8.9 %copy-start.1 = (bf16[512,512]{1,0:T(8,128)(2,1)S(1)}, bf16[512,512]{1,0:T(8,128)(2,1)}, u32[]{:S(2)}) copy-start(bf16[512,512]{1,0:T(8,128)(2,1)} %constant.5.clone.right) | copy-start | bytes 1572868
  0.6 8.9 %copy-start.2 = (bf16[512,512]{1,0:T(8,128)(2,1)S(1)}, bf16[512,512]{1,0:T(8,128)(2,1)}, u32[]{:S(2)}) copy-start(bf16[512,512]{1,0:T(8,128)(2,1)} %constant.4.clone.left) | copy-start | bytes 1572868
  0.7 8.9 %copy-start.3 = (f32[2,512,384]{2,1,0:T(8,128)S(1)}, f32[2,512,384]{2,1,0:T(8,128)}, u32[]{:S(2)}) copy-start(f32[2,512,384]{2,1,0:T(8,128)} %tile.3) | copy-start | bytes 4718596
  0.7 8.9 %copy-start = (f32[2,256,256]{2,1,0:T(8,128)S(1)}, f32[2,256,256]{2,1,0:T(8,128)}, u32[]{:S(2)}) copy-start(f32[2,256,256]{2,1,0:T(8,128)} %probe.17) | copy-start | bytes 1572868
  4.6 4.9 %collective-permute-start = (bf16[784,256]{1,0:T(8,128)(2,1)}, bf16[784,256]{1,0:T(8,128)(2,1)S(1)}, u32[]{:S(2)}, u32[]{:S(2)}) collective-permute-start(bf16[784,256]{1,0:T(8,128)(2,1)} %get-tuple-element.48), channel_id=1, source_target_pairs={{0,4},{4,0},{8,12},{12,8},{16,20},{20,16},{24,28},{28,24},{1,5},{5... | collective-permute-start | bytes 1204232 | tf_op jit(solution)/shard_map/ppermute | solution.py:36
  5.2 12.9 %collective-permute-start.2 = (bf16[784,256]{1,0:T(8,128)(2,1)}, bf16[784,256]{1,0:T(8,128)(2,1)S(1)}, u32[]{:S(2)}, u32[]{:S(2)}) collective-permute-start(bf16[784,256]{1,0:T(8,128)(2,1)} %get-tuple-element.51), channel_id=1, source_target_pairs={{0,8},{4,12},{8,0},{12,4},{16,24},{20,28},{24,16},{28,20},{1,9},{5... | collective-permute-start | bytes 1204232 | tf_op jit(solution)/shard_map/ppermute | solution.py:36
  7.7 13.7 %collective-permute-start.1 = (bf16[784,256]{1,0:T(8,128)(2,1)}, bf16[784,256]{1,0:T(8,128)(2,1)S(1)}, u32[]{:S(2)}, u32[]{:S(2)}) collective-permute-start(bf16[784,256]{1,0:T(8,128)(2,1)} %get-tuple-element.50), channel_id=1, source_target_pairs={{0,16},{4,20},{8,24},{12,28},{16,0},{20,4},{24,8},{28,12},{1,17},{... | collective-permute-start | bytes 1204232 | tf_op jit(solution)/shard_map/ppermute | solution.py:36
  9.2 18.8 %collective-permute-start.3 = (bf16[784,256]{1,0:T(8,128)(2,1)}, bf16[784,256]{1,0:T(8,128)(2,1)S(1)}, u32[]{:S(2)}, u32[]{:S(2)}) collective-permute-start(bf16[784,256]{1,0:T(8,128)(2,1)} %get-tuple-element.63), channel_id=1, source_target_pairs={{0,12},{4,8},{8,4},{12,0},{16,28},{20,24},{24,20},{28,16},{1,13},{... | collective-permute-start | bytes 1204232 | tf_op jit(solution)/shard_map/ppermute | solution.py:36
  9.3 3.5 %copy-start.4 = (bf16[784,256]{1,0:T(8,128)(2,1)S(1)}, bf16[784,256]{1,0:T(8,128)(2,1)}, u32[]{:S(2)}) copy-start(bf16[784,256]{1,0:T(8,128)(2,1)} %get-tuple-element.52.rest_0_) | copy-start | bytes 1204228
  9.3 22.7 %collective-permute-start.6 = (bf16[784,256]{1,0:T(8,128)(2,1)}, bf16[784,256]{1,0:T(8,128)(2,1)S(1)}, u32[]{:S(2)}, u32[]{:S(2)}) collective-permute-start(bf16[784,256]{1,0:T(8,128)(2,1)} %get-tuple-element.72), channel_id=1, source_target_pairs={{0,20},{4,16},{8,28},{12,24},{16,4},{20,0},{24,12},{28,8},{1,21},{... | collective-permute-start | bytes 1204232 | tf_op jit(solution)/shard_map/ppermute | solution.py:36
  21.4 3.6 %copy-start.7 = (bf16[784,256]{1,0:T(8,128)(2,1)S(1)}, bf16[784,256]{1,0:T(8,128)(2,1)}, u32[]{:S(2)}) copy-start(bf16[784,256]{1,0:T(8,128)(2,1)} %get-tuple-element.71) | copy-start | bytes 1204228
  25.0 6.4 %copy-start.6 = (bf16[784,256]{1,0:T(8,128)(2,1)S(1)}, bf16[784,256]{1,0:T(8,128)(2,1)}, u32[]{:S(2)}) copy-start(bf16[784,256]{1,0:T(8,128)(2,1)} %get-tuple-element.69) | copy-start | bytes 1204228
  25.0 13.2 %collective-permute-start.5 = (bf16[784,256]{1,0:T(8,128)(2,1)S(1)}, bf16[784,256]{1,0:T(8,128)(2,1)S(1)}, u32[]{:S(2)}, u32[]{:S(2)}) collective-permute-start(bf16[784,256]{1,0:T(8,128)(2,1)S(1)} %copy-done.7), channel_id=1, source_target_pairs={{0,24},{4,28},{8,16},{12,20},{16,8},{20,12},{24,0},{28,4},{1,25},{... | collective-permute-start | bytes 1204232 | tf_op jit(solution)/shard_map/ppermute | solution.py:36
  31.4 13.1 %collective-permute-start.4 = (bf16[784,256]{1,0:T(8,128)(2,1)S(1)}, bf16[784,256]{1,0:T(8,128)(2,1)S(1)}, u32[]{:S(2)}, u32[]{:S(2)}) collective-permute-start(bf16[784,256]{1,0:T(8,128)(2,1)S(1)} %copy-done.6), channel_id=1, source_target_pairs={{0,28},{4,24},{8,20},{12,16},{16,12},{20,8},{24,4},{28,0},{1,29},{... | collective-permute-start | bytes 1204232 | tf_op jit(solution)/shard_map/ppermute | solution.py:36
  44.5 12.5 %copy-start.5 = (f32[8,256]{1,0:T(8,128)S(1)}, f32[8,256]{1,0:T(8,128)}, u32[]{:S(2)}) copy-start(f32[8,256]{1,0:T(8,128)} %get-tuple-element.84) | copy-start | bytes 24580
  47.7 1.9 %collective-permute-start.7 = (f32[2,128,256]{2,1,0:T(8,128)S(1)}, f32[2,128,256]{2,1,0:T(8,128)S(1)}, u32[]{:S(2)}, u32[]{:S(2)}) collective-permute-start(f32[2,128,256]{2,1,0:T(8,128)S(1)} %get-tuple-element.79), channel_id=1, source_target_pairs={{0,4},{4,0},{8,12},{12,8},{16,20},{20,16},{24,28},{28,24},{1,5},{5... | collective-permute-start | bytes 786440 | tf_op jit(solution)/shard_map/ppermute | solution.py:36
  49.6 5.3 %collective-permute-start.8 = (f32[2,32,256]{2,1,0:T(8,128)S(1)}, f32[2,32,256]{2,1,0:T(8,128)S(1)}, u32[]{:S(2)}, u32[]{:S(2)}) collective-permute-start(f32[2,32,256]{2,1,0:T(8,128)S(1)} %get-tuple-element.81), channel_id=1, source_target_pairs={{0,24},{4,28},{8,16},{12,20},{16,8},{20,12},{24,0},{28,4},{1,25},{... | collective-permute-start | bytes 196616 | tf_op jit(solution)/shard_map/ppermute | solution.py:36
  52.2 4.3 %collective-permute-start.9 = (f32[2,32,256]{2,1,0:T(8,128)S(1)}, f32[2,32,256]{2,1,0:T(8,128)S(1)}, u32[]{:S(2)}, u32[]{:S(2)}) collective-permute-start(f32[2,32,256]{2,1,0:T(8,128)S(1)} %get-tuple-element.82), channel_id=1, source_target_pairs={{0,16},{4,20},{8,24},{12,28},{16,0},{20,4},{24,8},{28,12},{1,17},{... | collective-permute-start | bytes 196616 | tf_op jit(solution)/shard_map/ppermute | solution.py:36
  52.7 4.3 %collective-permute-start.10 = (f32[2,32,256]{2,1,0:T(8,128)S(1)}, f32[2,32,256]{2,1,0:T(8,128)S(1)}, u32[]{:S(2)}, u32[]{:S(2)}) collective-permute-start(f32[2,32,256]{2,1,0:T(8,128)S(1)} %get-tuple-element.83), channel_id=1, source_target_pairs={{0,8},{4,12},{8,0},{12,4},{16,24},{20,28},{24,16},{28,20},{1,9},{5... | collective-permute-start | bytes 196616 | tf_op jit(solution)/shard_map/ppermute | solution.py:36
  57.1 4.4 %collective-permute-start.11 = (f32[72,256]{1,0:T(8,128)S(1)}, f32[72,256]{1,0:T(8,128)S(1)}, u32[]{:S(2)}, u32[]{:S(2)}) collective-permute-start(f32[72,256]{1,0:T(8,128)S(1)} %pad_maximum_fusion), channel_id=1, source_target_pairs={{0,1},{1,0},{2,3},{3,2},{4,5},{5,4},{6,7},{7,6},{8,9},{9,8},{10,11... | collective-permute-start | bytes 221192 | tf_op jit(solution)/shard_map/ppermute | solution.py:36
  61.5 5.3 %collective-permute-start.12 = (f32[72,256]{1,0:T(8,128)S(1)}, f32[72,256]{1,0:T(8,128)S(1)}, u32[]{:S(2)}, u32[]{:S(2)}) collective-permute-start(f32[72,256]{1,0:T(8,128)S(1)} %pad_maximum_fusion.1), channel_id=1, source_target_pairs={{0,2},{1,3},{2,0},{3,1},{4,6},{5,7},{6,4},{7,5},{8,10},{9,11},{10,... | collective-permute-start | bytes 221192 | tf_op jit(solution)/shard_map/ppermute | solution.py:36
  66.9 6.3 %collective-permute-start.15 = (f32[2,32,256]{2,1,0:T(8,128)S(1)}, f32[2,32,256]{2,1,0:T(8,128)S(1)}, u32[]{:S(2)}, u32[]{:S(2)}) collective-permute-start(f32[2,32,256]{2,1,0:T(8,128)S(1)} %add.20.rest_0_), channel_id=1, source_target_pairs={{0,24},{4,28},{8,16},{12,20},{16,8},{20,12},{24,0},{28,4},{1,25},{... | collective-permute-start | bytes 196616 | tf_op jit(solution)/shard_map/ppermute | solution.py:36
  68.4 4.8 %collective-permute-start.14 = (f32[2,32,256]{2,1,0:T(8,128)S(1)}, f32[2,32,256]{2,1,0:T(8,128)S(1)}, u32[]{:S(2)}, u32[]{:S(2)}) collective-permute-start(f32[2,32,256]{2,1,0:T(8,128)S(1)} %add.20.rest_0_), channel_id=1, source_target_pairs={{0,16},{4,20},{8,24},{12,28},{16,0},{20,4},{24,8},{28,12},{1,17},{... | collective-permute-start | bytes 196616 | tf_op jit(solution)/shard_map/ppermute | solution.py:36
  69.4 4.3 %collective-permute-start.13 = (f32[2,32,256]{2,1,0:T(8,128)S(1)}, f32[2,32,256]{2,1,0:T(8,128)S(1)}, u32[]{:S(2)}, u32[]{:S(2)}) collective-permute-start(f32[2,32,256]{2,1,0:T(8,128)S(1)} %add.20.rest_0_), channel_id=1, source_target_pairs={{0,8},{4,12},{8,0},{12,4},{16,24},{20,28},{24,16},{28,20},{1,9},{5... | collective-permute-start | bytes 196616 | tf_op jit(solution)/shard_map/ppermute | solution.py:36
  73.7 1.6 %collective-permute-start.16 = (f32[2,128,256]{2,1,0:T(8,128)S(1)}, f32[2,128,256]{2,1,0:T(8,128)S(1)}, u32[]{:S(2)}, u32[]{:S(2)}) collective-permute-start(f32[2,128,256]{2,1,0:T(8,128)S(1)} %join.1.mine), channel_id=1, source_target_pairs={{0,4},{4,0},{8,12},{12,8},{16,20},{20,16},{24,28},{28,24},{1,5},{5... | collective-permute-start | bytes 786440 | tf_op jit(solution)/shard_map/ppermute | solution.py:36

commit v6 on v5

--- a/solution.py
+++ b/solution.py
@@ -194,7 +194,7 @@
     return jnp.concatenate([stacked[:size], stacked[size:]], axis=1)
 
 
-def buffer_terms(amp, tile, probe, left, right, emit, term, capacity, size, parts):
+def buffer_terms(amp, tile, probe, left, right, emit, term_in, term, capacity, size, parts):
     numbers = read_info(amp[capacity * size :, :], 3 * capacity)
     slots = [tuple(numbers[3 * k : 3 * k + 3]) for k in range(capacity)]
     probe_re = probe[0]
@@ -215,23 +215,22 @@
         wave_im = wave[:, size:]
         square = wave_re * wave_re + wave_im * wave_im
         measured = amp[k * size : (k + 1) * size, :].astype(f32)
-        factor = 1.0 - measured * lax.rsqrt(jnp.maximum(square, 0.25))
+        factor = (1.0 - measured * lax.rsqrt(jnp.maximum(square, 0.25))) * slots[k][2].astype(f32)
         diffs.append(jnp.concatenate([(wave_re * factor).astype(bf16), (wave_im * factor).astype(bf16)], axis=0))
     backs = [side_by_side(dot(right[...], diff).astype(bf16), size) for diff in diffs]
     chis = [dot(back, left[...]) for back in backs]
     sum_re = sum_im = 0.0
-    for slot, ((row, col, valid), (patch_re, patch_im), chi) in enumerate(zip(slots, patches, chis)):
-        weight = valid.astype(f32)
-        chi_re = chi[:, :size] * weight
-        chi_im = chi[:, size:] * weight
+    for slot, ((row, col, _), (patch_re, patch_im), chi) in enumerate(zip(slots, patches, chis)):
+        chi_re = chi[:, :size]
+        chi_im = chi[:, size:]
         emit(slot, 0, row, col, (probe_re * chi_re + probe_im * chi_im).astype(bf16))
         emit(slot, 1, row, col, (probe_re * chi_im - probe_im * chi_re).astype(bf16))
         patch_re = patch_re.astype(f32)
         patch_im = patch_im.astype(f32)
         sum_re += patch_re * chi_re + patch_im * chi_im
         sum_im += patch_re * chi_im - patch_im * chi_re
-    term[0] += sum_re
-    term[1] += sum_im
+    term[0] = term_in[0] + sum_re
+    term[1] = term_in[1] + sum_im
 
 
 def terms_kernel(count, capacity, first, last, probe, left, right, *rest):
@@ -246,15 +245,14 @@
                 tile[plane * parts + k] = block.astype(bf16).astype(f32)
         acc[...] = jnp.zeros(acc.shape, f32)
         term[...] = jnp.zeros(term.shape, f32)
+        term_in = term
     elif last:
         tile, term_in, grads, keep, send, term = rest
         parts = tile.shape[0] // 2
-        term[...] = term_in[...]
     else:
         tile, acc_in, term_in, acc, term = rest
         parts = tile.shape[0] // 2
         acc[...] = acc_in[...]
-        term[...] = term_in[...]
 
     def emit(slot, plane, row, col, grad):
         if last:
@@ -263,7 +261,8 @@
             add_window(acc, plane, row, col, grad.astype(f32), size, parts)
 
     for message in messages:
-        buffer_terms(message, tile, probe, left, right, emit, term, capacity, size, parts)
+        buffer_terms(message, tile, probe, left, right, emit, term_in, term, capacity, size, parts)
+        term_in = term
     if last:
         half = size // 2
         odd = lax.rem(lax.axis_index("pos"), 2)

time: 76.4 us -> 76.4 us (level)
  no operation moved by 1% of the time
where the time goes in v6:
time: 76.4 us; the launch traced here: 76.2 us
  Pallas kernels  34.8 us (46%)
  starting transfers between devices  20.8 us (27%)
  waiting for transfers between devices  19.4 us (25%)
  between operations  1.08 us (1%)
    pallas_call x8, Pallas kernels, terms(): pl.pallas_call(functools.partial(terms_kernel, count, capacity, state is...  26.5 us
    ppermute x17, starting transfers between devices, exchange(): return lax.ppermute(value, axis, [(i, i ^ distance) for i in range(count)])  20.8 us
    ppermute x17, waiting for transfers between devices, exchange(): return lax.ppermute(value, axis, [(i, i ^ distance) for i in range(count)])  19.4 us
    pallas_call x1, Pallas kernels, pack(): pl.pallas_call(functools.partial(pack_kernel, n_pos, capacity, order), in...  3.95 us
    pallas_call x1, Pallas kernels, finish(): pl.pallas_call(functools.partial(finish_kernel, n_pos, n_obj, ring, steps...  2.77 us
  transfers between devices with their start and end apart: 17, of which 11 were waited for; matrix products, arithmetic and copies ran while one was open for 0% of the time, Pallas kernels for 35%

profile of v6, /device:TPU:0, one launch (start us, length us, event | category | flops | bytes accessed | tf_op | source)
XLA Modules:
  0.0 76.2 jit_solution(8186203906501602389)
XLA Ops:
  0.6 0.0 copy-start.1
  0.6 0.0 copy-start.2
  0.7 0.0 copy-start.3
  0.7 0.0 copy-start
  0.7 4.0 %pack.1 = (bf16[784,256]{1,0:T(8,128)(2,1)}, bf16[784,256]{1,0:T(8,128)(2,1)}, bf16[784,256]{1,0:T(8,128)(2,1)}, bf16[784,256]{1,0:T(8,128)(2,1)}, bf16[784,256]...) custom-call(s32[16]{0:T(128)} %owner_in.1, ...), custom_call_target="tpu_custom_call" | custom-call | flops 1048576 | bytes 1048576 | tf_op jit(solution)/shard_map/pack/pallas_call | solution.py:137
  4.6 0.5 collective-permute-start
  5.2 2.6 %collective-permute-start.2 = (bf16[784,256]{1,0:T(8,128)(2,1)}, bf16[784,256]{1,0:T(8,128)(2,1)S(1)}, u32[]{:S(2)}, u32[]{:S(2)}) collective-permute-start(bf16[784,256]{1,0:T(8,128)(2,1)} %get-tuple-element.51), channel_id=1, source_target_pairs={{0,8},{4,12},{8,0},{12,4},{16,24},{20,28},{24,16},{28,20},{1,9},{5... | collective-permute-start | bytes 1204232 | tf_op jit(solution)/shard_map/ppermute | solution.py:36
  7.7 1.5 %collective-permute-start.1 = (bf16[784,256]{1,0:T(8,128)(2,1)}, bf16[784,256]{1,0:T(8,128)(2,1)S(1)}, u32[]{:S(2)}, u32[]{:S(2)}) collective-permute-start(bf16[784,256]{1,0:T(8,128)(2,1)} %get-tuple-element.50), channel_id=1, source_target_pairs={{0,16},{4,20},{8,24},{12,28},{16,0},{20,4},{24,8},{28,12},{1,17},{... | collective-permute-start | bytes 1204232 | tf_op jit(solution)/shard_map/ppermute | solution.py:36
  9.2 0.0 collective-permute-start.3
  9.3 0.0 copy-start.4
  9.3 0.3 collective-permute-start.6
  9.6 0.0 collective-permute-done.rest_0_.rest_2_
  9.6 0.0 copy-done.1
  9.6 0.0 copy-done.2
  9.6 0.0 copy-done.3
  9.6 0.0 copy-done
  9.6 3.2 %terms.8 = (f32[6,512,128]{2,1,0:T(8,128)S(1)}, f32[6,512,128]{2,1,0:T(8,128)S(1)}, f32[2,256,256]{2,1,0:T(8,128)S(1)}) custom-call(f32[2,256,256]{2,1,0:T(8,128)S(1)} %copy-done, bf16[512,512]{1,0:T(8,128)(2,1)S(1)} %copy-done.2, bf16[512,512]{1,0:T(8,128)(2,1)S(1)} %copy-done.1, bf16[784,256]{1,0:T(8,128)(2,1)S(1)} %collective-permute-done.rest_0_.rest_2_, ...), custom_call_target="tpu_custom_call" | custom-call | flops 100663296 | bytes 262144 | tf_op jit(solution)/shard_map/terms/pallas_call | solution.py:296
  12.8 0.0 copy-done.4
  12.8 3.4 %terms.9 = (f32[6,512,128]{2,1,0:T(8,128)S(1)}, f32[2,256,256]{2,1,0:T(8,128)S(1)}) custom-call(f32[2,256,256]{2,1,0:T(8,128)S(1)} %copy-done, bf16[512,512]{1,0:T(8,128)(2,1)S(1)} %copy-done.2, bf16[512,512]{1,0:T(8,128)(2,1)S(1)} %copy-done.1, bf16[784,256]{1,0:T(8,128)(2,1)S(1)} %copy-done.4, ...), custom_call_target="tpu_custom_call", output_to_operand_aliasing={{0}: (5, {}), {1}: (6, {})} | custom-call | flops 100663296 | bytes 262144 | tf_op jit(solution)/shard_map/terms/pallas_call | solution.py:296
  16.1 1.9 %collective-permute-done.2.rest_0_ = bf16[784,256]{1,0:T(8,128)(2,1)S(1)} collective-permute-done((bf16[784,256]{1,0:T(8,128)(2,1)}, bf16[784,256]{1,0:T(8,128)(2,1)S(1)}, u32[]{:S(2)}, u32[]{:S(2)}) %collective-permute-start.2) | collective-permute-done | bytes 401440 | tf_op jit(solution)/shard_map/ppermute | solution.py:36
  18.1 3.3 %terms.10 = (f32[6,512,128]{2,1,0:T(8,128)S(1)}, f32[2,256,256]{2,1,0:T(8,128)S(1)}) custom-call(f32[2,256,256]{2,1,0:T(8,128)S(1)} %copy-done, bf16[512,512]{1,0:T(8,128)(2,1)S(1)} %copy-done.2, bf16[512,512]{1,0:T(8,128)(2,1)S(1)} %copy-done.1, bf16[784,256]{1,0:T(8,128)(2,1)S(1)} %collective-permute-done.2.rest_0_, ...), custom_call_target="tpu_custom_call", output_to_operand_aliasing={{0}: (5, {}), {1}: (6, {})} | custom-call | flops 100663296 | bytes 262144 | tf_op jit(solution)/shard_map/terms/pallas_call | solution.py:296
  21.4 0.0 collective-permute-done.1.rest_0_
  21.4 0.0 copy-start.7
  21.4 3.5 %terms.11 = (f32[6,512,128]{2,1,0:T(8,128)S(1)}, f32[2,256,256]{2,1,0:T(8,128)S(1)}) custom-call(f32[2,256,256]{2,1,0:T(8,128)S(1)} %copy-done, bf16[512,512]{1,0:T(8,128)(2,1)S(1)} %copy-done.2, bf16[512,512]{1,0:T(8,128)(2,1)S(1)} %copy-done.1, bf16[784,256]{1,0:T(8,128)(2,1)S(1)} %collective-permute-done.1.rest_0_, ...), custom_call_target="tpu_custom_call", output_to_operand_aliasing={{0}: (5, {}), {1}: (6, {})} | custom-call | flops 100663296 | bytes 262144 | tf_op jit(solution)/shard_map/terms/pallas_call | solution.py:296
  25.0 0.0 copy-done.7
  25.0 0.0 copy-start.6
  25.0 3.0 %collective-permute-start.5 = (bf16[784,256]{1,0:T(8,128)(2,1)S(1)}, bf16[784,256]{1,0:T(8,128)(2,1)S(1)}, u32[]{:S(2)}, u32[]{:S(2)}) collective-permute-start(bf16[784,256]{1,0:T(8,128)(2,1)S(1)} %copy-done.7), channel_id=1, source_target_pairs={{0,24},{4,28},{8,16},{12,20},{16,8},{20,12},{24,0},{28,4},{1,25},{... | collective-permute-start | bytes 1204232 | tf_op jit(solution)/shard_map/ppermute | solution.py:36
  28.0 0.0 collective-permute-done.3.rest_0_.rest_3_
  28.0 3.3 %terms.12 = (f32[6,512,128]{2,1,0:T(8,128)S(1)}, f32[2,256,256]{2,1,0:T(8,128)S(1)}) custom-call(f32[2,256,256]{2,1,0:T(8,128)S(1)} %copy-done, bf16[512,512]{1,0:T(8,128)(2,1)S(1)} %copy-done.2, bf16[512,512]{1,0:T(8,128)(2,1)S(1)} %copy-done.1, ...), custom_call_target="tpu_custom_call", output_to_operand_aliasing={{0}: (5, {}), {1}: (6, {})} | custom-call | flops 100663296 | bytes 262144 | tf_op jit(solution)/shard_map/terms/pallas_call | solution.py:296
  31.3 0.0 copy-done.6
  31.3 0.7 collective-permute-start.4
  32.0 0.0 collective-permute-done.6.rest_0_
  32.0 3.4 %terms.13 = (f32[6,512,128]{2,1,0:T(8,128)S(1)}, f32[2,256,256]{2,1,0:T(8,128)S(1)}) custom-call(f32[2,256,256]{2,1,0:T(8,128)S(1)} %copy-done, bf16[512,512]{1,0:T(8,128)(2,1)S(1)} %copy-done.2, bf16[512,512]{1,0:T(8,128)(2,1)S(1)} %copy-done.1, bf16[784,256]{1,0:T(8,128)(2,1)S(1)} %collective-permute-done.6.rest_0_, ...), custom_call_target="tpu_custom_call", output_to_operand_aliasing={{0}: (5, {}), {1}: (6, {})} | custom-call | flops 100663296 | bytes 262144 | tf_op jit(solution)/shard_map/terms/pallas_call | solution.py:296
  35.4 2.8 %collective-permute-done.5.rest_0_ = bf16[784,256]{1,0:T(8,128)(2,1)S(1)} collective-permute-done((bf16[784,256]{1,0:T(8,128)(2,1)S(1)}, bf16[784,256]{1,0:T(8,128)(2,1)S(1)}, u32[]{:S(2)}, u32[]{:S(2)}) %collective-permute-start.5) | collective-permute-done | bytes 401440 | tf_op jit(solution)/shard_map/ppermute | solution.py:36
  38.2 3.3 %terms.14 = (f32[6,512,128]{2,1,0:T(8,128)S(1)}, f32[2,256,256]{2,1,0:T(8,128)S(1)}) custom-call(f32[2,256,256]{2,1,0:T(8,128)S(1)} %copy-done, bf16[512,512]{1,0:T(8,128)(2,1)S(1)} %copy-done.2, bf16[512,512]{1,0:T(8,128)(2,1)S(1)} %copy-done.1, bf16[784,256]{1,0:T(8,128)(2,1)S(1)} %collective-permute-done.5.rest_0_, ...), custom_call_target="tpu_custom_call", output_to_operand_aliasing={{0}: (5, {}), {1}: (6, {})} | custom-call | flops 100663296 | bytes 262144 | tf_op jit(solution)/shard_map/terms/pallas_call | solution.py:296
  41.5 3.0 %collective-permute-done.4.rest_0_.message.rest_4_ = bf16[784,256]{1,0:T(8,128)(2,1)S(1)} collective-permute-done((bf16[784,256]{1,0:T(8,128)(2,1)S(1)}, bf16[784,256]{1,0:T(8,128)(2,1)S(1)}, u32[]{:S(2)}, u32[]{:S(2)}) %collective-permute-start.4) | collective-permute-done | bytes 401440 | tf_op jit(solution)/shard_map/ppermute | solution.py:36
  44.5 0.0 copy-start.5
  44.5 3.1 %terms.15 = (bf16[3,2,256,256]{3,2,1,0:T(8,128)(2,1)S(1)}, f32[2,128,256]{2,1,0:T(8,128)S(1)}, f32[2,128,256]{2,1,0:T(8,128)S(1)}) custom-call(f32[2,256,256]{2,1,0:T(8,128)S(1)} %copy-done, bf16[512,512]{1,0:T(8,128)(2,1)S(1)} %copy-done.2, bf16[512,512]{1,0:T(8,128)(2,1)S(1)} %copy-done.1, ...), custom_call_target="tpu_custom_call" | custom-call | flops 100663296 | bytes 262144 | tf_op jit(solution)/shard_map/terms/pallas_call | solution.py:296
  47.6 0.8 %collective-permute-start.7 = (f32[2,128,256]{2,1,0:T(8,128)S(1)}, f32[2,128,256]{2,1,0:T(8,128)S(1)}, u32[]{:S(2)}, u32[]{:S(2)}) collective-permute-start(f32[2,128,256]{2,1,0:T(8,128)S(1)} %get-tuple-element.79), channel_id=1, source_target_pairs={{0,4},{4,0},{8,12},{12,8},{16,20},{20,16},{24,28},{28,24},{1,5},{5... | collective-permute-start | bytes 786440 | tf_op jit(solution)/shard_map/ppermute | solution.py:36
  48.4 1.2 %collective-permute-done.7.got = f32[2,128,256]{2,1,0:T(8,128)S(1)} collective-permute-done((f32[2,128,256]{2,1,0:T(8,128)S(1)}, f32[2,128,256]{2,1,0:T(8,128)S(1)}, u32[]{:S(2)}, u32[]{:S(2)}) %collective-permute-start.7) | collective-permute-done | bytes 262176 | tf_op jit(solution)/shard_map/ppermute | solution.py:36
  49.6 2.6 %collective-permute-start.8 = (f32[2,32,256]{2,1,0:T(8,128)S(1)}, f32[2,32,256]{2,1,0:T(8,128)S(1)}, u32[]{:S(2)}, u32[]{:S(2)}) collective-permute-start(f32[2,32,256]{2,1,0:T(8,128)S(1)} %get-tuple-element.81), channel_id=1, source_target_pairs={{0,24},{4,28},{8,16},{12,20},{16,8},{20,12},{24,0},{28,4},{1,25},{... | collective-permute-start | bytes 196616 | tf_op jit(solution)/shard_map/ppermute | solution.py:36
  52.1 0.5 collective-permute-start.9
  52.7 0.5 collective-permute-start.10
  53.1 1.8 %collective-permute-done.8 = f32[2,32,256]{2,1,0:T(8,128)S(1)} collective-permute-done((f32[2,32,256]{2,1,0:T(8,128)S(1)}, f32[2,32,256]{2,1,0:T(8,128)S(1)}, u32[]{:S(2)}, u32[]{:S(2)}) %collective-permute-start.8) | collective-permute-done | bytes 65568 | tf_op jit(solution)/shard_map/ppermute | solution.py:36
  54.9 1.5 %collective-permute-done.9 = f32[2,32,256]{2,1,0:T(8,128)S(1)} collective-permute-done((f32[2,32,256]{2,1,0:T(8,128)S(1)}, f32[2,32,256]{2,1,0:T(8,128)S(1)}, u32[]{:S(2)}, u32[]{:S(2)}) %collective-permute-start.9) | collective-permute-done | bytes 65568 | tf_op jit(solution)/shard_map/ppermute | solution.py:36
  56.4 0.5 collective-permute-done.10
  57.0 0.0 copy-done.5
  57.0 1.7 %collective-permute-start.11 = (f32[72,256]{1,0:T(8,128)S(1)}, f32[72,256]{1,0:T(8,128)S(1)}, u32[]{:S(2)}, u32[]{:S(2)}) collective-permute-start(f32[72,256]{1,0:T(8,128)S(1)} %pad_maximum_fusion), channel_id=1, source_target_pairs={{0,1},{1,0},{2,3},{3,2},{4,5},{5,4},{6,7},{7,6},{8,9},{9,8},{10,11... | collective-permute-start | bytes 221192 | tf_op jit(solution)/shard_map/ppermute | solution.py:36
  58.6 0.7 add.24.acc
  59.3 2.1 %collective-permute-done.11.rest_0_ = f32[72,256]{1,0:T(8,128)S(1)} collective-permute-done((f32[72,256]{1,0:T(8,128)S(1)}, f32[72,256]{1,0:T(8,128)S(1)}, u32[]{:S(2)}, u32[]{:S(2)}) %collective-permute-start.11) | collective-permute-done | bytes 73760 | tf_op jit(solution)/shard_map/ppermute | solution.py:36
  61.5 2.7 %collective-permute-start.12 = (f32[72,256]{1,0:T(8,128)S(1)}, f32[72,256]{1,0:T(8,128)S(1)}, u32[]{:S(2)}, u32[]{:S(2)}) collective-permute-start(f32[72,256]{1,0:T(8,128)S(1)} %pad_maximum_fusion.1), channel_id=1, source_target_pairs={{0,2},{1,3},{2,0},{3,1},{4,6},{5,7},{6,4},{7,5},{8,10},{9,11},{10,... | collective-permute-start | bytes 221192 | tf_op jit(solution)/shard_map/ppermute | solution.py:36
  64.1 2.7 %collective-permute-done.12.rest_1_ = f32[72,256]{1,0:T(8,128)S(1)} collective-permute-done((f32[72,256]{1,0:T(8,128)S(1)}, f32[72,256]{1,0:T(8,128)S(1)}, u32[]{:S(2)}, u32[]{:S(2)}) %collective-permute-start.12) | collective-permute-done | bytes 73760 | tf_op jit(solution)/shard_map/ppermute | solution.py:36
  66.8 1.6 %collective-permute-start.15 = (f32[2,32,256]{2,1,0:T(8,128)S(1)}, f32[2,32,256]{2,1,0:T(8,128)S(1)}, u32[]{:S(2)}, u32[]{:S(2)}) collective-permute-start(f32[2,32,256]{2,1,0:T(8,128)S(1)} %add.20.rest_0_), channel_id=1, source_target_pairs={{0,24},{4,28},{8,16},{12,20},{16,8},{20,12},{24,0},{28,4},{1,25},{... | collective-permute-start | bytes 196616 | tf_op jit(solution)/shard_map/ppermute | solution.py:36
  68.3 0.9 %collective-permute-start.14 = (f32[2,32,256]{2,1,0:T(8,128)S(1)}, f32[2,32,256]{2,1,0:T(8,128)S(1)}, u32[]{:S(2)}, u32[]{:S(2)}) collective-permute-start(f32[2,32,256]{2,1,0:T(8,128)S(1)} %add.20.rest_0_), channel_id=1, source_target_pairs={{0,16},{4,20},{8,24},{12,28},{16,0},{20,4},{24,8},{28,12},{1,17},{... | collective-permute-start | bytes 196616 | tf_op jit(solution)/shard_map/ppermute | solution.py:36
  69.3 1.1 %collective-permute-start.13 = (f32[2,32,256]{2,1,0:T(8,128)S(1)}, f32[2,32,256]{2,1,0:T(8,128)S(1)}, u32[]{:S(2)}, u32[]{:S(2)}) collective-permute-start(f32[2,32,256]{2,1,0:T(8,128)S(1)} %add.20.rest_0_), channel_id=1, source_target_pairs={{0,8},{4,12},{8,0},{12,4},{16,24},{20,28},{24,16},{28,20},{1,9},{5... | collective-permute-start | bytes 196616 | tf_op jit(solution)/shard_map/ppermute | solution.py:36
  70.3 2.8 %finish.1 = f32[2,512,384]{2,1,0:T(8,128)} custom-call(f32[2,512,384]{2,1,0:T(8,128)S(1)} %copy-done.3, f32[6,512,128]{2,1,0:T(8,128)S(1)} %add.24.acc, f32[72,256]{1,0:T(8,128)S(1)} %collective-permute-done.11.rest_0_, f32[72,256]{1,0:T(8,128)S(1)} %collective-permute-done.12.rest_1_, bf16[784,256]{1,0:T(8,128)(2,1)S(1)} %collective-permute-done.rest_0_.rest_2_, ...), custom_call_target="tpu_custom_call" | custom-call | flops 16777216 | bytes 8388608 | tf_op jit(solution)/shard_map/finish/pallas_call | solution.py:400
  73.1 0.0 collective-permute-done.15.rest_3_
  73.1 0.0 collective-permute-done.14.rest_2_
  73.1 0.4 collective-permute-done.13.rest_1_
  73.6 0.1 collective-permute-start.16
  73.7 1.5 %collective-permute-done.16.other = f32[2,128,256]{2,1,0:T(8,128)S(1)} collective-permute-done((f32[2,128,256]{2,1,0:T(8,128)S(1)}, f32[2,128,256]{2,1,0:T(8,128)S(1)}, u32[]{:S(2)}, u32[]{:S(2)}) %collective-permute-start.16) | collective-permute-done | bytes 262176 | tf_op jit(solution)/shard_map/ppermute | solution.py:36
  75.2 0.8 %whole.1 = f32[2,256,256]{2,1,0:T(8,128)} custom-call(f32[2,128,256]{2,1,0:T(8,128)S(1)} %join.1.mine, f32[2,128,256]{2,1,0:T(8,128)S(1)} %collective-permute-done.16.other), custom_call_target="tpu_custom_call" | custom-call | tf_op jit(solution)/shard_map/whole/pallas_call | solution.py:460
  (10 shorter events, 0.1 us)
Async XLA Ops:
  0.6 8.9 %copy-start.1 = (bf16[512,512]{1,0:T(8,128)(2,1)S(1)}, bf16[512,512]{1,0:T(8,128)(2,1)}, u32[]{:S(2)}) copy-start(bf16[512,512]{1,0:T(8,128)(2,1)} %constant.5.clone.right) | copy-start | bytes 1572868
  0.6 8.9 %copy-start.2 = (bf16[512,512]{1,0:T(8,128)(2,1)S(1)}, bf16[512,512]{1,0:T(8,128)(2,1)}, u32[]{:S(2)}) copy-start(bf16[512,512]{1,0:T(8,128)(2,1)} %constant.4.clone.left) | copy-start | bytes 1572868
  0.7 8.9 %copy-start.3 = (f32[2,512,384]{2,1,0:T(8,128)S(1)}, f32[2,512,384]{2,1,0:T(8,128)}, u32[]{:S(2)}) copy-start(f32[2,512,384]{2,1,0:T(8,128)} %tile.3) | copy-start | bytes 4718596
  0.7 8.9 %copy-start = (f32[2,256,256]{2,1,0:T(8,128)S(1)}, f32[2,256,256]{2,1,0:T(8,128)}, u32[]{:S(2)}) copy-start(f32[2,256,256]{2,1,0:T(8,128)} %probe.17) | copy-start | bytes 1572868
  4.6 4.9 %collective-permute-start = (bf16[784,256]{1,0:T(8,128)(2,1)}, bf16[784,256]{1,0:T(8,128)(2,1)S(1)}, u32[]{:S(2)}, u32[]{:S(2)}) collective-permute-start(bf16[784,256]{1,0:T(8,128)(2,1)} %get-tuple-element.48), channel_id=1, source_target_pairs={{0,4},{4,0},{8,12},{12,8},{16,20},{20,16},{24,28},{28,24},{1,5},{5... | collective-permute-start | bytes 1204232 | tf_op jit(solution)/shard_map/ppermute | solution.py:36
  5.2 12.9 %collective-permute-start.2 = (bf16[784,256]{1,0:T(8,128)(2,1)}, bf16[784,256]{1,0:T(8,128)(2,1)S(1)}, u32[]{:S(2)}, u32[]{:S(2)}) collective-permute-start(bf16[784,256]{1,0:T(8,128)(2,1)} %get-tuple-element.51), channel_id=1, source_target_pairs={{0,8},{4,12},{8,0},{12,4},{16,24},{20,28},{24,16},{28,20},{1,9},{5... | collective-permute-start | bytes 1204232 | tf_op jit(solution)/shard_map/ppermute | solution.py:36
  7.7 13.7 %collective-permute-start.1 = (bf16[784,256]{1,0:T(8,128)(2,1)}, bf16[784,256]{1,0:T(8,128)(2,1)S(1)}, u32[]{:S(2)}, u32[]{:S(2)}) collective-permute-start(bf16[784,256]{1,0:T(8,128)(2,1)} %get-tuple-element.50), channel_id=1, source_target_pairs={{0,16},{4,20},{8,24},{12,28},{16,0},{20,4},{24,8},{28,12},{1,17},{... | collective-permute-start | bytes 1204232 | tf_op jit(solution)/shard_map/ppermute | solution.py:36
  9.2 18.7 %collective-permute-start.3 = (bf16[784,256]{1,0:T(8,128)(2,1)}, bf16[784,256]{1,0:T(8,128)(2,1)S(1)}, u32[]{:S(2)}, u32[]{:S(2)}) collective-permute-start(bf16[784,256]{1,0:T(8,128)(2,1)} %get-tuple-element.63), channel_id=1, source_target_pairs={{0,12},{4,8},{8,4},{12,0},{16,28},{20,24},{24,20},{28,16},{1,13},{... | collective-permute-start | bytes 1204232 | tf_op jit(solution)/shard_map/ppermute | solution.py:36
  9.3 3.5 %copy-start.4 = (bf16[784,256]{1,0:T(8,128)(2,1)S(1)}, bf16[784,256]{1,0:T(8,128)(2,1)}, u32[]{:S(2)}) copy-start(bf16[784,256]{1,0:T(8,128)(2,1)} %get-tuple-element.52.rest_0_) | copy-start | bytes 1204228
  9.3 22.7 %collective-permute-start.6 = (bf16[784,256]{1,0:T(8,128)(2,1)}, bf16[784,256]{1,0:T(8,128)(2,1)S(1)}, u32[]{:S(2)}, u32[]{:S(2)}) collective-permute-start(bf16[784,256]{1,0:T(8,128)(2,1)} %get-tuple-element.72), channel_id=1, source_target_pairs={{0,20},{4,16},{8,28},{12,24},{16,4},{20,0},{24,12},{28,8},{1,21},{... | collective-permute-start | bytes 1204232 | tf_op jit(solution)/shard_map/ppermute | solution.py:36
  21.4 3.5 %copy-start.7 = (bf16[784,256]{1,0:T(8,128)(2,1)S(1)}, bf16[784,256]{1,0:T(8,128)(2,1)}, u32[]{:S(2)}) copy-start(bf16[784,256]{1,0:T(8,128)(2,1)} %get-tuple-element.71) | copy-start | bytes 1204228
  25.0 6.4 %copy-start.6 = (bf16[784,256]{1,0:T(8,128)(2,1)S(1)}, bf16[784,256]{1,0:T(8,128)(2,1)}, u32[]{:S(2)}) copy-start(bf16[784,256]{1,0:T(8,128)(2,1)} %get-tuple-element.69) | copy-start | bytes 1204228
  25.0 13.2 %collective-permute-start.5 = (bf16[784,256]{1,0:T(8,128)(2,1)S(1)}, bf16[784,256]{1,0:T(8,128)(2,1)S(1)}, u32[]{:S(2)}, u32[]{:S(2)}) collective-permute-start(bf16[784,256]{1,0:T(8,128)(2,1)S(1)} %copy-done.7), channel_id=1, source_target_pairs={{0,24},{4,28},{8,16},{12,20},{16,8},{20,12},{24,0},{28,4},{1,25},{... | collective-permute-start | bytes 1204232 | tf_op jit(solution)/shard_map/ppermute | solution.py:36
  31.3 13.2 %collective-permute-start.4 = (bf16[784,256]{1,0:T(8,128)(2,1)S(1)}, bf16[784,256]{1,0:T(8,128)(2,1)S(1)}, u32[]{:S(2)}, u32[]{:S(2)}) collective-permute-start(bf16[784,256]{1,0:T(8,128)(2,1)S(1)} %copy-done.6), channel_id=1, source_target_pairs={{0,28},{4,24},{8,20},{12,16},{16,12},{20,8},{24,4},{28,0},{1,29},{... | collective-permute-start | bytes 1204232 | tf_op jit(solution)/shard_map/ppermute | solution.py:36
  44.5 12.5 %copy-start.5 = (f32[8,256]{1,0:T(8,128)S(1)}, f32[8,256]{1,0:T(8,128)}, u32[]{:S(2)}) copy-start(f32[8,256]{1,0:T(8,128)} %get-tuple-element.84) | copy-start | bytes 24580
  47.6 1.9 %collective-permute-start.7 = (f32[2,128,256]{2,1,0:T(8,128)S(1)}, f32[2,128,256]{2,1,0:T(8,128)S(1)}, u32[]{:S(2)}, u32[]{:S(2)}) collective-permute-start(f32[2,128,256]{2,1,0:T(8,128)S(1)} %get-tuple-element.79), channel_id=1, source_target_pairs={{0,4},{4,0},{8,12},{12,8},{16,20},{20,16},{24,28},{28,24},{1,5},{5... | collective-permute-start | bytes 786440 | tf_op jit(solution)/shard_map/ppermute | solution.py:36
  49.6 5.3 %collective-permute-start.8 = (f32[2,32,256]{2,1,0:T(8,128)S(1)}, f32[2,32,256]{2,1,0:T(8,128)S(1)}, u32[]{:S(2)}, u32[]{:S(2)}) collective-permute-start(f32[2,32,256]{2,1,0:T(8,128)S(1)} %get-tuple-element.81), channel_id=1, source_target_pairs={{0,24},{4,28},{8,16},{12,20},{16,8},{20,12},{24,0},{28,4},{1,25},{... | collective-permute-start | bytes 196616 | tf_op jit(solution)/shard_map/ppermute | solution.py:36
  52.1 4.3 %collective-permute-start.9 = (f32[2,32,256]{2,1,0:T(8,128)S(1)}, f32[2,32,256]{2,1,0:T(8,128)S(1)}, u32[]{:S(2)}, u32[]{:S(2)}) collective-permute-start(f32[2,32,256]{2,1,0:T(8,128)S(1)} %get-tuple-element.82), channel_id=1, source_target_pairs={{0,16},{4,20},{8,24},{12,28},{16,0},{20,4},{24,8},{28,12},{1,17},{... | collective-permute-start | bytes 196616 | tf_op jit(solution)/shard_map/ppermute | solution.py:36
  52.7 4.3 %collective-permute-start.10 = (f32[2,32,256]{2,1,0:T(8,128)S(1)}, f32[2,32,256]{2,1,0:T(8,128)S(1)}, u32[]{:S(2)}, u32[]{:S(2)}) collective-permute-start(f32[2,32,256]{2,1,0:T(8,128)S(1)} %get-tuple-element.83), channel_id=1, source_target_pairs={{0,8},{4,12},{8,0},{12,4},{16,24},{20,28},{24,16},{28,20},{1,9},{5... | collective-permute-start | bytes 196616 | tf_op jit(solution)/shard_map/ppermute | solution.py:36
  57.0 4.4 %collective-permute-start.11 = (f32[72,256]{1,0:T(8,128)S(1)}, f32[72,256]{1,0:T(8,128)S(1)}, u32[]{:S(2)}, u32[]{:S(2)}) collective-permute-start(f32[72,256]{1,0:T(8,128)S(1)} %pad_maximum_fusion), channel_id=1, source_target_pairs={{0,1},{1,0},{2,3},{3,2},{4,5},{5,4},{6,7},{7,6},{8,9},{9,8},{10,11... | collective-permute-start | bytes 221192 | tf_op jit(solution)/shard_map/ppermute | solution.py:36
  61.5 5.3 %collective-permute-start.12 = (f32[72,256]{1,0:T(8,128)S(1)}, f32[72,256]{1,0:T(8,128)S(1)}, u32[]{:S(2)}, u32[]{:S(2)}) collective-permute-start(f32[72,256]{1,0:T(8,128)S(1)} %pad_maximum_fusion.1), channel_id=1, source_target_pairs={{0,2},{1,3},{2,0},{3,1},{4,6},{5,7},{6,4},{7,5},{8,10},{9,11},{10,... | collective-permute-start | bytes 221192 | tf_op jit(solution)/shard_map/ppermute | solution.py:36
  66.8 6.3 %collective-permute-start.15 = (f32[2,32,256]{2,1,0:T(8,128)S(1)}, f32[2,32,256]{2,1,0:T(8,128)S(1)}, u32[]{:S(2)}, u32[]{:S(2)}) collective-permute-start(f32[2,32,256]{2,1,0:T(8,128)S(1)} %add.20.rest_0_), channel_id=1, source_target_pairs={{0,24},{4,28},{8,16},{12,20},{16,8},{20,12},{24,0},{28,4},{1,25},{... | collective-permute-start | bytes 196616 | tf_op jit(solution)/shard_map/ppermute | solution.py:36
  68.3 4.8 %collective-permute-start.14 = (f32[2,32,256]{2,1,0:T(8,128)S(1)}, f32[2,32,256]{2,1,0:T(8,128)S(1)}, u32[]{:S(2)}, u32[]{:S(2)}) collective-permute-start(f32[2,32,256]{2,1,0:T(8,128)S(1)} %add.20.rest_0_), channel_id=1, source_target_pairs={{0,16},{4,20},{8,24},{12,28},{16,0},{20,4},{24,8},{28,12},{1,17},{... | collective-permute-start | bytes 196616 | tf_op jit(solution)/shard_map/ppermute | solution.py:36
  69.3 4.3 %collective-permute-start.13 = (f32[2,32,256]{2,1,0:T(8,128)S(1)}, f32[2,32,256]{2,1,0:T(8,128)S(1)}, u32[]{:S(2)}, u32[]{:S(2)}) collective-permute-start(f32[2,32,256]{2,1,0:T(8,128)S(1)} %add.20.rest_0_), channel_id=1, source_target_pairs={{0,8},{4,12},{8,0},{12,4},{16,24},{20,28},{24,16},{28,20},{1,9},{5... | collective-permute-start | bytes 196616 | tf_op jit(solution)/shard_map/ppermute | solution.py:36
  73.6 1.6 %collective-permute-start.16 = (f32[2,128,256]{2,1,0:T(8,128)S(1)}, f32[2,128,256]{2,1,0:T(8,128)S(1)}, u32[]{:S(2)}, u32[]{:S(2)}) collective-permute-start(f32[2,128,256]{2,1,0:T(8,128)S(1)} %join.1.mine), channel_id=1, source_target_pairs={{0,4},{4,0},{8,12},{12,8},{16,20},{20,16},{24,28},{28,24},{1,5},{5... | collective-permute-start | bytes 786440 | tf_op jit(solution)/shard_map/ppermute | solution.py:36
